TPU v7x, 32 devices: a whole 2x2x4 slice. The times are simulated.
32 devices in a mesh: gx: 16 (over z, y, x), gz: 2 (over core).
Axes of the slice: x: 2, y: 2, z: 4, core: 2. Of those that a mesh axis runs over, the one named last changes fastest.
Arguments:
- state: float32 [16, 4, 4, 64, 128], P('gx', 'gz'), may hold values from -6 to 6
- target: float32 [16, 4, 4, 64, 128], P('gx', 'gz'), may hold values from -6 to 6
- coarse_logk: float32 [1024], P(('gx', 'gz')), may hold values from -1 to 1
- cell_slot: int32 [1024], replicated, may hold values from 0 to 1023, each once
- cell_of: int32 [16, 4, 128], P('gx', 'gz'), may hold values from 0 to 1023, as said below
- wall_flags_xaxis: int32 [2, 4, 128], P(None, 'gz'), may hold values 0 or 1
- z_wall: int32 [2, 16, 128], P(None, 'gx'), may hold values 0 or 1
Outputs:
- adjoint_field: float32 [16, 4, 4, 64, 128], P('gx', 'gz')
- coarse_gradient: float32 [1024], P(('gx', 'gz'))
Inputs may be any that keep to these rules, and one draw needn't show every extreme that they name: `cell_of`: element (x, z, y) lies in coarse cell (q * 2 + z // 2) * 128 + y, where q = x // 4, except that q may be x // 4 - 1 when x % 4 == 0 and x // 4 + 1 when x % 4 == 3, always within 0 to 3. A permutation: coarse cell c is held at position cell_slot[c] of coarse_logk and coarse_gradient.
All inputs are finite; a program needn't handle non-finite values. No bound on the sum of `wall_flags_xaxis` or of `z_wall` on one device may be relied on, other than what follows from the above.
Results may differ from a plain program's by a relative error of at most 0.0003.
Values sent between devices are 32-bit elements; how exact they have to be, the bound alone decides.
No kernel may reach another device: no remote copies, remote signals or barrier semaphores. Data moves between devices by JAX's collectives and lax.ppermute only.
A program may use at most 64 MiB of HBM per device.

v0:
```python
import math

import jax
import jax.numpy as jnp
import numpy as np
from jax import lax
from jax.sharding import PartitionSpec as P

penalty = 0.5
operator_scale = 0.25
lift_factor = 6.0


def padded_2(block, sides, width):
    for axis, dim in sides:
        count = lax.axis_size(axis)
        forward = [(i, i + 1) for i in range(count - 1)]
        backward = [(target, source) for source, target in forward]
        low = lax.ppermute(
            lax.slice_in_dim(block, block.shape[dim] - width, None, axis=dim), axis, forward
        )
        high = lax.ppermute(lax.slice_in_dim(block, 0, width, axis=dim), axis, backward)
        block = jnp.concatenate([low, block, high], axis=dim)
    return block


def derivative_tables():
    points = np.array([-1.0, -math.sqrt(0.2), math.sqrt(0.2), 1.0])
    products = np.array(
        [
            np.prod([points[first] - points[other] for other in range(4) if other != first])
            for first in range(4)
        ]
    )
    matrix = np.zeros((4, 4))
    for first in range(4):
        for second in range(4):
            if first != second:
                matrix[first, second] = (
                    products[first] / products[second] / (points[first] - points[second])
                )
        matrix[first, first] = sum(
            (1.0 / (points[first] - points[other]) for other in range(4) if other != first)
        )
    identity = np.eye(4)
    tables = np.stack(
        [
            np.kron(np.kron(matrix, identity), identity),
            np.kron(np.kron(identity, matrix), identity),
            np.kron(np.kron(identity, identity), matrix),
        ]
    )
    return jnp.asarray(tables, jnp.float32)


def flux_matrix(axis, sign):
    matrix = -penalty * np.eye(4)
    matrix[axis, 3] = 0.5 * sign
    matrix[3, axis] = 0.5 * sign
    return jnp.asarray(matrix, jnp.float32)


def flux(axis, sign, values):
    return jnp.einsum(
        "gf,xzfpqy->xzgpqy", flux_matrix(axis, sign), values, precision=lax.Precision.HIGHEST
    )


def sign_fields(flags, axis):
    wall = np.ones(4)
    wall[axis] = -1.0
    opened = np.ones(4)
    opened[3] = -1.0
    wall = jnp.asarray(wall, jnp.float32)[None, :, None]
    opened = jnp.asarray(opened, jnp.float32)[None, :, None]
    return flags[:, None, :] * wall + (1.0 - flags[:, None, :]) * opened


def volume_terms(field, resistance, adjoint):
    tables = derivative_tables()
    velocity = field[:, :, 0:3]
    pressure = field[:, :, 3]
    if adjoint:
        grads = jnp.einsum("knm,xzny->xzkmy", tables, pressure, precision=lax.Precision.HIGHEST)
        divergence = jnp.einsum(
            "knm,xzkny->xzmy", tables, velocity, precision=lax.Precision.HIGHEST
        )
    else:
        grads = jnp.einsum("kmn,xzny->xzkmy", tables, pressure, precision=lax.Precision.HIGHEST)
        divergence = jnp.einsum(
            "kmn,xzkny->xzmy", tables, velocity, precision=lax.Precision.HIGHEST
        )
    shifted_result = resistance[:, :, None, None, :] * velocity + grads
    return jnp.concatenate([shifted_result, divergence[:, :, None]], axis=2)


def face_traces(field7):
    return {
        (0, -1): field7[:, :, :, 0],
        (0, 1): field7[:, :, :, 3],
        (1, -1): field7[:, :, :, :, 0],
        (1, 1): field7[:, :, :, :, 3],
        (2, -1): field7[:, :, :, :, :, 0],
        (2, 1): field7[:, :, :, :, :, 3],
    }


def add_face(result7, axis, sign, values):
    position = 0 if sign < 0 else 3
    index = (slice(None),) * (3 + axis) + (position,)
    return result7.at[index].add(values)


def neighbour_payloads(payload):
    x_count, z_count, _, _, _, y_count = payload[0, -1].shape
    x_pack = jnp.stack([payload[0, -1], payload[0, 1]], axis=2).reshape(
        x_count, z_count, 128, y_count
    )
    z_pack = jnp.stack([payload[2, -1], payload[2, 1]], axis=2).reshape(
        x_count, z_count, 128, y_count
    )
    joined = jnp.concatenate([x_pack, z_pack], axis=2)
    padded = padded_2(joined, (("gx", 0), ("gz", 1)), 1)
    x_lower = padded[:x_count, 1 : z_count + 1, :128]
    x_upper = padded[2:, 1 : z_count + 1, :128]
    z_lower = padded[1 : x_count + 1, :z_count, 128:]
    z_upper = padded[1 : x_count + 1, 2:, 128:]
    shape_faces = (x_count, z_count, 2, 4, 4, 4, y_count)
    return {
        (0, -1): x_lower.reshape(shape_faces)[:, :, 1],
        (0, 1): x_upper.reshape(shape_faces)[:, :, 0],
        (2, -1): z_lower.reshape(shape_faces)[:, :, 1],
        (2, 1): z_upper.reshape(shape_faces)[:, :, 0],
    }


def apply_operator(field, resistance, x_flags, z_flags, bounds, adjoint):
    x_count, z_count, _, _, y_count = field.shape
    field7 = field.reshape(x_count, z_count, 4, 4, 4, 4, y_count)
    result7 = volume_terms(field, resistance, adjoint).reshape(
        x_count, z_count, 4, 4, 4, 4, y_count
    )
    faces = face_traces(field7)
    if adjoint:
        payload = {key: flux(key[0], key[1], value) for key, value in faces.items()}
    else:
        payload = faces
    received = neighbour_payloads(payload)
    for axis in range(3):
        for sign in (-1, 1):
            face = faces[axis, sign]
            base = payload[axis, sign]
            if axis == 1:
                outer = jnp.roll(payload[1, -sign], -sign, axis=5)
            elif axis == 0:
                signs = sign_fields(x_flags[(sign + 1) // 2], 0)[None, :, :, None, None, :]
                marked = bounds[0, sign][:, None, None, None, None, None]
                outer = jnp.where(marked, signs * base, received[0, sign])
            else:
                signs = sign_fields(z_flags[(sign + 1) // 2], 2)[:, None, :, None, None, :]
                marked = bounds[2, sign][None, :, None, None, None, None]
                outer = jnp.where(marked, signs * base, received[2, sign])
            if adjoint:
                jump = outer - base
            else:
                jump = flux(axis, sign, outer - face)
            result7 = add_face(result7, axis, sign, lift_factor * jump)
    return operator_scale * result7.reshape(x_count, z_count, 4, 64, y_count)


def shards(state, target, coarse_logk, cell_slot, cell_of, wall_flags_xaxis, z_wall):
    x_count, z_count, _, _, y_count = state.shape
    logk_rows = lax.all_gather(coarse_logk, "gz", axis=0, tiled=True)
    logk_whole = lax.all_gather(logk_rows, "gx", axis=0, tiled=True)
    slots = cell_slot[cell_of]
    resistance = jnp.exp(-logk_whole[slots])
    x_place = lax.axis_index("gx")
    z_place = lax.axis_index("gz")
    x_size = lax.axis_size("gx")
    z_size = lax.axis_size("gz")
    local_x = jnp.arange(x_count)
    local_z = jnp.arange(z_count)
    bounds = {
        (0, -1): (x_place == 0) & (local_x == 0),
        (0, 1): (x_place == x_size - 1) & (local_x == x_count - 1),
        (2, -1): (z_place == 0) & (local_z == 0),
        (2, 1): (z_place == z_size - 1) & (local_z == z_count - 1),
    }
    x_flags = wall_flags_xaxis.astype(jnp.float32)
    z_flags = z_wall.astype(jnp.float32)
    residual = apply_operator(state, resistance, x_flags, z_flags, bounds, False) - target
    adjoint_field = apply_operator(residual, resistance, x_flags, z_flags, bounds, True)
    term = (
        -(operator_scale / 64.0)
        * resistance
        * jnp.sum(residual[:, :, 0:3] * state[:, :, 0:3], axis=(2, 3))
    )
    total_cells = cell_slot.shape[0]
    partial_value = (
        jnp.zeros((total_cells,), jnp.float32).at[slots.reshape(-1)].add(term.reshape(-1))
    )
    blocks = partial_value.reshape(x_size, z_size, total_cells // (x_size * z_size))
    summed_z = lax.psum_scatter(blocks, "gz", scatter_dimension=1, tiled=True)
    coarse_gradient = lax.psum_scatter(summed_z, "gx", scatter_dimension=0, tiled=True).reshape(-1)
    return (adjoint_field, coarse_gradient)


def solution(mesh):
    placed = (
        P("gx", "gz", None, None, None),
        P("gx", "gz", None, None, None),
        P(("gx", "gz")),
        P(),
        P("gx", "gz", None),
        P(None, "gz", None),
        P(None, "gx", None),
    )
    return jax.shard_map(
        shards,
        mesh=mesh,
        in_specs=placed,
        out_specs=(P("gx", "gz", None, None, None), P(("gx", "gz"))),
        check_vma=False,
    )
```

profile of v0, /device:TPU:0, one launch (start us, length us, event | category | flops | bytes accessed | tf_op | source)
XLA Modules:
  0.0 163.5 jit_solution(3395456172198089525)
XLA Ops:
  7.2 1.2 fusion.94
  8.6 4.9 %collective-permute-start = (f32[1,2,256,128]{3,2,1,0:T(8,128)S(1)}, f32[1,2,256,128]{3,2,1,0:T(8,128)S(1)}, u32[]{:S(2)}, u32[]{:S(2)}) collective-permute-start(f32[1,2,256,128]{3,2,1,0:T(8,128)S(1)} %pad_maximum_fusion.4), channel_id=1, source_target_pairs={{0,2},{2,4},{4,6},{6,8},{8,10},{10,12},{12,14},{14,16},{16,18},{18... | collective-permute-start | bytes 786440 | tf_op jit(solution)/shard_map/ppermute | solution.py:19
  13.5 1.3 collective-permute-start.1
  14.8 0.6 copy-done.16
  15.5 0.7 copy-done.18
  16.2 0.7 copy-done.23
  16.8 0.6 dynamic-slice.96
  18.1 0.6 copy-done.22
  18.9 2.4 %all-reduce = f32[64]{0:T(128)S(1)} all-reduce(f32[64]{0:T(128)S(1)} %dynamic-update-slice.36), channel_id=1, replica_groups=mesh['gx'=16,'gz'=2] {'gz'}, use_global_device_ids=true, to_apply=%add | all-reduce | flops 64 | bytes 512
  21.3 0.6 fusion.95
  22.8 43.2 %all-reduce.1 = f32[1024]{0:T(1024)S(1)} all-reduce(f32[1024]{0:T(1024)S(1)} %dynamic-update-slice.37), channel_id=1, replica_groups=mesh['gx'=16,'gz'=2] {'gx'}, use_global_device_ids=true, to_apply=%add.1 | all-reduce | flops 1024 | bytes 8192
  66.1 1.4 gather_fusion
  67.5 1.4 gather_fusion.1
  69.3 0.6 copy-done.17
  70.0 0.7 copy-done.21
  71.2 1.3 collective-permute-start.2
  72.5 1.3 collective-permute-start.3
  74.3 1.8 %collective-permute-done.3 = f32[3,1,256,128]{3,2,1,0:T(8,128)S(1)} collective-permute-done((f32[3,1,256,128]{3,2,1,0:T(8,128)S(1)}, f32[3,1,256,128]{3,2,1,0:T(8,128)S(1)}, u32[]{:S(2)}, u32[]{:S(2)}) %collective-permute-start.3) | collective-permute-done | bytes 393248 | tf_op jit(solution)/shard_map/ppermute | solution.py:22
  77.9 0.6 copy-done.12
  81.4 0.9 copy-done.3
  84.3 1.3 collective-permute-start.4
  85.6 1.3 collective-permute-start.5
  87.7 9.6 %collective-permute-done.4 = f32[1,2,256,128]{3,2,1,0:T(8,128)S(1)} collective-permute-done((f32[1,2,256,128]{3,2,1,0:T(8,128)S(1)}, f32[1,2,256,128]{3,2,1,0:T(8,128)S(1)}, u32[]{:S(2)}, u32[]{:S(2)}) %collective-permute-start.4) | collective-permute-done | bytes 262176 | tf_op jit(solution)/shard_map/ppermute | solution.py:19
  97.6 1.5 collective-permute-start.6
  99.1 1.3 collective-permute-start.7
  100.6 2.3 %scatter_custom_fusion = f32[1024]{0:T(1024)S(1)} fusion(s32[256]{0:T(256)S(1)} %bitcast.507, f32[256]{0:T(256)S(1)} %multiply_bitcast_fusion, f32[]{:T(128)} %constant.327.clone.1), kind=kCustom, calls=%fused_computation.181 | custom fusion | flops 256 | bytes 4100 | tf_op jit(solution)/shard_map/scatter-add | solution.py:200
  103.0 0.6 copy.458
  104.7 5.5 %reduce-scatter.2.cloned.1.call-done = f32[16,1,32]{2,0,1:T(8,128)} async-done(((f32[16,2,32]{2,0,1:T(8,128)}), f32[16,1,32]{2,0,1:T(8,128)}) %reduce-scatter.2.cloned.1.call-update) | async-done | bytes 2064 | tf_op jit(solution)/shard_map/reduce_scatter | solution.py:203
  110.2 42.6 %all-reduce.2 = f32[16,1,32]{2,1,0:T(1,128)S(1)} all-reduce(f32[16,1,32]{2,1,0:T(1,128)} %bitcast.506), channel_id=3, replica_groups=mesh['gx'=16,'gz'=2] {'gx'}, use_global_device_ids=true, to_apply=%region_3.4.clone | all-reduce | flops 512 | bytes 4096
  152.8 1.1 dynamic-slice_bitcast_fusion
  154.2 0.7 copy-done.7
  155.9 0.8 copy.457
  (138 shorter events, 12.1 us)
Async XLA Ops:
  7.2 58.9 %copy-start = (s32[1024]{0:T(1024)S(1)}, s32[1024]{0:T(1024)}, u32[]{:S(2)}) copy-start(s32[1024]{0:T(1024)} %param.64) | copy-start | bytes 12292
  7.2 1.3 copy-start.1
  7.2 103.0 %reduce-scatter.2.cloned.1.call-start = ((), (), s32[]{:S(2)}) async-start(), calls=%async_computation.1 | async-start | bytes 24576 | tf_op jit(solution)/shard_map/reduce_scatter | solution.py:203
  8.6 62.5 %collective-permute-start = (f32[1,2,256,128]{3,2,1,0:T(8,128)S(1)}, f32[1,2,256,128]{3,2,1,0:T(8,128)S(1)}, u32[]{:S(2)}, u32[]{:S(2)}) collective-permute-start(f32[1,2,256,128]{3,2,1,0:T(8,128)S(1)} %pad_maximum_fusion.4), channel_id=1, source_target_pairs={{0,2},{2,4},{4,6},{6,8},{8,10},{10,12},{12,14},{14,16},{16,18},{18... | collective-permute-start | bytes 786440 | tf_op jit(solution)/shard_map/ppermute | solution.py:19
  13.5 57.6 %collective-permute-start.1 = (f32[1,2,256,128]{3,2,1,0:T(8,128)S(1)}, f32[1,2,256,128]{3,2,1,0:T(8,128)S(1)}, u32[]{:S(2)}, u32[]{:S(2)}) collective-permute-start(f32[1,2,256,128]{3,2,1,0:T(8,128)S(1)} %pad_maximum_fusion.4), channel_id=1, source_target_pairs={{2,0},{4,2},{6,4},{8,6},{10,8},{12,10},{14,12},{16,14},{18,16},{20... | collective-permute-start | bytes 786440 | tf_op jit(solution)/shard_map/ppermute | solution.py:22
  14.8 0.7 copy-start.16
  15.5 0.7 copy-start.18
  16.2 0.7 copy-start.23
  16.8 4.5 %copy-start.15 = (u32[32]{0:T(128)S(1)}, u32[32]{0:T(128)}, u32[]{:S(2)}) copy-start(u32[32]{0:T(128)} %constant.350) | copy-start | bytes 388
  18.1 0.7 copy-start.22
  22.8 43.2 %copy-start.19 = (s32[1,2,128]{2,1,0:T(2,128)S(1)}, s32[1,2,128]{2,1,0:T(2,128)}, u32[]{:S(2)}) copy-start(s32[1,2,128]{2,1,0:T(2,128)} %param.65) | copy-start | bytes 3076
  67.5 1.4 copy-start.4
  69.2 1.6 copy-start.2
  69.3 0.7 copy-start.17
  69.3 0.7 copy-start.20
  71.2 3.1 %collective-permute-start.2 = (f32[3,1,256,128]{3,2,1,0:T(8,128)S(1)}, f32[3,1,256,128]{3,2,1,0:T(8,128)S(1)}, u32[]{:S(2)}, u32[]{:S(2)}) collective-permute-start(f32[3,1,256,128]{3,2,1,0:T(8,128)S(1)} %get-tuple-element.153), channel_id=1, source_target_pairs={{0,1},{2,3},{4,5},{6,7},{8,9},{10,11},{12,13},{14,15},{16,17},{18,... | collective-permute-start | bytes 1179656 | tf_op jit(solution)/shard_map/ppermute | solution.py:19
  72.5 3.6 %collective-permute-start.3 = (f32[3,1,256,128]{3,2,1,0:T(8,128)S(1)}, f32[3,1,256,128]{3,2,1,0:T(8,128)S(1)}, u32[]{:S(2)}, u32[]{:S(2)}) collective-permute-start(f32[3,1,256,128]{3,2,1,0:T(8,128)S(1)} %get-tuple-element.152), channel_id=1, source_target_pairs={{1,0},{3,2},{5,4},{7,6},{9,8},{11,10},{13,12},{15,14},{17,16},{19,... | collective-permute-start | bytes 1179656 | tf_op jit(solution)/shard_map/ppermute | solution.py:22
  76.2 0.7 copy-start.14
  76.9 0.7 copy-start.13
  77.8 0.7 copy-start.12
  78.5 0.7 copy-start.11
  79.5 0.7 copy-start.6
  80.2 0.7 copy-start.5
  81.3 1.0 copy-start.3
  82.3 0.7 copy-start.10
  82.3 1.0 copy-start.9
  84.3 13.0 %collective-permute-start.4 = (f32[1,2,256,128]{3,2,1,0:T(8,128)S(1)}, f32[1,2,256,128]{3,2,1,0:T(8,128)S(1)}, u32[]{:S(2)}, u32[]{:S(2)}) collective-permute-start(f32[1,2,256,128]{3,2,1,0:T(8,128)S(1)} %pad_maximum_fusion.5), channel_id=1, source_target_pairs={{0,2},{2,4},{4,6},{6,8},{8,10},{10,12},{12,14},{14,16},{16,18},{18... | collective-permute-start | bytes 786440 | tf_op jit(solution)/shard_map/ppermute | solution.py:19
  85.6 11.8 %collective-permute-start.5 = (f32[1,2,256,128]{3,2,1,0:T(8,128)S(1)}, f32[1,2,256,128]{3,2,1,0:T(8,128)S(1)}, u32[]{:S(2)}, u32[]{:S(2)}) collective-permute-start(f32[1,2,256,128]{3,2,1,0:T(8,128)S(1)} %pad_maximum_fusion.5), channel_id=1, source_target_pairs={{2,0},{4,2},{6,4},{8,6},{10,8},{12,10},{14,12},{16,14},{18,16},{20... | collective-permute-start | bytes 786440 | tf_op jit(solution)/shard_map/ppermute | solution.py:22
  97.6 56.4 %collective-permute-start.6 = (f32[3,1,256,128]{3,2,1,0:T(8,128)S(1)}, f32[3,1,256,128]{3,2,1,0:T(8,128)S(1)}, u32[]{:S(2)}, u32[]{:S(2)}) collective-permute-start(f32[3,1,256,128]{3,2,1,0:T(8,128)S(1)} %get-tuple-element.149), channel_id=1, source_target_pairs={{0,1},{2,3},{4,5},{6,7},{8,9},{10,11},{12,13},{14,15},{16,17},{18,... | collective-permute-start | bytes 1179656 | tf_op jit(solution)/shard_map/ppermute | solution.py:19
  99.1 54.9 %collective-permute-start.7 = (f32[3,1,256,128]{3,2,1,0:T(8,128)S(1)}, f32[3,1,256,128]{3,2,1,0:T(8,128)S(1)}, u32[]{:S(2)}, u32[]{:S(2)}) collective-permute-start(f32[3,1,256,128]{3,2,1,0:T(8,128)S(1)} %get-tuple-element.148), channel_id=1, source_target_pairs={{1,0},{3,2},{5,4},{7,6},{9,8},{11,10},{13,12},{15,14},{17,16},{19,... | collective-permute-start | bytes 1179656 | tf_op jit(solution)/shard_map/ppermute | solution.py:22
  103.6 0.7 copy-start.8
  154.2 0.7 copy-start.7
  (1 other events, 0.7 us)
Sparse Core Ops, SparseCore 0:
  103.7 6.4 reduce-scatter.1
where the time goes:
time: 164 us
  blocking collectives  88.2 us (54%)
  local copies, waits for them, and re-layouts  19.1 us (12%)
  waiting for transfers between devices  17.1 us (10%)
  between operations  16.2 us (10%)
  starting transfers between devices  14.2 us (9%)
  matrix products  4.66 us (3%)
  other arithmetic  4.13 us (3%)
    unnamed x3, blocking collectives  88.2 us
    unnamed x57, local copies, waits for them, and re-layouts  11.2 us
    ppermute x4, waiting for transfers between devices, padded_2(): lax.ppermute(lax.slice_in_dim(block, block.shape[dim] - width, None, axis...  9.63 us
    ppermute x4, starting transfers between devices, padded_2(): lax.ppermute(lax.slice_in_dim(block, block.shape[dim] - width, None, axis...  8.97 us
    reduce_scatter x1, waiting for transfers between devices, shards(): summed_z = lax.psum_scatter(blocks, 'gz', scatter_dimension=1, tiled=True)  5.53 us
    ppermute x4, starting transfers between devices, padded_2(): lax.ppermute(lax.slice_in_dim(block, 0, width, axis=dim), axis, backward)  5.17 us
    dot_general x12, matrix products, flux(): jnp.einsum('gf,xzfpqy->xzgpqy', flux_matrix(axis, sign), values, precisio...  3.38 us
  transfers between devices with their start and end apart: 9, of which 4 were waited for; matrix products, arithmetic and copies ran while one was open for 7% of the time, Pallas kernels for 0%

commit v1 on v0

v1 whole, which is shorter than its diff:
```python
import functools
import math

import jax
import jax.numpy as jnp
import numpy as np
from jax import lax
from jax.experimental import pallas as pl
from jax.experimental.pallas import tpu as pltpu
from jax.sharding import PartitionSpec as P

SCALE = 0.25
JUMP = 0.75
LANES = 128
VMEM = pl.BlockSpec(memory_space=pltpu.VMEM)

X_FIELDS, X_TRACES, X_SLOTS, X_BLOCKS = 0, 16, 28, 29
Z_SLOTS, Z_BLOCKS = 32, 33
W_CORNERS, W_BLOCKS = 32, 48


def derivative_matrix():
    points = np.array([-1.0, -math.sqrt(0.2), math.sqrt(0.2), 1.0])
    products = np.array(
        [
            np.prod([points[first] - points[other] for other in range(4) if other != first])
            for first in range(4)
        ]
    )
    matrix = np.zeros((4, 4))
    for first in range(4):
        for second in range(4):
            if first != second:
                matrix[first, second] = (
                    products[first] / products[second] / (points[first] - points[second])
                )
        matrix[first, first] = sum(
            (1.0 / (points[first] - points[other]) for other in range(4) if other != first)
        )
    return matrix


class Rows:
    def __init__(self):
        row = lax.broadcasted_iota(jnp.int32, (8, LANES), 0)
        self.upper = row >= 4
        self.c = row & 3

    def halves(self, low, high):
        return jnp.where(self.upper, jnp.float32(high), jnp.float32(low))

    def by_c(self, values):
        result = jnp.full((8, LANES), values[0], jnp.float32)
        for c in range(1, 4):
            result = jnp.where(self.c == c, jnp.float32(values[c]), result)
        return result


class Derivative:
    def __init__(self, rows, matrix):
        self.matrix = matrix
        self.same = [
            [rows.halves(matrix[2 * h, 2 * g], matrix[2 * h + 1, 2 * g + 1]) for g in range(2)]
            for h in range(2)
        ]
        self.cross = [
            [rows.halves(matrix[2 * h, 2 * g + 1], matrix[2 * h + 1, 2 * g]) for g in range(2)]
            for h in range(2)
        ]
        self.shift = {
            delta: rows.by_c(
                [matrix[c, c + delta] if 0 <= c + delta < 4 else 0.0 for c in range(4)]
            )
            for delta in range(-3, 4)
        }

    def along(self, axis, u):
        if axis == 0:
            return jnp.stack(
                [sum(float(self.matrix[a, j]) * u[j] for j in range(4)) for a in range(4)]
            )
        if axis == 1:
            swapped = pltpu.roll(u, 4, 2)
            return jnp.stack(
                [
                    sum(self.same[h][g] * u[:, g] + self.cross[h][g] * swapped[:, g] for g in range(2))
                    for h in range(2)
                ],
                axis=1,
            )
        return sum(
            coefficient * (u if delta == 0 else pltpu.roll(u, -delta % 8, 2))
            for delta, coefficient in self.shift.items()
        )


def traces(fields, axis, sign):
    others = [fields[f] for f in range(3) if f != axis]
    return others + [fields[axis] + sign * fields[3]]


def face_terms(inner, outer, axis, sign, weight, adjoint):
    tangential = [weight * (i - o) for i, o in zip(inner[:2], outer[:2])]
    normal = weight * (inner[2] - outer[2])
    if adjoint:
        pressure = (-sign) * (weight * (inner[2] + outer[2]))
    else:
        pressure = (-sign) * normal
    terms = tangential[:]
    terms.insert(axis, normal)
    return terms + [pressure]


def y_terms(fields, rows, adjoint):
    high_weight = rows.halves(0.0, JUMP)
    low_weight = rows.halves(JUMP, 0.0)
    first = [field[:, 0] for field in fields]
    second = [field[:, 1] for field in fields]
    moved = lambda value, step: pltpu.roll(pltpu.roll(value, 4, 1), step, 2)
    flip = 1.0 if adjoint else -1.0
    high_out = [moved(t, LANES - 1) for t in traces(first, 1, flip)]
    high = face_terms(traces(second, 1, -1.0), high_out, 1, 1.0, high_weight, adjoint)
    low_out = [moved(t, 1) for t in traces(second, 1, -flip)]
    low = face_terms(traces(first, 1, 1.0), low_out, 1, -1.0, low_weight, adjoint)
    return [jnp.stack([l, h], axis=1) for l, h in zip(low, high)]


def z_terms(inner, outer_fields, sign, weight, adjoint):
    flip = sign if adjoint else -sign
    outer = [pltpu.roll(t, 3 if sign > 0 else 5, t.ndim - 2) for t in traces(outer_fields, 2, flip)]
    return face_terms(traces(inner, 2, -sign), outer, 2, sign, weight, adjoint)


def wall_terms(fields, axis, sign, weight, flag, adjoint):
    inner = traces(fields, axis, -sign)
    image = inner[2] if adjoint else fields[axis] + sign * fields[3]
    outer = inner[:2] + [(1.0 - 2.0 * flag) * image]
    return face_terms(inner, outer, axis, sign, weight, adjoint)


def z_weights(rows):
    return {-1: jnp.where(rows.c == 0, JUMP, 0.0), 1: jnp.where(rows.c == 3, JUMP, 0.0)}


def load(ref, z):
    return [ref[z, f] for f in range(4)]


def local_kernel(sizes, state, target, cell_of, cell_slot, z_wall, local, pay_a, pay_b, *z_pay):
    nx, nz = sizes
    x_place, z_place = lax.axis_index("gx"), lax.axis_index("gz")
    rows = Rows()
    derivative = Derivative(rows, derivative_matrix())
    weights = z_weights(rows)
    cell_rows = cell_slot.shape[0]
    slots = []
    for z in range(2):
        row_of = lax.shift_right_logical(cell_of[z : z + 1, :], 7)
        slot = jnp.zeros((1, LANES), jnp.int32)
        for step in (-1, 0, 1):
            row = (x_place // 4 + step) * nz + z_place
            row = jnp.clip(row, 0, cell_rows - 1)
            slot = jnp.where(row_of == row, cell_slot[pl.ds(row, 1), :], slot)
        slots.append(slot.astype(jnp.float32))
    row = lax.broadcasted_iota(jnp.int32, (8, LANES), 0)
    slot_block = jnp.where(row == 0, slots[0], jnp.where(row == 1, slots[1], 0.0))
    even = x_place % 2 == 0
    pay_a[X_SLOTS] = slot_block
    pay_b[X_SLOTS] = slot_block
    for z in range(2):
        u = load(state, z)
        other = load(state, 1 - z)
        grads = [derivative.along(k, u[3]) for k in range(3)]
        divergence = sum(derivative.along(k, u[k]) for k in range(3))
        jumps = y_terms(u, rows, False)
        sign = 1.0 if z == 0 else -1.0
        across = z_terms(u, other, sign, weights[int(sign)], False)
        end = (z_place == 0) if z == 0 else (z_place == nz - 1)
        weight = weights[-int(sign)] * jnp.where(end, 1.0, 0.0)
        flag = z_wall[z : z + 1, :].astype(jnp.float32)
        wall = wall_terms(u, 2, -sign, weight, flag, False)
        result = [
            SCALE * v + j + a + w - target[z, f]
            for f, (v, j, a, w) in enumerate(zip(grads + [divergence], jumps, across, wall))
        ]
        for f in range(4):
            local[z, f] = result[f]
        low = [u[f][0] for f in range(4)] + traces([r[0] for r in result], 0, 1.0)[2:] + [
            result[f][0] for f in (1, 2)
        ]
        high = [u[f][3] for f in range(4)] + traces([r[3] for r in result], 0, -1.0)[2:] + [
            result[f][3] for f in (1, 2)
        ]
        for j in range(7):
            pay_a[pl.ds(4 * j + 2 * z, 2)] = jnp.where(even, high[j], low[j])
            pay_b[pl.ds(4 * j + 2 * z, 2)] = jnp.where(even, low[j], high[j])
    if nz == 2:
        layer = 1 - z_place
        for f in range(4):
            z_pay[0][pl.ds(8 * f, 8)] = state[layer, f].reshape(8, 8, LANES)
        z_pay[0][Z_SLOTS] = jnp.broadcast_to(jnp.where(layer == 0, slots[0], slots[1]), (8, LANES))
    else:
        for direction in range(2):
            layer = 1 - direction
            for f in range(4):
                z_pay[direction][pl.ds(8 * f, 8)] = state[layer, f].reshape(8, 8, LANES)
            z_pay[direction][Z_SLOTS] = jnp.broadcast_to(slots[layer], (8, LANES))


def x_side(side, even, got_a, got_b, block):
    a, b = got_a[pl.ds(block, 2)], got_b[pl.ds(block, 2)]
    return jnp.where(even, b, a) if side == 0 else jnp.where(even, a, b)


def sums_kernel(
    sizes, state, local, got_a, got_b, x_wall, logk, own_slots, *refs
):
    nx, nz = sizes
    count = 1 if nz == 2 else 2
    z_got, (whole, send), z_pay = refs[:count], refs[count : count + 2], refs[count + 2 :]
    z_from = [z_got[0], z_got[-1]]
    x_place, z_place = lax.axis_index("gx"), lax.axis_index("gz")
    even = x_place % 2 == 0
    rows = Rows()
    weights = z_weights(rows)
    corners = {}
    first_sums, second_sums = [], []
    for z in range(2):
        u = load(state, z)
        for f in range(4):
            whole[z, f] = local[z, f]
        sign = -1 if z == 0 else 1
        inside = (z_place > 0) if z == 0 else (z_place < nz - 1)
        outer = [z_from[z][pl.ds(8 * f, 8)].reshape(4, 2, 8, LANES) for f in range(4)]
        terms = z_terms(u, outer, float(sign), weights[sign] * jnp.where(inside, 1.0, 0.0), False)
        for f in range(4):
            whole[z, f] += terms[f]
        for side in range(2):
            sign = 1.0 if side else -1.0
            a = 3 * side
            end = (x_place == nx - 1) if side else (x_place == 0)
            mine = [u[f][a] for f in range(4)]
            theirs = [x_side(side, even, got_a, got_b, 4 * f + 2 * z) for f in range(4)]
            corners[side, z] = theirs
            flag = x_wall[side, z : z + 1, :].astype(jnp.float32)
            inner = traces(mine, 0, -sign)
            image = (1.0 - 2.0 * flag) * (mine[0] + sign * mine[3])
            outer = [
                jnp.where(end, e, o)
                for e, o in zip(inner[:2] + [image], traces(theirs, 0, -sign))
            ]
            terms = face_terms(inner, outer, 0, sign, JUMP, False)
            for f in range(4):
                whole[z, f, a] += terms[f]
        first = sum(whole[z, k] * u[k] for k in range(3))
        second = sum(u[k] * u[k] for k in range(3))
        first_sums.append(jnp.sum(first, axis=(0, 1, 2))[None])
        second_sums.append(jnp.sum(second, axis=(0, 1, 2))[None])
    length = logk.shape[1]
    devices = send.shape[0]
    slots = own_slots[X_SLOTS].astype(jnp.int32)
    total = jnp.zeros((devices, LANES), jnp.float32)
    place = lax.broadcasted_iota(jnp.int32, (LANES, LANES), 0)
    owner = lax.broadcasted_iota(jnp.int32, (devices, LANES), 0)
    for z in range(2):
        slot = slots[z : z + 1, :]
        chosen = jnp.where(owner == slot // length, 1.0, 0.0).astype(jnp.bfloat16)
        position = slot % length
        values = jnp.where(
            place == position + length,
            first_sums[z],
            jnp.where(place == position + 2 * length, second_sums[z], 0.0),
        )
        for _ in range(3):
            piece = values.astype(jnp.bfloat16)
            total += lax.dot_general(
                chosen, piece, (((1,), (1,)), ((), ())), preferred_element_type=jnp.float32
            )
            values = values - piece.astype(jnp.float32)
    send[...] = total
    send[:, 0:length] = jnp.broadcast_to(logk[...], (devices, length))
    for direction in range(count):
        layer = 1 - z_place if nz == 2 else 1 - direction
        for f in range(4):
            z_pay[direction][pl.ds(8 * f, 8)] = whole[layer, f].reshape(8, 8, LANES)
            for side in range(2):
                if nz == 2:
                    value = jnp.where(layer == 0, corners[side, 0][f], corners[side, 1][f])
                else:
                    value = corners[side, layer][f]
                z_pay[direction][pl.ds(W_CORNERS + 8 * side + 2 * f, 2)] = value


def look_up(table, length, slots):
    devices = table.shape[0]
    fold = LANES // length
    table_rows = devices // fold
    chunk = min(8, table_rows)
    lane = lax.broadcasted_iota(jnp.int32, (chunk, LANES), 1)
    in_lane = slots & (LANES - 1)
    in_row = lax.shift_right_logical(slots, 7)

    def step(index, result):
        rows = jnp.zeros((chunk, LANES), jnp.float32)
        for j in range(fold):
            part = table[pl.ds(index * chunk * fold + j, chunk, stride=fold), :]
            rows += pltpu.roll(jnp.where(lane < length, part, 0.0), j * length, 1)
        for i in range(chunk):
            wide = jnp.broadcast_to(rows[i : i + 1, :], (8, LANES))
            taken = jnp.take_along_axis(wide, in_lane, axis=1)
            result = jnp.where(in_row == index * chunk + i, taken, result)
        return result

    result = jnp.zeros((8, LANES), jnp.float32)
    if table_rows == chunk:
        return step(0, result)
    return lax.fori_loop(0, table_rows // chunk, step, result)


def adjoint_kernel(sizes, state, whole, got_a, got_b, own_slots, x_wall, z_wall, received, logk, *refs):
    nx, nz = sizes
    count = 1 if nz == 2 else 2
    z_got, w_got, (adjoint, gradient) = refs[:count], refs[count : 2 * count], refs[2 * count :]
    z_from, w_from = [z_got[0], z_got[-1]], [w_got[0], w_got[-1]]
    x_place, z_place = lax.axis_index("gx"), lax.axis_index("gz")
    even = x_place % 2 == 0
    rows = Rows()
    weights = z_weights(rows)
    derivative = Derivative(rows, derivative_matrix().T)
    length = logk.shape[1]
    held = jnp.exp(-logk[...])
    summed = jnp.sum(received[...], axis=0, keepdims=True)
    first, second = summed[:, length : 2 * length], summed[:, 2 * length : 3 * length]
    gradient[...] = -(SCALE / 64.0) * held * (first + SCALE * held * second)
    slot_a, slot_b = got_a[X_SLOTS], got_b[X_SLOTS]
    row = lax.broadcasted_iota(jnp.int32, (8, LANES), 0)
    slots = own_slots[X_SLOTS]
    slots = jnp.where(row // 2 == 1, pltpu.roll(jnp.where(even, slot_b, slot_a), 2, 0), slots)
    slots = jnp.where(row // 2 == 2, pltpu.roll(jnp.where(even, slot_a, slot_b), 4, 0), slots)
    slots = jnp.where(row == 6, z_from[0][Z_SLOTS], slots)
    slots = jnp.where(row == 7, z_from[1][Z_SLOTS], slots)
    quarter = jnp.exp(-look_up(received, length, slots.astype(jnp.int32)))
    resistance = [quarter[i : i + 1, :] for i in range(8)]
    residual = []
    for z in range(2):
        scaled = SCALE * resistance[z]
        residual.append(
            [whole[z, k] + scaled * state[z, k] for k in range(3)] + [whole[z, 3]]
        )
    for z in range(2):
        w = residual[z]
        jumps = y_terms(w, rows, True)
        sign = 1 if z == 0 else -1
        across = z_terms(w, residual[1 - z], float(sign), weights[sign], True)
        sign = -sign
        end = (z_place == 0) if z == 0 else (z_place == nz - 1)
        scaled = SCALE * resistance[6 + z]
        theirs = [w_from[z][pl.ds(8 * f, 8)].reshape(4, 2, 8, LANES) for f in range(4)]
        for k in range(3):
            field = z_from[z][pl.ds(8 * k, 8)].reshape(4, 2, 8, LANES)
            theirs[k] = theirs[k] + scaled * field
        flag = z_wall[z : z + 1, :].astype(jnp.float32)
        inner = traces(w, 2, -float(sign))
        outer = [
            pltpu.roll(t, 3 if sign > 0 else 5, 2) for t in traces(theirs, 2, float(sign))
        ]
        image = inner[:2] + [(1.0 - 2.0 * flag) * inner[2]]
        outer = [jnp.where(end, i, o) for i, o in zip(image, outer)]
        beyond = face_terms(inner, outer, 2, float(sign), weights[sign], True)
        grads = [derivative.along(k, w[3]) for k in range(3)]
        divergence = sum(derivative.along(k, w[k]) for k in range(3))
        volume = [SCALE * (resistance[z] * w[k] + grads[k]) for k in range(3)]
        volume.append(SCALE * divergence)
        for f in range(4):
            adjoint[z, f] = volume[f] + jumps[f] + across[f] + beyond[f]
        for side in range(2):
            a = 3 * side
            s = 1.0 if side else -1.0
            u_out = [x_side(side, even, got_a, got_b, 4 * f + 2 * z) for f in range(4)]
            trace = [
                x_side(side, even, got_a, got_b, X_TRACES + 4 * j + 2 * z) for j in range(3)
            ]
            normal, tangential = trace[0], trace[1:]
            mine = traces([state[z, f, a] for f in range(4)], 0, s)
            there = traces(u_out, 0, s)
            normal = normal - (2.0 * JUMP) * (mine[2] - there[2])
            tangential = [t - JUMP * (m - o) for t, m, o in zip(tangential, mine[:2], there[:2])]
            t = float(sign)
            weight = weights[sign] * jnp.where(end, 0.0, 1.0)
            corner = [
                w_from[z][pl.ds(W_CORNERS + 8 * side + 2 * f, 2)] for f in range(4)
            ]
            edge = z_terms(u_out, corner, t, weight, False)
            normal = normal + edge[0] + s * edge[3]
            tangential = [tangential[0] + edge[1], tangential[1] + edge[2]]
            scaled = SCALE * resistance[2 + 2 * side + z]
            normal = normal + scaled * u_out[0]
            tangential = [v + scaled * u_out[1 + j] for j, v in enumerate(tangential)]
            inner = traces([w[f][a] for f in range(4)], 0, -s)
            flag = x_wall[side, z : z + 1, :].astype(jnp.float32)
            image = inner[:2] + [(1.0 - 2.0 * flag) * inner[2]]
            last = (x_place == nx - 1) if side else (x_place == 0)
            outer = [jnp.where(last, i, o) for i, o in zip(image, tangential + [normal])]
            terms = face_terms(inner, outer, 0, s, JUMP, True)
            for f in range(4):
                adjoint[z, f, a] += terms[f]


def call(kernel, shapes, operands, flops):
    return pl.pallas_call(
        kernel,
        out_shape=[jax.ShapeDtypeStruct(shape, jnp.float32) for shape in shapes],
        in_specs=[VMEM] * len(operands),
        out_specs=[VMEM] * len(shapes),
        compiler_params=pltpu.CompilerParams(vmem_limit_bytes=32 * 1024 * 1024),
        cost_estimate=pl.CostEstimate(flops=flops, bytes_accessed=800000, transcendentals=0),
    )(*operands)


def both_ways(pairs):
    return pairs + [(second, first) for first, second in pairs]


def along_z(payloads, nz):
    if nz == 2:
        return [lax.ppermute(payloads[0], "gz", [(0, 1), (1, 0)])]
    up = [(i, i + 1) for i in range(nz - 1)]
    down = [(second, first) for first, second in up]
    return [lax.ppermute(payloads[0], "gz", up), lax.ppermute(payloads[1], "gz", down)]


def shards(nx, nz, state, target, coarse_logk, cell_slot, cell_of, wall_flags_xaxis, z_wall):
    sizes = (nx, nz)
    shape = (2, 4, 4, 2, 8, LANES)
    state6 = state.reshape(shape)
    target6 = target.reshape(shape)
    logk = coarse_logk.reshape(1, -1)
    slots2 = cell_slot.reshape(-1, LANES)
    cells2 = cell_of.reshape(2, LANES)
    z_flags = z_wall.reshape(2, LANES)
    count = 1 if nz == 2 else 2
    x_shape, z_shape, w_shape = ((n, 8, LANES) for n in (X_BLOCKS, Z_BLOCKS, W_BLOCKS))
    local, pay_a, pay_b, *z_pay = call(
        functools.partial(local_kernel, sizes),
        [shape, x_shape, x_shape] + [z_shape] * count,
        [state6, target6, cells2, slots2, z_flags],
        2000000,
    )
    pairs_b = both_ways([(i, i + 1) for i in range(1, nx - 1, 2)])
    pairs_a = both_ways([(i, i + 1) for i in range(0, nx - 1, 2)])
    got_b = lax.ppermute(pay_b, "gx", pairs_b)
    got_a = lax.ppermute(pay_a, "gx", pairs_a)
    z_got = along_z(z_pay, nz)
    whole, send, *w_pay = call(
        functools.partial(sums_kernel, sizes),
        [shape, (nx * nz, LANES)] + [w_shape] * count,
        [state6, local, got_a, got_b, wall_flags_xaxis, logk, pay_a] + z_got,
        2000000,
    )
    w_got = along_z(w_pay, nz)
    received = lax.all_to_all(send, ("gx", "gz"), 0, 0, tiled=True)
    adjoint, gradient = call(
        functools.partial(adjoint_kernel, sizes),
        [shape, logk.shape],
        [state6, whole, got_a, got_b, pay_a, wall_flags_xaxis, z_flags, received, logk]
        + z_got
        + w_got,
        2000000,
    )
    return adjoint.reshape(state.shape), gradient.reshape(-1)


def solution(mesh):
    placed = (
        P("gx", "gz", None, None, None),
        P("gx", "gz", None, None, None),
        P(("gx", "gz")),
        P(),
        P("gx", "gz", None),
        P(None, "gz", None),
        P(None, "gx", None),
    )
    return jax.shard_map(
        functools.partial(shards, mesh.shape["gx"], mesh.shape["gz"]),
        mesh=mesh,
        in_specs=placed,
        out_specs=(P("gx", "gz", None, None, None), P(("gx", "gz"))),
        check_vma=False,
    )
```

time: 164 us -> 30.5 us (0.19)
  blocking collectives: 88.2 us -> 11.9 us
  local copies, waits for them, and re-layouts: 19.1 us -> 3.24 us
  between operations: 16.2 us -> 0.7 us
  waiting for transfers between devices: 17.1 us -> 6.05 us
  starting transfers between devices: 14.2 us -> 6.48 us
  matrix products: 4.66 us -> 0 us
  other arithmetic: 4.13 us -> 0 us
  Pallas kernels: 0 us -> 1.87 us
    unnamed x3 -> x0, blocking collectives: 88.2 us -> none
    all_to_all x0 -> x1, blocking collectives: none -> 11.9 us  [shards(): received = lax.all_to_all(send, ('gx', 'gz'), 0, 0, tiled=True)]
    unnamed x57 -> x14, local copies, waits for them, and re-layouts: 11.2 us -> 3.24 us
    ppermute x8 -> x4, starting transfers between devices: 14.1 us -> 6.48 us  [the longest x1 5.31 us: shards(): got_a = lax.ppermute(pay_a, 'gx', pairs_a)]
    ppermute x8 -> x4, waiting for transfers between devices: 11.6 us -> 6.05 us  [the longest x1 6.04 us: shards(): got_a = lax.ppermute(pay_a, 'gx', pairs_a)]
    reduce_scatter x1 -> x0, waiting for transfers between devices: 5.53 us -> none  [shards(): summed_z = lax.psum_scatter(blocks, 'gz', scatter_dimension=1, tiled=True)]
    dot_general x16 -> x0, matrix products: 4.66 us -> none  [the longest x12 3.38 us: flux(): jnp.einsum('gf,xzfpqy->xzgpqy', flux_matrix(axis, sign), values, precisio...]
    scatter-add x6 -> x0, other arithmetic: 2.83 us -> none  [the longest x1 2.32 us: shards(): jnp.zeros((total_cells,), jnp.float32).at[slots.reshape(-1)]]
  transfers between devices with their start and end apart: 9 -> 4, of which waited for: 4 -> 1; matrix products, arithmetic and copies ran while one was open for 7% -> 0% of each run, Pallas kernels for 0% -> 0%
where the time goes in v1:
time: 30.5 us; the launch traced here: 30.3 us
  blocking collectives  11.9 us (39%)
  starting transfers between devices  6.48 us (21%)
  waiting for transfers between devices  6.05 us (20%)
  local copies, waits for them, and re-layouts  3.24 us (11%)
  Pallas kernels  1.87 us (6%)
  between operations  0.7 us (2%)
    all_to_all x1, blocking collectives, shards(): received = lax.all_to_all(send, ('gx', 'gz'), 0, 0, tiled=True)  11.9 us
    ppermute x1, waiting for transfers between devices, shards(): got_a = lax.ppermute(pay_a, 'gx', pairs_a)  6.04 us
    ppermute x1, starting transfers between devices, shards(): got_a = lax.ppermute(pay_a, 'gx', pairs_a)  5.31 us
    unnamed x14, local copies, waits for them, and re-layouts  3.24 us
    pallas_call x3, Pallas kernels, call(): pl.pallas_call(kernel, out_shape=[jax.ShapeDtypeStruct(shape, jnp.float32...  1.87 us
    ppermute x1, starting transfers between devices, shards(): got_b = lax.ppermute(pay_b, 'gx', pairs_b)  0.66 us
  transfers between devices with their start and end apart: 4, of which 1 were waited for; matrix products, arithmetic and copies ran while one was open for 0% of the time, Pallas kernels for 0%

profile of v1, /device:TPU:0, one launch (start us, length us, event | category | flops | bytes accessed | tf_op | source)
XLA Modules:
  0.0 30.3 jit_solution(16124023210407725532)
XLA Ops:
  0.6 0.0 copy-start.3
  0.6 0.0 copy-start.6
  0.7 0.0 copy-start.4
  0.7 0.7 %copy-done.3 = s32[1024]{0:T(1024)S(1)} copy-done((s32[1024]{0:T(1024)S(1)}, s32[1024]{0:T(1024)}, u32[]{:S(2)}) %copy-start.3) | copy-done | bytes 4120
  1.3 0.0 copy-done.6
  1.3 0.0 copy-done.4
  1.3 0.0 copy-start
  1.3 0.9 %copy-done = f32[1,2,4,64,128]{4,3,2,1,0:T(8,128)S(1)} copy-done((f32[1,2,4,64,128]{4,3,2,1,0:T(8,128)S(1)}, f32[1,2,4,64,128]{4,3,2,1,0:T(8,128)}, u32[]{:S(2)}) %copy-start) | copy-done | bytes 262168
  2.3 0.0 copy-start.1
  2.3 0.9 %copy-done.1 = f32[1,2,4,64,128]{4,3,2,1,0:T(8,128)S(1)} copy-done((f32[1,2,4,64,128]{4,3,2,1,0:T(8,128)S(1)}, f32[1,2,4,64,128]{4,3,2,1,0:T(8,128)}, u32[]{:S(2)}) %copy-start.1) | copy-done | bytes 262168
  3.2 0.3 %shard_map.86 = (f32[2,4,4,2,8,128]{5,4,3,2,1,0:T(8,128)S(1)}, f32[29,8,128]{2,1,0:T(8,128)S(1)}, f32[29,8,128]{2,1,0:T(8,128)S(1)}, f32[33,8,128]{2,1,0:T(8,128)S(1)}) custom-call(f32[2,4,4,2,8,128]{5,4,3,2,1,0:T(8,128)S(1)} %bitcast.12, f32[2,4,4,2,8,128]{5,4,3,2,1,0:T(8,128)S(1)} %bitcast.15, s32[2,128]{1,0:T(2,128)S(1)} %bitcast.23, ...), custom_call_target="tpu_custom_call" | custom-call | flops 2000000 | bytes 800000 | tf_op jit(solution)/shard_map/pallas_call | solution.py:410
  3.5 0.5 %collective-permute-start.2 = (f32[33,8,128]{2,1,0:T(8,128)S(1)}, f32[33,8,128]{2,1,0:T(8,128)S(1)}, u32[]{:S(2)}, u32[]{:S(2)}) collective-permute-start(f32[33,8,128]{2,1,0:T(8,128)S(1)} %get-tuple-element.14), channel_id=1, source_target_pairs={{0,1},{1,0},{2,3},{3,2},{4,5},{5,4},{6,7},{7,6},{8,9},{9,8},{10,11... | collective-permute-start | bytes 405512 | tf_op jit(solution)/shard_map/ppermute | solution.py:426
  4.1 0.7 %collective-permute-start.1 = (f32[29,8,128]{2,1,0:T(8,128)S(1)}, f32[29,8,128]{2,1,0:T(8,128)S(1)}, u32[]{:S(2)}, u32[]{:S(2)}) collective-permute-start(f32[29,8,128]{2,1,0:T(8,128)S(1)} %get-tuple-element.13), channel_id=1, source_target_pairs={{2,4},{6,8},{10,12},{14,16},{18,20},{22,24},{26,28},{4,2},{8,6},{1... | collective-permute-start | bytes 356360 | tf_op jit(solution)/shard_map/ppermute | solution.py:451
  4.7 0.0 copy-start.2
  4.7 5.3 %collective-permute-start = (f32[29,8,128]{2,1,0:T(8,128)S(1)}, f32[29,8,128]{2,1,0:T(8,128)S(1)}, u32[]{:S(2)}, u32[]{:S(2)}) collective-permute-start(f32[29,8,128]{2,1,0:T(8,128)S(1)} %get-tuple-element.12.own_slots), channel_id=1, source_target_pairs={{0,2},{4,6},{8,10},{12,14},{16,18},{20,22},{24,26},{28,30},{2,0},{... | collective-permute-start | bytes 356360 | tf_op jit(solution)/shard_map/ppermute | solution.py:452
  10.1 0.0 collective-permute-done.1.got_b
  10.1 6.0 %collective-permute-done.got_a = f32[29,8,128]{2,1,0:T(8,128)S(1)} collective-permute-done((f32[29,8,128]{2,1,0:T(8,128)S(1)}, f32[29,8,128]{2,1,0:T(8,128)S(1)}, u32[]{:S(2)}, u32[]{:S(2)}) %collective-permute-start) | collective-permute-done | bytes 118816 | tf_op jit(solution)/shard_map/ppermute | solution.py:452
  16.1 0.0 collective-permute-done.2.refs_0_
  16.1 0.0 copy-start.5
  16.1 0.0 copy-done.2
  16.1 0.6 %copy-done.5 = f32[32]{0:T(128)S(1)} copy-done((f32[32]{0:T(128)S(1)}, f32[32]{0:T(128)}, u32[]{:S(2)}) %copy-start.5) | copy-done | bytes 152
  16.8 0.3 %shard_map.87 = (f32[2,4,4,2,8,128]{5,4,3,2,1,0:T(8,128)S(1)}, f32[32,128]{1,0:T(8,128)S(1)}, f32[48,8,128]{2,1,0:T(8,128)S(1)}) custom-call(f32[2,4,4,2,8,128]{5,4,3,2,1,0:T(8,128)S(1)} %bitcast.13, f32[2,4,4,2,8,128]{5,4,3,2,1,0:T(8,128)S(1)} %get-tuple-element.11.local, f32[29,8,128]{2,1,0:T(8,128)S(1)} %collective-permute-done.got_a, ...), custom_call_target="tpu_custom_call" | custom-call | flops 2000000 | bytes 800000 | tf_op jit(solution)/shard_map/pallas_call | solution.py:410
  17.1 0.0 collective-permute-start.3
  17.1 11.9 %all_to_all.11 = f32[32,1,128]{2,1,0:T(1,128)S(1)} all-to-all(f32[32,1,128]{2,1,0:T(1,128)S(1)} %bitcast.17), channel_id=1, replica_groups=mesh['gx'=16,'gz'=2] {'gx','gz'}, dimensions={0} | all-to-all | bytes 32768 | tf_op jit(solution)/shard_map/all_to_all | solution.py:461
  29.0 0.0 collective-permute-done.3.refs_1_
  29.0 1.2 %shard_map.88 = (f32[2,4,4,2,8,128]{5,4,3,2,1,0:T(8,128)}, f32[1,32]{1,0:T(1,128)}) custom-call(f32[2,4,4,2,8,128]{5,4,3,2,1,0:T(8,128)S(1)} %bitcast.14, f32[2,4,4,2,8,128]{5,4,3,2,1,0:T(8,128)S(1)} %get-tuple-element.15.whole, f32[29,8,128]{2,1,0:T(8,128)S(1)} %collective-permute-done.got_a, f32[29,8,128]{2,1,0:T(8,128)S(1)} %collective-permute-done.1.got_b, ...), custom_call_target="tpu_custom_call" | custom-call | flops 2000000 | bytes 800000 | tf_op jit(solution)/shard_map/pallas_call | solution.py:410
Async XLA Ops:
  0.6 0.7 %copy-start.3 = (s32[1024]{0:T(1024)S(1)}, s32[1024]{0:T(1024)}, u32[]{:S(2)}) copy-start(s32[1024]{0:T(1024)} %param.10) | copy-start | bytes 12292
  0.6 0.7 %copy-start.6 = (s32[1,2,128]{2,1,0:T(2,128)S(1)}, s32[1,2,128]{2,1,0:T(2,128)}, u32[]{:S(2)}) copy-start(s32[1,2,128]{2,1,0:T(2,128)} %param.11) | copy-start | bytes 3076
  0.7 0.7 %copy-start.4 = (s32[2,1,128]{2,1,0:T(1,128)S(1)}, s32[2,1,128]{2,1,0:T(1,128)}, u32[]{:S(2)}) copy-start(s32[2,1,128]{2,1,0:T(1,128)} %param.13) | copy-start | bytes 3076
  1.3 0.9 %copy-start = (f32[1,2,4,64,128]{4,3,2,1,0:T(8,128)S(1)}, f32[1,2,4,64,128]{4,3,2,1,0:T(8,128)}, u32[]{:S(2)}) copy-start(f32[1,2,4,64,128]{4,3,2,1,0:T(8,128)} %param.7) | copy-start | bytes 786436
  2.3 0.9 %copy-start.1 = (f32[1,2,4,64,128]{4,3,2,1,0:T(8,128)S(1)}, f32[1,2,4,64,128]{4,3,2,1,0:T(8,128)}, u32[]{:S(2)}) copy-start(f32[1,2,4,64,128]{4,3,2,1,0:T(8,128)} %param.8) | copy-start | bytes 786436
  3.5 12.5 %collective-permute-start.2 = (f32[33,8,128]{2,1,0:T(8,128)S(1)}, f32[33,8,128]{2,1,0:T(8,128)S(1)}, u32[]{:S(2)}, u32[]{:S(2)}) collective-permute-start(f32[33,8,128]{2,1,0:T(8,128)S(1)} %get-tuple-element.14), channel_id=1, source_target_pairs={{0,1},{1,0},{2,3},{3,2},{4,5},{5,4},{6,7},{7,6},{8,9},{9,8},{10,11... | collective-permute-start | bytes 405512 | tf_op jit(solution)/shard_map/ppermute | solution.py:426
  4.1 6.0 %collective-permute-start.1 = (f32[29,8,128]{2,1,0:T(8,128)S(1)}, f32[29,8,128]{2,1,0:T(8,128)S(1)}, u32[]{:S(2)}, u32[]{:S(2)}) collective-permute-start(f32[29,8,128]{2,1,0:T(8,128)S(1)} %get-tuple-element.13), channel_id=1, source_target_pairs={{2,4},{6,8},{10,12},{14,16},{18,20},{22,24},{26,28},{4,2},{8,6},{1... | collective-permute-start | bytes 356360 | tf_op jit(solution)/shard_map/ppermute | solution.py:451
  4.7 11.4 %copy-start.2 = (s32[2,2,128]{2,1,0:T(2,128)S(1)}, s32[2,2,128]{2,1,0:T(2,128)}, u32[]{:S(2)}) copy-start(s32[2,2,128]{2,1,0:T(2,128)} %x_wall.3) | copy-start | bytes 6148
  4.7 11.4 %collective-permute-start = (f32[29,8,128]{2,1,0:T(8,128)S(1)}, f32[29,8,128]{2,1,0:T(8,128)S(1)}, u32[]{:S(2)}, u32[]{:S(2)}) collective-permute-start(f32[29,8,128]{2,1,0:T(8,128)S(1)} %get-tuple-element.12.own_slots), channel_id=1, source_target_pairs={{0,2},{4,6},{8,10},{12,14},{16,18},{20,22},{24,26},{28,30},{2,0},{... | collective-permute-start | bytes 356360 | tf_op jit(solution)/shard_map/ppermute | solution.py:452
  16.1 0.7 %copy-start.5 = (f32[32]{0:T(128)S(1)}, f32[32]{0:T(128)}, u32[]{:S(2)}) copy-start(f32[32]{0:T(128)} %param.9) | copy-start | bytes 388
  17.1 11.9 %collective-permute-start.3 = (f32[48,8,128]{2,1,0:T(8,128)S(1)}, f32[48,8,128]{2,1,0:T(8,128)S(1)}, u32[]{:S(2)}, u32[]{:S(2)}) collective-permute-start(f32[48,8,128]{2,1,0:T(8,128)S(1)} %get-tuple-element.17), channel_id=1, source_target_pairs={{0,1},{1,0},{2,3},{3,2},{4,5},{5,4},{6,7},{7,6},{8,9},{9,8},{10,11... | collective-permute-start | bytes 589832 | tf_op jit(solution)/shard_map/ppermute | solution.py:426

commit v2 on v1

--- a/solution.py
+++ b/solution.py
@@ -13,10 +13,12 @@
 JUMP = 0.75
 LANES = 128
 VMEM = pl.BlockSpec(memory_space=pltpu.VMEM)
+HBM = pl.BlockSpec(memory_space=pltpu.HBM)
 
 X_FIELDS, X_TRACES, X_SLOTS, X_BLOCKS = 0, 16, 28, 29
 Z_SLOTS, Z_BLOCKS = 32, 33
 W_CORNERS, W_BLOCKS = 32, 48
+X_WALL, Z_WALL, LOGK = 0, 4, 6
 
 
 def derivative_matrix():
@@ -146,8 +148,21 @@
     return [ref[z, f] for f in range(4)]
 
 
-def local_kernel(sizes, state, target, cell_of, cell_slot, z_wall, local, pay_a, pay_b, *z_pay):
+def local_kernel(sizes, *refs):
     nx, nz = sizes
+    count = 1 if nz == 2 else 2
+    sources, refs = refs[:7], refs[7:]
+    (state, small, local, pay_a, pay_b), refs = refs[:5], refs[5:]
+    z_pay, places, arrived = refs[:count], refs[count:-1], refs[-1]
+    target, cell_of, cell_slot, x_wall, z_wall, logk = places
+    copies = [
+        pltpu.make_async_copy(source, place, arrived.at[i])
+        for i, (source, place) in enumerate(zip(sources, (state,) + tuple(places)))
+    ]
+    for copy in copies:
+        copy.start()
+    for copy in copies:
+        copy.wait()
     x_place, z_place = lax.axis_index("gx"), lax.axis_index("gz")
     rows = Rows()
     derivative = Derivative(rows, derivative_matrix())
@@ -167,6 +182,11 @@
     even = x_place % 2 == 0
     pay_a[X_SLOTS] = slot_block
     pay_b[X_SLOTS] = slot_block
+    small[0] = slot_block
+    for side in range(2):
+        small[1, X_WALL + 2 * side : X_WALL + 2 * side + 2, :] = x_wall[side].astype(jnp.float32)
+    small[1, Z_WALL : Z_WALL + 2, :] = z_wall[...].astype(jnp.float32)
+    small[1, LOGK : LOGK + 1, 0 : logk.shape[1]] = logk[...]
     for z in range(2):
         u = load(state, z)
         other = load(state, 1 - z)
@@ -177,7 +197,7 @@
         across = z_terms(u, other, sign, weights[int(sign)], False)
         end = (z_place == 0) if z == 0 else (z_place == nz - 1)
         weight = weights[-int(sign)] * jnp.where(end, 1.0, 0.0)
-        flag = z_wall[z : z + 1, :].astype(jnp.float32)
+        flag = small[1, Z_WALL + z : Z_WALL + z + 1, :]
         wall = wall_terms(u, 2, -sign, weight, flag, False)
         result = [
             SCALE * v + j + a + w - target[z, f]
@@ -212,9 +232,7 @@
     return jnp.where(even, b, a) if side == 0 else jnp.where(even, a, b)
 
 
-def sums_kernel(
-    sizes, state, local, got_a, got_b, x_wall, logk, own_slots, *refs
-):
+def sums_kernel(sizes, length, state, small, local, got_a, got_b, *refs):
     nx, nz = sizes
     count = 1 if nz == 2 else 2
     z_got, (whole, send), z_pay = refs[:count], refs[count : count + 2], refs[count + 2 :]
@@ -242,7 +260,7 @@
             mine = [u[f][a] for f in range(4)]
             theirs = [x_side(side, even, got_a, got_b, 4 * f + 2 * z) for f in range(4)]
             corners[side, z] = theirs
-            flag = x_wall[side, z : z + 1, :].astype(jnp.float32)
+            flag = small[1, X_WALL + 2 * side + z : X_WALL + 2 * side + z + 1, :]
             inner = traces(mine, 0, -sign)
             image = (1.0 - 2.0 * flag) * (mine[0] + sign * mine[3])
             outer = [
@@ -256,9 +274,8 @@
         second = sum(u[k] * u[k] for k in range(3))
         first_sums.append(jnp.sum(first, axis=(0, 1, 2))[None])
         second_sums.append(jnp.sum(second, axis=(0, 1, 2))[None])
-    length = logk.shape[1]
     devices = send.shape[0]
-    slots = own_slots[X_SLOTS].astype(jnp.int32)
+    slots = small[0].astype(jnp.int32)
     total = jnp.zeros((devices, LANES), jnp.float32)
     place = lax.broadcasted_iota(jnp.int32, (LANES, LANES), 0)
     owner = lax.broadcasted_iota(jnp.int32, (devices, LANES), 0)
@@ -278,7 +295,8 @@
             )
             values = values - piece.astype(jnp.float32)
     send[...] = total
-    send[:, 0:length] = jnp.broadcast_to(logk[...], (devices, length))
+    logk = small[1, LOGK : LOGK + 1, 0:length]
+    send[:, 0:length] = jnp.broadcast_to(logk, (devices, length))
     for direction in range(count):
         layer = 1 - z_place if nz == 2 else 1 - direction
         for f in range(4):
@@ -317,24 +335,26 @@
     return lax.fori_loop(0, table_rows // chunk, step, result)
 
 
-def adjoint_kernel(sizes, state, whole, got_a, got_b, own_slots, x_wall, z_wall, received, logk, *refs):
+def adjoint_kernel(sizes, length, state, small, whole, got_a, got_b, received, *refs):
     nx, nz = sizes
     count = 1 if nz == 2 else 2
-    z_got, w_got, (adjoint, gradient) = refs[:count], refs[count : 2 * count], refs[2 * count :]
+    z_got, w_got, refs = refs[:count], refs[count : 2 * count], refs[2 * count :]
+    adjoint_out, gradient_out, adjoint, gradient, done = refs
     z_from, w_from = [z_got[0], z_got[-1]], [w_got[0], w_got[-1]]
     x_place, z_place = lax.axis_index("gx"), lax.axis_index("gz")
     even = x_place % 2 == 0
     rows = Rows()
     weights = z_weights(rows)
     derivative = Derivative(rows, derivative_matrix().T)
-    length = logk.shape[1]
-    held = jnp.exp(-logk[...])
+    held = jnp.exp(-small[1, LOGK : LOGK + 1, 0:length])
     summed = jnp.sum(received[...], axis=0, keepdims=True)
     first, second = summed[:, length : 2 * length], summed[:, 2 * length : 3 * length]
     gradient[...] = -(SCALE / 64.0) * held * (first + SCALE * held * second)
+    copies = [pltpu.make_async_copy(gradient, gradient_out, done.at[2])]
+    copies[0].start()
     slot_a, slot_b = got_a[X_SLOTS], got_b[X_SLOTS]
     row = lax.broadcasted_iota(jnp.int32, (8, LANES), 0)
-    slots = own_slots[X_SLOTS]
+    slots = small[0]
     slots = jnp.where(row // 2 == 1, pltpu.roll(jnp.where(even, slot_b, slot_a), 2, 0), slots)
     slots = jnp.where(row // 2 == 2, pltpu.roll(jnp.where(even, slot_a, slot_b), 4, 0), slots)
     slots = jnp.where(row == 6, z_from[0][Z_SLOTS], slots)
@@ -359,7 +379,7 @@
         for k in range(3):
             field = z_from[z][pl.ds(8 * k, 8)].reshape(4, 2, 8, LANES)
             theirs[k] = theirs[k] + scaled * field
-        flag = z_wall[z : z + 1, :].astype(jnp.float32)
+        flag = small[1, Z_WALL + z : Z_WALL + z + 1, :]
         inner = traces(w, 2, -float(sign))
         outer = [
             pltpu.roll(t, 3 if sign > 0 else 5, 2) for t in traces(theirs, 2, float(sign))
@@ -397,23 +417,28 @@
             normal = normal + scaled * u_out[0]
             tangential = [v + scaled * u_out[1 + j] for j, v in enumerate(tangential)]
             inner = traces([w[f][a] for f in range(4)], 0, -s)
-            flag = x_wall[side, z : z + 1, :].astype(jnp.float32)
+            flag = small[1, X_WALL + 2 * side + z : X_WALL + 2 * side + z + 1, :]
             image = inner[:2] + [(1.0 - 2.0 * flag) * inner[2]]
             last = (x_place == nx - 1) if side else (x_place == 0)
             outer = [jnp.where(last, i, o) for i, o in zip(image, tangential + [normal])]
             terms = face_terms(inner, outer, 0, s, JUMP, True)
             for f in range(4):
                 adjoint[z, f, a] += terms[f]
-
-
-def call(kernel, shapes, operands, flops):
+        copies.append(pltpu.make_async_copy(adjoint.at[z], adjoint_out.at[z], done.at[z]))
+        copies[-1].start()
+    for copy in copies:
+        copy.wait()
+
+
+def call(kernel, operands, in_spec, shapes, out_spec, scratch, room):
     return pl.pallas_call(
         kernel,
         out_shape=[jax.ShapeDtypeStruct(shape, jnp.float32) for shape in shapes],
-        in_specs=[VMEM] * len(operands),
-        out_specs=[VMEM] * len(shapes),
-        compiler_params=pltpu.CompilerParams(vmem_limit_bytes=32 * 1024 * 1024),
-        cost_estimate=pl.CostEstimate(flops=flops, bytes_accessed=800000, transcendentals=0),
+        in_specs=[in_spec] * len(operands),
+        out_specs=[out_spec] * len(shapes),
+        scratch_shapes=scratch,
+        compiler_params=pltpu.CompilerParams(vmem_limit_bytes=room * 1024),
+        cost_estimate=pl.CostEstimate(flops=2000000, bytes_accessed=800000, transcendentals=0),
     )(*operands)
 
 
@@ -432,40 +457,55 @@
 def shards(nx, nz, state, target, coarse_logk, cell_slot, cell_of, wall_flags_xaxis, z_wall):
     sizes = (nx, nz)
     shape = (2, 4, 4, 2, 8, LANES)
-    state6 = state.reshape(shape)
-    target6 = target.reshape(shape)
-    logk = coarse_logk.reshape(1, -1)
-    slots2 = cell_slot.reshape(-1, LANES)
-    cells2 = cell_of.reshape(2, LANES)
-    z_flags = z_wall.reshape(2, LANES)
+    length = coarse_logk.shape[0]
+    inputs = [
+        state.reshape(shape),
+        target.reshape(shape),
+        cell_of.reshape(2, LANES),
+        cell_slot.reshape(-1, LANES),
+        wall_flags_xaxis,
+        z_wall.reshape(2, LANES),
+        coarse_logk.reshape(1, -1),
+    ]
     count = 1 if nz == 2 else 2
     x_shape, z_shape, w_shape = ((n, 8, LANES) for n in (X_BLOCKS, Z_BLOCKS, W_BLOCKS))
-    local, pay_a, pay_b, *z_pay = call(
+    held, small, local, pay_a, pay_b, *z_pay = call(
         functools.partial(local_kernel, sizes),
-        [shape, x_shape, x_shape] + [z_shape] * count,
-        [state6, target6, cells2, slots2, z_flags],
-        2000000,
+        inputs,
+        HBM,
+        [shape, (2, 8, LANES), shape, x_shape, x_shape] + [z_shape] * count,
+        VMEM,
+        [pltpu.VMEM(i.shape, i.dtype) for i in inputs[1:]] + [pltpu.SemaphoreType.DMA((7,))],
+        54200,
     )
     pairs_b = both_ways([(i, i + 1) for i in range(1, nx - 1, 2)])
     pairs_a = both_ways([(i, i + 1) for i in range(0, nx - 1, 2)])
+    got_a = lax.ppermute(pay_a, "gx", pairs_a)
     got_b = lax.ppermute(pay_b, "gx", pairs_b)
-    got_a = lax.ppermute(pay_a, "gx", pairs_a)
     z_got = along_z(z_pay, nz)
     whole, send, *w_pay = call(
-        functools.partial(sums_kernel, sizes),
+        functools.partial(sums_kernel, sizes, length),
+        [held, small, local, got_a, got_b] + z_got,
+        VMEM,
         [shape, (nx * nz, LANES)] + [w_shape] * count,
-        [state6, local, got_a, got_b, wall_flags_xaxis, logk, pay_a] + z_got,
-        2000000,
+        VMEM,
+        [],
+        16 * 1024,
     )
     w_got = along_z(w_pay, nz)
     received = lax.all_to_all(send, ("gx", "gz"), 0, 0, tiled=True)
     adjoint, gradient = call(
-        functools.partial(adjoint_kernel, sizes),
-        [shape, logk.shape],
-        [state6, whole, got_a, got_b, pay_a, wall_flags_xaxis, z_flags, received, logk]
-        + z_got
-        + w_got,
-        2000000,
+        functools.partial(adjoint_kernel, sizes, length),
+        [held, small, whole, got_a, got_b, received] + z_got + w_got,
+        VMEM,
+        [shape, (1, length)],
+        HBM,
+        [
+            pltpu.VMEM(shape, jnp.float32),
+            pltpu.VMEM((1, length), jnp.float32),
+            pltpu.SemaphoreType.DMA((3,)),
+        ],
+        16 * 1024,
     )
     return adjoint.reshape(state.shape), gradient.reshape(-1)
 

time: 30.5 us -> 27.7 us (0.908)
  blocking collectives: 11.9 us -> 16.3 us
  waiting for transfers between devices: 6.05 us -> 3.17 us
  starting transfers between devices: 6.48 us -> 3.74 us
  local copies, waits for them, and re-layouts: 3.24 us -> 0.69 us
  Pallas kernels: 1.87 us -> 2.94 us
    all_to_all x1, blocking collectives: 11.9 us -> 16.3 us  [shards(): received = lax.all_to_all(send, ('gx', 'gz'), 0, 0, tiled=True)]
    ppermute x1, waiting for transfers between devices: 6.04 us -> 3.16 us  [shards(): got_a = lax.ppermute(pay_a, 'gx', pairs_a)]
    ppermute x1, starting transfers between devices: 5.31 us -> 2.56 us  [shards(): got_a = lax.ppermute(pay_a, 'gx', pairs_a)]
    unnamed x14 -> x10, local copies, waits for them, and re-layouts: 3.24 us -> 0.69 us
    pallas_call x3, Pallas kernels: 1.87 us -> 2.94 us  [call(): pl.pallas_call(kernel, out_shape=[jax.ShapeDtypeStruct(shape, jnp.float32...]
where the time goes in v2:
time: 27.7 us; the launch traced here: 27.5 us
  blocking collectives  16.3 us (59%)
  starting transfers between devices  3.74 us (14%)
  waiting for transfers between devices  3.17 us (11%)
  Pallas kernels  2.94 us (11%)
  between operations  0.71 us (3%)
  local copies, waits for them, and re-layouts  0.69 us (2%)
    all_to_all x1, blocking collectives, shards(): received = lax.all_to_all(send, ('gx', 'gz'), 0, 0, tiled=True)  16.3 us
    ppermute x1, waiting for transfers between devices, shards(): got_a = lax.ppermute(pay_a, 'gx', pairs_a)  3.16 us
    pallas_call x3, Pallas kernels, call(): pl.pallas_call(kernel, out_shape=[jax.ShapeDtypeStruct(shape, jnp.float32...  2.94 us
    ppermute x1, starting transfers between devices, shards(): got_a = lax.ppermute(pay_a, 'gx', pairs_a)  2.56 us
    unnamed x10, local copies, waits for them, and re-layouts  0.69 us
    ppermute x1, starting transfers between devices, shards(): got_b = lax.ppermute(pay_b, 'gx', pairs_b)  0.66 us
  transfers between devices with their start and end apart: 4, of which 1 were waited for; matrix products, arithmetic and copies ran while one was open for 0% of the time, Pallas kernels for 0%

profile of v2, /device:TPU:0, one launch (start us, length us, event | category | flops | bytes accessed | tf_op | source)
XLA Modules:
  0.0 27.5 jit_solution(6351706779166821156)
XLA Ops:
  0.6 0.0 copy-start.3
  0.6 0.0 copy-start
  0.7 0.0 copy-start.1
  0.7 0.0 copy-start.2
  0.7 0.0 copy-start.4
  0.7 0.6 %copy-done.3 = s32[2,1,128]{2,1,0:T(1,128)S(1)} copy-done((s32[2,1,128]{2,1,0:T(1,128)S(1)}, s32[2,1,128]{2,1,0:T(1,128)}, u32[]{:S(2)}) %copy-start.3) | copy-done | bytes 1048
  1.3 0.0 copy-done
  1.3 0.0 copy-done.1
  1.3 0.0 copy-done.2
  1.4 0.0 copy-done.4
  1.4 1.4 %shard_map.86 = (f32[2,4,4,2,8,128]{5,4,3,2,1,0:T(8,128)S(1)}, f32[2,8,128]{2,1,0:T(8,128)S(1)}, f32[2,4,4,2,8,128]{5,4,3,2,1,0:T(8,128)S(1)}, f32[29,8,128]{2,1...) custom-call(f32[2,4,4,2,8,128]{5,4,3,2,1,0:T(8,128)} %bitcast.18, ...), custom_call_target="tpu_custom_call" | custom-call | flops 2000000 | bytes 800000 | tf_op jit(solution)/shard_map/pallas_call | solution.py:434
  2.8 0.5 %collective-permute-start.2 = (f32[33,8,128]{2,1,0:T(8,128)S(1)}, f32[33,8,128]{2,1,0:T(8,128)S(1)}, u32[]{:S(2)}, u32[]{:S(2)}) collective-permute-start(f32[33,8,128]{2,1,0:T(8,128)S(1)} %get-tuple-element.18), channel_id=1, source_target_pairs={{0,1},{1,0},{2,3},{3,2},{4,5},{5,4},{6,7},{7,6},{8,9},{9,8},{10,11... | collective-permute-start | bytes 405512 | tf_op jit(solution)/shard_map/ppermute | solution.py:451
  3.3 2.6 %collective-permute-start = (f32[29,8,128]{2,1,0:T(8,128)S(1)}, f32[29,8,128]{2,1,0:T(8,128)S(1)}, u32[]{:S(2)}, u32[]{:S(2)}) collective-permute-start(f32[29,8,128]{2,1,0:T(8,128)S(1)} %get-tuple-element.16), channel_id=1, source_target_pairs={{0,2},{4,6},{8,10},{12,14},{16,18},{20,22},{24,26},{28,30},{2,0},{... | collective-permute-start | bytes 356360 | tf_op jit(solution)/shard_map/ppermute | solution.py:483
  5.9 0.7 %collective-permute-start.1 = (f32[29,8,128]{2,1,0:T(8,128)S(1)}, f32[29,8,128]{2,1,0:T(8,128)S(1)}, u32[]{:S(2)}, u32[]{:S(2)}) collective-permute-start(f32[29,8,128]{2,1,0:T(8,128)S(1)} %get-tuple-element.17), channel_id=1, source_target_pairs={{2,4},{6,8},{10,12},{14,16},{18,20},{22,24},{26,28},{4,2},{8,6},{1... | collective-permute-start | bytes 356360 | tf_op jit(solution)/shard_map/ppermute | solution.py:484
  6.5 3.2 %collective-permute-done.got_a = f32[29,8,128]{2,1,0:T(8,128)S(1)} collective-permute-done((f32[29,8,128]{2,1,0:T(8,128)S(1)}, f32[29,8,128]{2,1,0:T(8,128)S(1)}, u32[]{:S(2)}, u32[]{:S(2)}) %collective-permute-start) | collective-permute-done | bytes 118816 | tf_op jit(solution)/shard_map/ppermute | solution.py:483
  9.7 0.0 collective-permute-done.1.got_b
  9.7 0.0 collective-permute-done.2.refs_0_
  9.7 0.3 %shard_map.87 = (f32[2,4,4,2,8,128]{5,4,3,2,1,0:T(8,128)S(1)}, f32[32,128]{1,0:T(8,128)S(1)}, f32[48,8,128]{2,1,0:T(8,128)S(1)}) custom-call(f32[2,4,4,2,8,128]{5,4,3,2,1,0:T(8,128)S(1)} %get-tuple-element.13.state, f32[2,8,128]{2,1,0:T(8,128)S(1)} %get-tuple-element.14.small, f32[2,4,4,2,8,128]{5,4,3,2,1,0:T(8,128)S(1)} %get-tuple-element.15.local, ...), custom_call_target="tpu_custom_call" | custom-call | flops 2000000 | bytes 800000 | tf_op jit(solution)/shard_map/pallas_call | solution.py:434
  10.0 0.0 collective-permute-start.3
  10.0 16.3 %all_to_all.11 = f32[32,1,128]{2,1,0:T(1,128)S(1)} all-to-all(f32[32,1,128]{2,1,0:T(1,128)S(1)} %bitcast.13), channel_id=1, replica_groups=mesh['gx'=16,'gz'=2] {'gx','gz'}, dimensions={0} | all-to-all | bytes 32768 | tf_op jit(solution)/shard_map/all_to_all | solution.py:496
  26.3 0.0 collective-permute-done.3.refs_1_
  26.3 1.2 %shard_map.88 = (f32[2,4,4,2,8,128]{5,4,3,2,1,0:T(8,128)}, f32[1,32]{1,0:T(1,128)}) custom-call(f32[2,4,4,2,8,128]{5,4,3,2,1,0:T(8,128)S(1)} %get-tuple-element.13.state, f32[2,8,128]{2,1,0:T(8,128)S(1)} %get-tuple-element.14.small, f32[2,4,4,2,8,128]{5,4,3,2,1,0:T(8,128)S(1)} %get-tuple-element.19.whole, f32[29,8,128]{2,1,0:T(8,128)S(1)} %collective-permute-done.got_a, ...), custom_call_target="tpu_custom_call" | custom-call | flops 2000000 | bytes 800000 | tf_op jit(solution)/shard_map/pallas_call | solution.py:434
Async XLA Ops:
  0.6 0.7 %copy-start.3 = (s32[2,1,128]{2,1,0:T(1,128)S(1)}, s32[2,1,128]{2,1,0:T(1,128)}, u32[]{:S(2)}) copy-start(s32[2,1,128]{2,1,0:T(1,128)} %param.13) | copy-start | bytes 3076
  0.6 0.7 %copy-start = (s32[1024]{0:T(1024)S(1)}, s32[1024]{0:T(1024)}, u32[]{:S(2)}) copy-start(s32[1024]{0:T(1024)} %param.10) | copy-start | bytes 12292
  0.7 0.7 %copy-start.1 = (s32[2,2,128]{2,1,0:T(2,128)S(1)}, s32[2,2,128]{2,1,0:T(2,128)}, u32[]{:S(2)}) copy-start(s32[2,2,128]{2,1,0:T(2,128)} %refs_4_.1) | copy-start | bytes 6148
  0.7 0.7 %copy-start.2 = (s32[1,2,128]{2,1,0:T(2,128)S(1)}, s32[1,2,128]{2,1,0:T(2,128)}, u32[]{:S(2)}) copy-start(s32[1,2,128]{2,1,0:T(2,128)} %param.11) | copy-start | bytes 3076
  0.7 0.7 %copy-start.4 = (f32[32]{0:T(128)S(1)}, f32[32]{0:T(128)}, u32[]{:S(2)}) copy-start(f32[32]{0:T(128)} %param.9) | copy-start | bytes 388
  2.8 6.9 %collective-permute-start.2 = (f32[33,8,128]{2,1,0:T(8,128)S(1)}, f32[33,8,128]{2,1,0:T(8,128)S(1)}, u32[]{:S(2)}, u32[]{:S(2)}) collective-permute-start(f32[33,8,128]{2,1,0:T(8,128)S(1)} %get-tuple-element.18), channel_id=1, source_target_pairs={{0,1},{1,0},{2,3},{3,2},{4,5},{5,4},{6,7},{7,6},{8,9},{9,8},{10,11... | collective-permute-start | bytes 405512 | tf_op jit(solution)/shard_map/ppermute | solution.py:451
  3.3 6.4 %collective-permute-start = (f32[29,8,128]{2,1,0:T(8,128)S(1)}, f32[29,8,128]{2,1,0:T(8,128)S(1)}, u32[]{:S(2)}, u32[]{:S(2)}) collective-permute-start(f32[29,8,128]{2,1,0:T(8,128)S(1)} %get-tuple-element.16), channel_id=1, source_target_pairs={{0,2},{4,6},{8,10},{12,14},{16,18},{20,22},{24,26},{28,30},{2,0},{... | collective-permute-start | bytes 356360 | tf_op jit(solution)/shard_map/ppermute | solution.py:483
  5.9 3.8 %collective-permute-start.1 = (f32[29,8,128]{2,1,0:T(8,128)S(1)}, f32[29,8,128]{2,1,0:T(8,128)S(1)}, u32[]{:S(2)}, u32[]{:S(2)}) collective-permute-start(f32[29,8,128]{2,1,0:T(8,128)S(1)} %get-tuple-element.17), channel_id=1, source_target_pairs={{2,4},{6,8},{10,12},{14,16},{18,20},{22,24},{26,28},{4,2},{8,6},{1... | collective-permute-start | bytes 356360 | tf_op jit(solution)/shard_map/ppermute | solution.py:484
  10.0 16.3 %collective-permute-start.3 = (f32[48,8,128]{2,1,0:T(8,128)S(1)}, f32[48,8,128]{2,1,0:T(8,128)S(1)}, u32[]{:S(2)}, u32[]{:S(2)}) collective-permute-start(f32[48,8,128]{2,1,0:T(8,128)S(1)} %get-tuple-element.21), channel_id=1, source_target_pairs={{0,1},{1,0},{2,3},{3,2},{4,5},{5,4},{6,7},{7,6},{8,9},{9,8},{10,11... | collective-permute-start | bytes 589832 | tf_op jit(solution)/shard_map/ppermute | solution.py:451

commit v3 on v2

--- a/solution.py
+++ b/solution.py
@@ -16,8 +16,8 @@
 HBM = pl.BlockSpec(memory_space=pltpu.HBM)
 
 X_FIELDS, X_TRACES, X_SLOTS, X_BLOCKS = 0, 16, 28, 29
-Z_SLOTS, Z_BLOCKS = 32, 33
-W_CORNERS, W_BLOCKS = 32, 48
+Z_SLOTS, Z_BLOCKS = 8, 9
+W_CORNERS, W_BLOCKS = 8, 12
 X_WALL, Z_WALL, LOGK = 0, 4, 6
 
 
@@ -76,11 +76,12 @@
             for delta in range(-3, 4)
         }
 
+    def across(self, a, u):
+        return sum(float(self.matrix[a, j]) * u[j : j + 1] for j in range(4))
+
     def along(self, axis, u):
         if axis == 0:
-            return jnp.stack(
-                [sum(float(self.matrix[a, j]) * u[j] for j in range(4)) for a in range(4)]
-            )
+            return jnp.concatenate([self.across(a, u) for a in range(4)])
         if axis == 1:
             swapped = pltpu.roll(u, 4, 2)
             return jnp.stack(
@@ -133,6 +134,27 @@
     return face_terms(traces(inner, 2, -sign), outer, 2, sign, weight, adjoint)
 
 
+def packed_face(rows, fields, sign):
+    c = 3 if sign > 0 else 0
+    axis = fields[0].ndim - 2
+    result = None
+    for f, field in enumerate(fields):
+        moved = field if f == c else pltpu.roll(field, (f - c) % 8, axis)
+        result = moved if result is None else jnp.where(rows.c == f, moved, result)
+    return result
+
+
+def unpacked_face(packed, sign):
+    c = 3 if sign > 0 else 0
+    axis = packed.ndim - 2
+    return [packed if f == c else pltpu.roll(packed, (c - f) % 8, axis) for f in range(4)]
+
+
+def met_terms(inner, packed, sign, weight):
+    outer = traces(unpacked_face(packed, sign), 2, -sign)
+    return face_terms(traces(inner, 2, -sign), outer, 2, sign, weight, False)
+
+
 def wall_terms(fields, axis, sign, weight, flag, adjoint):
     inner = traces(fields, axis, -sign)
     image = inner[2] if adjoint else fields[axis] + sign * fields[3]
@@ -148,24 +170,58 @@
     return [ref[z, f] for f in range(4)]
 
 
-def local_kernel(sizes, *refs):
-    nx, nz = sizes
-    count = 1 if nz == 2 else 2
-    sources, refs = refs[:7], refs[7:]
-    (state, small, local, pay_a, pay_b), refs = refs[:5], refs[5:]
-    z_pay, places, arrived = refs[:count], refs[count:-1], refs[-1]
-    target, cell_of, cell_slot, x_wall, z_wall, logk = places
-    copies = [
-        pltpu.make_async_copy(source, place, arrived.at[i])
-        for i, (source, place) in enumerate(zip(sources, (state,) + tuple(places)))
-    ]
+def faces_kernel(state_in, target_in, state, pay_a, pay_b, target, arrived):
+    copies = [pltpu.make_async_copy(state_in, state, arrived.at[0])]
+    for side in range(2):
+        copies.append(
+            pltpu.make_async_copy(
+                target_in.at[:, :, 3 * side], target.at[side], arrived.at[1 + side]
+            )
+        )
     for copy in copies:
         copy.start()
+    even = lax.axis_index("gx") % 2 == 0
+    rows = Rows()
+    derivative = Derivative(rows, derivative_matrix())
+    weights = z_weights(rows)
     for copy in copies:
         copy.wait()
+    for z in range(2):
+        sign = 1 if z == 0 else -1
+        values = []
+        for side in range(2):
+            a = 3 * side
+            u = [state[z, f, a : a + 1] for f in range(4)]
+            other = [state[1 - z, f, a : a + 1] for f in range(4)]
+            grads = [derivative.across(a, state[z, 3])]
+            grads += [derivative.along(k, u[3]) for k in (1, 2)]
+            divergence = derivative.across(a, state[z, 0])
+            divergence += derivative.along(1, u[1]) + derivative.along(2, u[2])
+            jumps = y_terms(u, rows, False)
+            terms = z_terms(u, other, float(sign), weights[sign], False)
+            result = [
+                (SCALE * v + j + t)[0] - target[side, z, f]
+                for f, (v, j, t) in enumerate(zip(grads + [divergence], jumps, terms))
+            ]
+            normal = result[0] - result[3] if side else result[0] + result[3]
+            values.append([v[0] for v in u] + [normal, result[1], result[2]])
+        low, high = values
+        for j in range(7):
+            pay_a[pl.ds(4 * j + 2 * z, 2)] = jnp.where(even, high[j], low[j])
+            pay_b[pl.ds(4 * j + 2 * z, 2)] = jnp.where(even, low[j], high[j])
+
+
+def wall_rows(sizes, rows, weights, z, flags):
+    z_place = lax.axis_index("gz")
+    end = (z_place == 0) if z == 0 else (z_place == sizes[1] - 1)
+    weight = weights[-1 if z == 0 else 1] * jnp.where(end, 1.0, 0.0)
+    return weight, flags[z : z + 1, :].astype(jnp.float32)
+
+
+def edges_kernel(sizes, first_a, first_b, cell_of, cell_slot, z_wall, pay_a, pay_b, positions):
+    nx, nz = sizes
     x_place, z_place = lax.axis_index("gx"), lax.axis_index("gz")
     rows = Rows()
-    derivative = Derivative(rows, derivative_matrix())
     weights = z_weights(rows)
     cell_rows = cell_slot.shape[0]
     slots = []
@@ -178,11 +234,27 @@
             slot = jnp.where(row_of == row, cell_slot[pl.ds(row, 1), :], slot)
         slots.append(slot.astype(jnp.float32))
     row = lax.broadcasted_iota(jnp.int32, (8, LANES), 0)
-    slot_block = jnp.where(row == 0, slots[0], jnp.where(row == 1, slots[1], 0.0))
-    even = x_place % 2 == 0
-    pay_a[X_SLOTS] = slot_block
-    pay_b[X_SLOTS] = slot_block
-    small[0] = slot_block
+    block = jnp.where(row == 0, slots[0], jnp.where(row == 1, slots[1], 0.0))
+    positions[...] = block
+    flip = jnp.where(x_place % 2 == 0, -1.0, 1.0)
+    for first, pay, factor in ((first_a, pay_a, flip), (first_b, pay_b, -flip)):
+        pay[X_SLOTS] = block
+        for z in range(2):
+            weight, flag = wall_rows(sizes, rows, weights, z, z_wall)
+            fields = [first[pl.ds(4 * f + 2 * z, 2)] for f in range(4)]
+            terms = wall_terms(fields, 2, -1.0 if z == 0 else 1.0, weight, flag, False)
+            normal, tangential = X_TRACES + 2 * z, X_TRACES + 8 + 2 * z
+            pay[pl.ds(normal, 2)] = first[pl.ds(normal, 2)] + factor * terms[3]
+            pay[pl.ds(tangential, 2)] = first[pl.ds(tangential, 2)] + terms[2]
+
+
+def local_kernel(sizes, state, positions, target, x_wall, z_wall, logk, small, local, *z_pay):
+    nx, nz = sizes
+    z_place = lax.axis_index("gz")
+    rows = Rows()
+    derivative = Derivative(rows, derivative_matrix())
+    weights = z_weights(rows)
+    small[0] = positions[...]
     for side in range(2):
         small[1, X_WALL + 2 * side : X_WALL + 2 * side + 2, :] = x_wall[side].astype(jnp.float32)
     small[1, Z_WALL : Z_WALL + 2, :] = z_wall[...].astype(jnp.float32)
@@ -193,38 +265,18 @@
         grads = [derivative.along(k, u[3]) for k in range(3)]
         divergence = sum(derivative.along(k, u[k]) for k in range(3))
         jumps = y_terms(u, rows, False)
-        sign = 1.0 if z == 0 else -1.0
-        across = z_terms(u, other, sign, weights[int(sign)], False)
-        end = (z_place == 0) if z == 0 else (z_place == nz - 1)
-        weight = weights[-int(sign)] * jnp.where(end, 1.0, 0.0)
-        flag = small[1, Z_WALL + z : Z_WALL + z + 1, :]
-        wall = wall_terms(u, 2, -sign, weight, flag, False)
-        result = [
-            SCALE * v + j + a + w - target[z, f]
-            for f, (v, j, a, w) in enumerate(zip(grads + [divergence], jumps, across, wall))
-        ]
-        for f in range(4):
-            local[z, f] = result[f]
-        low = [u[f][0] for f in range(4)] + traces([r[0] for r in result], 0, 1.0)[2:] + [
-            result[f][0] for f in (1, 2)
-        ]
-        high = [u[f][3] for f in range(4)] + traces([r[3] for r in result], 0, -1.0)[2:] + [
-            result[f][3] for f in (1, 2)
-        ]
-        for j in range(7):
-            pay_a[pl.ds(4 * j + 2 * z, 2)] = jnp.where(even, high[j], low[j])
-            pay_b[pl.ds(4 * j + 2 * z, 2)] = jnp.where(even, low[j], high[j])
-    if nz == 2:
-        layer = 1 - z_place
-        for f in range(4):
-            z_pay[0][pl.ds(8 * f, 8)] = state[layer, f].reshape(8, 8, LANES)
-        z_pay[0][Z_SLOTS] = jnp.broadcast_to(jnp.where(layer == 0, slots[0], slots[1]), (8, LANES))
-    else:
-        for direction in range(2):
-            layer = 1 - direction
-            for f in range(4):
-                z_pay[direction][pl.ds(8 * f, 8)] = state[layer, f].reshape(8, 8, LANES)
-            z_pay[direction][Z_SLOTS] = jnp.broadcast_to(slots[layer], (8, LANES))
+        sign = 1 if z == 0 else -1
+        across = z_terms(u, other, float(sign), weights[sign], False)
+        weight, flag = wall_rows(sizes, rows, weights, z, z_wall)
+        wall = wall_terms(u, 2, -float(sign), weight, flag, False)
+        for f, (v, j, a, w) in enumerate(zip(grads + [divergence], jumps, across, wall)):
+            local[z, f] = SCALE * v + j + a + w - target[z, f]
+    faces = [packed_face(rows, load(state, z), 2 * z - 1) for z in range(2)]
+    for direction in range(len(z_pay)):
+        upper = z_place == 0 if nz == 2 else direction == 0
+        z_pay[direction][0:8] = jnp.where(upper, faces[1], faces[0]).reshape(8, 8, LANES)
+        slot = jnp.where(upper, positions[1:2, :], positions[0:1, :])
+        z_pay[direction][Z_SLOTS] = jnp.broadcast_to(slot, (8, LANES))
 
 
 def x_side(side, even, got_a, got_b, block):
@@ -249,8 +301,8 @@
             whole[z, f] = local[z, f]
         sign = -1 if z == 0 else 1
         inside = (z_place > 0) if z == 0 else (z_place < nz - 1)
-        outer = [z_from[z][pl.ds(8 * f, 8)].reshape(4, 2, 8, LANES) for f in range(4)]
-        terms = z_terms(u, outer, float(sign), weights[sign] * jnp.where(inside, 1.0, 0.0), False)
+        packed = z_from[z][0:8].reshape(4, 2, 8, LANES)
+        terms = met_terms(u, packed, float(sign), weights[sign] * jnp.where(inside, 1.0, 0.0))
         for f in range(4):
             whole[z, f] += terms[f]
         for side in range(2):
@@ -297,16 +349,14 @@
     send[...] = total
     logk = small[1, LOGK : LOGK + 1, 0:length]
     send[:, 0:length] = jnp.broadcast_to(logk, (devices, length))
+    faces = [packed_face(rows, load(whole, z), 2 * z - 1) for z in range(2)]
+    edges = [[packed_face(rows, corners[side, z], 2 * z - 1) for z in range(2)] for side in range(2)]
     for direction in range(count):
-        layer = 1 - z_place if nz == 2 else 1 - direction
-        for f in range(4):
-            z_pay[direction][pl.ds(8 * f, 8)] = whole[layer, f].reshape(8, 8, LANES)
-            for side in range(2):
-                if nz == 2:
-                    value = jnp.where(layer == 0, corners[side, 0][f], corners[side, 1][f])
-                else:
-                    value = corners[side, layer][f]
-                z_pay[direction][pl.ds(W_CORNERS + 8 * side + 2 * f, 2)] = value
+        upper = z_place == 0 if nz == 2 else direction == 0
+        z_pay[direction][0:8] = jnp.where(upper, faces[1], faces[0]).reshape(8, 8, LANES)
+        for side in range(2):
+            block = W_CORNERS + 2 * side
+            z_pay[direction][block : block + 2] = jnp.where(upper, edges[side][1], edges[side][0])
 
 
 def look_up(table, length, slots):
@@ -375,15 +425,12 @@
         sign = -sign
         end = (z_place == 0) if z == 0 else (z_place == nz - 1)
         scaled = SCALE * resistance[6 + z]
-        theirs = [w_from[z][pl.ds(8 * f, 8)].reshape(4, 2, 8, LANES) for f in range(4)]
-        for k in range(3):
-            field = z_from[z][pl.ds(8 * k, 8)].reshape(4, 2, 8, LANES)
-            theirs[k] = theirs[k] + scaled * field
+        theirs = unpacked_face(w_from[z][0:8].reshape(4, 2, 8, LANES), sign)
+        fields = unpacked_face(z_from[z][0:8].reshape(4, 2, 8, LANES), sign)
+        theirs = [theirs[k] + scaled * fields[k] for k in range(3)] + [theirs[3]]
         flag = small[1, Z_WALL + z : Z_WALL + z + 1, :]
         inner = traces(w, 2, -float(sign))
-        outer = [
-            pltpu.roll(t, 3 if sign > 0 else 5, 2) for t in traces(theirs, 2, float(sign))
-        ]
+        outer = traces(theirs, 2, float(sign))
         image = inner[:2] + [(1.0 - 2.0 * flag) * inner[2]]
         outer = [jnp.where(end, i, o) for i, o in zip(image, outer)]
         beyond = face_terms(inner, outer, 2, float(sign), weights[sign], True)
@@ -407,10 +454,8 @@
             tangential = [t - JUMP * (m - o) for t, m, o in zip(tangential, mine[:2], there[:2])]
             t = float(sign)
             weight = weights[sign] * jnp.where(end, 0.0, 1.0)
-            corner = [
-                w_from[z][pl.ds(W_CORNERS + 8 * side + 2 * f, 2)] for f in range(4)
-            ]
-            edge = z_terms(u_out, corner, t, weight, False)
+            block = W_CORNERS + 2 * side
+            edge = met_terms(u_out, w_from[z][block : block + 2], t, weight)
             normal = normal + edge[0] + s * edge[3]
             tangential = [tangential[0] + edge[1], tangential[1] + edge[2]]
             scaled = SCALE * resistance[2 + 2 * side + z]
@@ -430,13 +475,14 @@
         copy.wait()
 
 
-def call(kernel, operands, in_spec, shapes, out_spec, scratch, room):
+def call(kernel, operands, in_spec, shapes, out_spec, scratch, room, aliases={}):
     return pl.pallas_call(
         kernel,
         out_shape=[jax.ShapeDtypeStruct(shape, jnp.float32) for shape in shapes],
         in_specs=[in_spec] * len(operands),
         out_specs=[out_spec] * len(shapes),
         scratch_shapes=scratch,
+        input_output_aliases=aliases,
         compiler_params=pltpu.CompilerParams(vmem_limit_bytes=room * 1024),
         cost_estimate=pl.CostEstimate(flops=2000000, bytes_accessed=800000, transcendentals=0),
     )(*operands)
@@ -458,30 +504,42 @@
     sizes = (nx, nz)
     shape = (2, 4, 4, 2, 8, LANES)
     length = coarse_logk.shape[0]
-    inputs = [
-        state.reshape(shape),
-        target.reshape(shape),
-        cell_of.reshape(2, LANES),
-        cell_slot.reshape(-1, LANES),
-        wall_flags_xaxis,
-        z_wall.reshape(2, LANES),
-        coarse_logk.reshape(1, -1),
-    ]
+    state6, target6 = state.reshape(shape), target.reshape(shape)
+    z_flags = z_wall.reshape(2, LANES)
     count = 1 if nz == 2 else 2
     x_shape, z_shape, w_shape = ((n, 8, LANES) for n in (X_BLOCKS, Z_BLOCKS, W_BLOCKS))
-    held, small, local, pay_a, pay_b, *z_pay = call(
-        functools.partial(local_kernel, sizes),
-        inputs,
+    held, first_a, first_b = call(
+        faces_kernel,
+        [state6, target6],
         HBM,
-        [shape, (2, 8, LANES), shape, x_shape, x_shape] + [z_shape] * count,
-        VMEM,
-        [pltpu.VMEM(i.shape, i.dtype) for i in inputs[1:]] + [pltpu.SemaphoreType.DMA((7,))],
-        54200,
+        [shape, x_shape, x_shape],
+        VMEM,
+        [pltpu.VMEM((2, 2, 4, 2, 8, LANES), jnp.float32), pltpu.SemaphoreType.DMA((3,))],
+        54600,
+    )
+    pay_a, pay_b, positions = call(
+        functools.partial(edges_kernel, sizes),
+        [first_a, first_b, cell_of.reshape(2, LANES), cell_slot.reshape(-1, LANES), z_flags],
+        VMEM,
+        [x_shape, x_shape, (8, LANES)],
+        VMEM,
+        [],
+        16 * 1024,
+        {0: 0, 1: 1},
     )
     pairs_b = both_ways([(i, i + 1) for i in range(1, nx - 1, 2)])
     pairs_a = both_ways([(i, i + 1) for i in range(0, nx - 1, 2)])
     got_a = lax.ppermute(pay_a, "gx", pairs_a)
     got_b = lax.ppermute(pay_b, "gx", pairs_b)
+    small, local, *z_pay = call(
+        functools.partial(local_kernel, sizes),
+        [held, positions, target6, wall_flags_xaxis, z_flags, coarse_logk.reshape(1, -1)],
+        VMEM,
+        [(2, 8, LANES), shape] + [z_shape] * count,
+        VMEM,
+        [],
+        16 * 1024,
+    )
     z_got = along_z(z_pay, nz)
     whole, send, *w_pay = call(
         functools.partial(sums_kernel, sizes, length),

time: 27.7 us -> 26.3 us (0.949)
  waiting for transfers between devices: 3.17 us -> 1.53 us
    ppermute x1, waiting for transfers between devices: 3.16 us -> 0.32 us  [shards(): got_a = lax.ppermute(pay_a, 'gx', pairs_a)]
    ppermute x2, waiting for transfers between devices: 0.01 us -> 1.2 us  [along_z(): return [lax.ppermute(payloads[0], 'gz', [(0, 1), (1, 0)])]]
    ppermute x2, starting transfers between devices: 0.52 us -> 0.07 us  [along_z(): return [lax.ppermute(payloads[0], 'gz', [(0, 1), (1, 0)])]]
    ppermute x1, starting transfers between devices: 2.56 us -> 3 us  [shards(): got_a = lax.ppermute(pay_a, 'gx', pairs_a)]
    pallas_call x3 -> x5, Pallas kernels: 2.94 us -> 3.04 us  [call(): pl.pallas_call(kernel, out_shape=[jax.ShapeDtypeStruct(shape, jnp.float32...]
    unnamed x10 -> x12, local copies, waits for them, and re-layouts: 0.69 us -> 0.65 us
  transfers between devices with their start and end apart: 4 -> 4, of which waited for: 1 -> 2; matrix products, arithmetic and copies ran while one was open for 0% -> 0% of each run, Pallas kernels for 0% -> 1%
where the time goes in v3:
time: 26.3 us; the launch traced here: 26.1 us
  blocking collectives  16.4 us (62%)
  starting transfers between devices  3.73 us (14%)
  Pallas kernels  3.04 us (12%)
  waiting for transfers between devices  1.53 us (6%)
  between operations  0.77 us (3%)
  local copies, waits for them, and re-layouts  0.65 us (2%)
    all_to_all x1, blocking collectives, shards(): received = lax.all_to_all(send, ('gx', 'gz'), 0, 0, tiled=True)  16.4 us
    pallas_call x5, Pallas kernels, call(): pl.pallas_call(kernel, out_shape=[jax.ShapeDtypeStruct(shape, jnp.float32...  3.04 us
    ppermute x1, starting transfers between devices, shards(): got_a = lax.ppermute(pay_a, 'gx', pairs_a)  3 us
    ppermute x2, waiting for transfers between devices, along_z(): return [lax.ppermute(payloads[0], 'gz', [(0, 1), (1, 0)])]  1.2 us
    ppermute x1, starting transfers between devices, shards(): got_b = lax.ppermute(pay_b, 'gx', pairs_b)  0.66 us
    unnamed x12, local copies, waits for them, and re-layouts  0.65 us
  transfers between devices with their start and end apart: 4, of which 2 were waited for; matrix products, arithmetic and copies ran while one was open for 0% of the time, Pallas kernels for 1%

profile of v3, /device:TPU:0, one launch (start us, length us, event | category | flops | bytes accessed | tf_op | source)
XLA Modules:
  0.0 26.1 jit_solution(13990487076142045118)
XLA Ops:
  0.6 0.0 copy-start.1
  0.6 0.0 copy-start.2
  0.7 0.0 copy-start.4
  0.7 0.0 copy-start.3
  0.7 1.1 %shard_map.86 = (f32[2,4,4,2,8,128]{5,4,3,2,1,0:T(8,128)S(1)}, f32[29,8,128]{2,1,0:T(8,128)S(1)}, f32[29,8,128]{2,1,0:T(8,128)S(1)}) custom-call(f32[2,4,4,2,8,128]{5,4,3,2,1,0:T(8,128)} %bitcast.21, f32[2,4,4,2,8,128]{5,4,3,2,1,0:T(8,128)} %bitcast.12), custom_call_target="tpu_custom_call" | custom-call | flops 2000000 | bytes 800000 | tf_op jit(solution)/shard_map/pallas_call | solution.py:479
  1.8 0.0 copy-start
  1.8 0.0 copy-done.1
  1.8 0.0 copy-done.2
  1.9 0.0 copy-done.4
  1.9 3.0 %collective-permute-start = (f32[29,8,128]{2,1,0:T(8,128)S(1)}, f32[29,8,128]{2,1,0:T(8,128)S(1)}, u32[]{:S(2)}, u32[]{:S(2)}) collective-permute-start(f32[29,8,128]{2,1,0:T(8,128)S(1)} %get-tuple-element.22), channel_id=1, source_target_pairs={{0,2},{4,6},{8,10},{12,14},{16,18},{20,22},{24,26},{28,30},{2,0},{... | collective-permute-start | bytes 356360 | tf_op jit(solution)/shard_map/ppermute | solution.py:532
  4.9 0.7 %collective-permute-start.1 = (f32[29,8,128]{2,1,0:T(8,128)S(1)}, f32[29,8,128]{2,1,0:T(8,128)S(1)}, u32[]{:S(2)}, u32[]{:S(2)}) collective-permute-start(f32[29,8,128]{2,1,0:T(8,128)S(1)} %get-tuple-element.23), channel_id=1, source_target_pairs={{2,4},{6,8},{10,12},{14,16},{18,20},{22,24},{26,28},{4,2},{8,6},{1... | collective-permute-start | bytes 356360 | tf_op jit(solution)/shard_map/ppermute | solution.py:533
  5.6 0.0 copy-start.5
  5.6 0.0 copy-done.3
  5.6 0.0 copy-done
  5.6 0.6 %copy-done.5 = f32[32]{0:T(128)S(1)} copy-done((f32[32]{0:T(128)S(1)}, f32[32]{0:T(128)}, u32[]{:S(2)}) %copy-start.5) | copy-done | bytes 152
  6.2 0.3 %shard_map.88 = (f32[2,8,128]{2,1,0:T(8,128)S(1)}, f32[2,4,4,2,8,128]{5,4,3,2,1,0:T(8,128)S(1)}, f32[9,8,128]{2,1,0:T(8,128)S(1)}) custom-call(f32[2,4,4,2,8,128]{5,4,3,2,1,0:T(8,128)S(1)} %get-tuple-element.16.state, f32[8,128]{1,0:T(8,128)S(1)} %get-tuple-element.19.positions, f32[2,4,4,2,8,128]{5,4,3,2,1,0:T(8,128)S(1)} %bitcast.13, ...), custom_call_target="tpu_custom_call" | custom-call | flops 2000000 | bytes 800000 | tf_op jit(solution)/shard_map/pallas_call | solution.py:479
  6.5 0.1 collective-permute-start.2
  6.6 1.2 %collective-permute-done.2.refs_0_ = f32[9,8,128]{2,1,0:T(8,128)S(1)} collective-permute-done((f32[9,8,128]{2,1,0:T(8,128)S(1)}, f32[9,8,128]{2,1,0:T(8,128)S(1)}, u32[]{:S(2)}, u32[]{:S(2)}) %collective-permute-start.2) | collective-permute-done | bytes 36896 | tf_op jit(solution)/shard_map/ppermute | solution.py:497
  7.8 0.3 %collective-permute-done.got_a = f32[29,8,128]{2,1,0:T(8,128)S(1)} collective-permute-done((f32[29,8,128]{2,1,0:T(8,128)S(1)}, f32[29,8,128]{2,1,0:T(8,128)S(1)}, u32[]{:S(2)}, u32[]{:S(2)}) %collective-permute-start) | collective-permute-done | bytes 118816 | tf_op jit(solution)/shard_map/ppermute | solution.py:532
  8.1 0.0 collective-permute-done.1.got_b
  8.1 0.3 %shard_map.89 = (f32[2,4,4,2,8,128]{5,4,3,2,1,0:T(8,128)S(1)}, f32[32,128]{1,0:T(8,128)S(1)}, f32[12,8,128]{2,1,0:T(8,128)S(1)}) custom-call(f32[2,4,4,2,8,128]{5,4,3,2,1,0:T(8,128)S(1)} %get-tuple-element.16.state, f32[2,8,128]{2,1,0:T(8,128)S(1)} %get-tuple-element.20.small, f32[2,4,4,2,8,128]{5,4,3,2,1,0:T(8,128)S(1)} %get-tuple-element.21.local, ...), custom_call_target="tpu_custom_call" | custom-call | flops 2000000 | bytes 800000 | tf_op jit(solution)/shard_map/pallas_call | solution.py:479
  8.5 0.0 collective-permute-start.3
  8.5 16.4 %all_to_all.11 = f32[32,1,128]{2,1,0:T(1,128)S(1)} all-to-all(f32[32,1,128]{2,1,0:T(1,128)S(1)} %bitcast.15), channel_id=1, replica_groups=mesh['gx'=16,'gz'=2] {'gx','gz'}, dimensions={0} | all-to-all | bytes 32768 | tf_op jit(solution)/shard_map/all_to_all | solution.py:554
  24.9 0.0 collective-permute-done.3.refs_1_
  24.9 1.2 %shard_map.90 = (f32[2,4,4,2,8,128]{5,4,3,2,1,0:T(8,128)}, f32[1,32]{1,0:T(1,128)}) custom-call(f32[2,4,4,2,8,128]{5,4,3,2,1,0:T(8,128)S(1)} %get-tuple-element.16.state, f32[2,8,128]{2,1,0:T(8,128)S(1)} %get-tuple-element.20.small, f32[2,4,4,2,8,128]{5,4,3,2,1,0:T(8,128)S(1)} %get-tuple-element.25.whole, f32[29,8,128]{2,1,0:T(8,128)S(1)} %collective-permute-done.got_a, ...), custom_call_target="tpu_custom_call" | custom-call | flops 2000000 | bytes 800000 | tf_op jit(solution)/shard_map/pallas_call | solution.py:479
  (1 shorter events, 0.0 us)
Async XLA Ops:
  0.6 1.2 %copy-start.1 = (s32[1024]{0:T(1024)S(1)}, s32[1024]{0:T(1024)}, u32[]{:S(2)}) copy-start(s32[1024]{0:T(1024)} %param.10) | copy-start | bytes 12292
  0.6 1.2 %copy-start.2 = (s32[2,1,128]{2,1,0:T(1,128)S(1)}, s32[2,1,128]{2,1,0:T(1,128)}, u32[]{:S(2)}) copy-start(s32[2,1,128]{2,1,0:T(1,128)} %param.13) | copy-start | bytes 3076
  0.7 1.2 %copy-start.4 = (s32[1,2,128]{2,1,0:T(2,128)S(1)}, s32[1,2,128]{2,1,0:T(2,128)}, u32[]{:S(2)}) copy-start(s32[1,2,128]{2,1,0:T(2,128)} %param.11) | copy-start | bytes 3076
  0.7 4.9 %copy-start.3 = (s32[2,2,128]{2,1,0:T(2,128)S(1)}, s32[2,2,128]{2,1,0:T(2,128)}, u32[]{:S(2)}) copy-start(s32[2,2,128]{2,1,0:T(2,128)} %x_wall.1) | copy-start | bytes 6148
  1.8 3.8 %copy-start = (f32[1,2,4,64,128]{4,3,2,1,0:T(8,128)S(1)}, f32[1,2,4,64,128]{4,3,2,1,0:T(8,128)}, u32[]{:S(2)}) copy-start(f32[1,2,4,64,128]{4,3,2,1,0:T(8,128)} %param.8) | copy-start | bytes 786436
  1.9 6.2 %collective-permute-start = (f32[29,8,128]{2,1,0:T(8,128)S(1)}, f32[29,8,128]{2,1,0:T(8,128)S(1)}, u32[]{:S(2)}, u32[]{:S(2)}) collective-permute-start(f32[29,8,128]{2,1,0:T(8,128)S(1)} %get-tuple-element.22), channel_id=1, source_target_pairs={{0,2},{4,6},{8,10},{12,14},{16,18},{20,22},{24,26},{28,30},{2,0},{... | collective-permute-start | bytes 356360 | tf_op jit(solution)/shard_map/ppermute | solution.py:532
  4.9 3.2 %collective-permute-start.1 = (f32[29,8,128]{2,1,0:T(8,128)S(1)}, f32[29,8,128]{2,1,0:T(8,128)S(1)}, u32[]{:S(2)}, u32[]{:S(2)}) collective-permute-start(f32[29,8,128]{2,1,0:T(8,128)S(1)} %get-tuple-element.23), channel_id=1, source_target_pairs={{2,4},{6,8},{10,12},{14,16},{18,20},{22,24},{26,28},{4,2},{8,6},{1... | collective-permute-start | bytes 356360 | tf_op jit(solution)/shard_map/ppermute | solution.py:533
  5.6 0.7 %copy-start.5 = (f32[32]{0:T(128)S(1)}, f32[32]{0:T(128)}, u32[]{:S(2)}) copy-start(f32[32]{0:T(128)} %param.9) | copy-start | bytes 388
  6.5 1.3 %collective-permute-start.2 = (f32[9,8,128]{2,1,0:T(8,128)S(1)}, f32[9,8,128]{2,1,0:T(8,128)S(1)}, u32[]{:S(2)}, u32[]{:S(2)}) collective-permute-start(f32[9,8,128]{2,1,0:T(8,128)S(1)} %get-tuple-element.24), channel_id=1, source_target_pairs={{0,1},{1,0},{2,3},{3,2},{4,5},{5,4},{6,7},{7,6},{8,9},{9,8},{10,11... | collective-permute-start | bytes 110600 | tf_op jit(solution)/shard_map/ppermute | solution.py:497
  8.5 16.4 %collective-permute-start.3 = (f32[12,8,128]{2,1,0:T(8,128)S(1)}, f32[12,8,128]{2,1,0:T(8,128)S(1)}, u32[]{:S(2)}, u32[]{:S(2)}) collective-permute-start(f32[12,8,128]{2,1,0:T(8,128)S(1)} %get-tuple-element.27), channel_id=1, source_target_pairs={{0,1},{1,0},{2,3},{3,2},{4,5},{5,4},{6,7},{7,6},{8,9},{9,8},{10,11... | collective-permute-start | bytes 147464 | tf_op jit(solution)/shard_map/ppermute | solution.py:497

commit v4 on v3

--- a/solution.py
+++ b/solution.py
@@ -19,6 +19,7 @@
 Z_SLOTS, Z_BLOCKS = 8, 9
 W_CORNERS, W_BLOCKS = 8, 12
 X_WALL, Z_WALL, LOGK = 0, 4, 6
+SUMS = 2
 
 
 def derivative_matrix():
@@ -238,6 +239,8 @@
     positions[...] = block
     flip = jnp.where(x_place % 2 == 0, -1.0, 1.0)
     for first, pay, factor in ((first_a, pay_a, flip), (first_b, pay_b, -flip)):
+        for i in range(X_SLOTS):
+            pay[i] = first[i]
         pay[X_SLOTS] = block
         for z in range(2):
             weight, flag = wall_rows(sizes, rows, weights, z, z_wall)
@@ -271,6 +274,10 @@
         wall = wall_terms(u, 2, -float(sign), weight, flag, False)
         for f, (v, j, a, w) in enumerate(zip(grads + [divergence], jumps, across, wall)):
             local[z, f] = SCALE * v + j + a + w - target[z, f]
+        first = sum(local[z, k] * u[k] for k in range(3))
+        second = sum(u[k] * u[k] for k in range(3))
+        small[SUMS, z : z + 1, :] = jnp.sum(first, axis=(0, 1, 2))[None]
+        small[SUMS, 2 + z : 3 + z, :] = jnp.sum(second, axis=(0, 1, 2))[None]
     faces = [packed_face(rows, load(state, z), 2 * z - 1) for z in range(2)]
     for direction in range(len(z_pay)):
         upper = z_place == 0 if nz == 2 else direction == 0
@@ -294,7 +301,7 @@
     rows = Rows()
     weights = z_weights(rows)
     corners = {}
-    first_sums, second_sums = [], []
+    sums = []
     for z in range(2):
         u = load(state, z)
         for f in range(4):
@@ -305,6 +312,7 @@
         terms = met_terms(u, packed, float(sign), weights[sign] * jnp.where(inside, 1.0, 0.0))
         for f in range(4):
             whole[z, f] += terms[f]
+        total = sum(jnp.sum(terms[k] * u[k], axis=(0, 1)) for k in range(3))
         for side in range(2):
             sign = 1.0 if side else -1.0
             a = 3 * side
@@ -322,31 +330,29 @@
             terms = face_terms(inner, outer, 0, sign, JUMP, False)
             for f in range(4):
                 whole[z, f, a] += terms[f]
-        first = sum(whole[z, k] * u[k] for k in range(3))
-        second = sum(u[k] * u[k] for k in range(3))
-        first_sums.append(jnp.sum(first, axis=(0, 1, 2))[None])
-        second_sums.append(jnp.sum(second, axis=(0, 1, 2))[None])
+            total += sum(jnp.sum(terms[k] * mine[k], axis=0) for k in range(3))
+        local_sum = small[SUMS, z : z + 1, :]
+        sums.append((local_sum + jnp.sum(total, axis=0)[None], small[SUMS, 2 + z : 3 + z, :]))
     devices = send.shape[0]
     slots = small[0].astype(jnp.int32)
-    total = jnp.zeros((devices, LANES), jnp.float32)
     place = lax.broadcasted_iota(jnp.int32, (LANES, LANES), 0)
     owner = lax.broadcasted_iota(jnp.int32, (devices, LANES), 0)
-    for z in range(2):
+    chosen, values = [], []
+    for z, (first, second) in enumerate(sums):
         slot = slots[z : z + 1, :]
-        chosen = jnp.where(owner == slot // length, 1.0, 0.0).astype(jnp.bfloat16)
+        chosen.append(jnp.where(owner == slot // length, 1.0, 0.0).astype(jnp.bfloat16))
         position = slot % length
-        values = jnp.where(
-            place == position + length,
-            first_sums[z],
-            jnp.where(place == position + 2 * length, second_sums[z], 0.0),
+        value = jnp.where(
+            place == position + length, first, jnp.where(place == position + 2 * length, second, 0.0)
         )
-        for _ in range(3):
-            piece = values.astype(jnp.bfloat16)
-            total += lax.dot_general(
-                chosen, piece, (((1,), (1,)), ((), ())), preferred_element_type=jnp.float32
-            )
-            values = values - piece.astype(jnp.float32)
-    send[...] = total
+        piece = value.astype(jnp.bfloat16)
+        values += [piece, (value - piece.astype(jnp.float32)).astype(jnp.bfloat16)]
+    send[...] = lax.dot_general(
+        jnp.concatenate([chosen[0], chosen[0], chosen[1], chosen[1]], axis=1),
+        jnp.concatenate(values, axis=1),
+        (((1,), (1,)), ((), ())),
+        preferred_element_type=jnp.float32,
+    )
     logk = small[1, LOGK : LOGK + 1, 0:length]
     send[:, 0:length] = jnp.broadcast_to(logk, (devices, length))
     faces = [packed_face(rows, load(whole, z), 2 * z - 1) for z in range(2)]
@@ -475,14 +481,13 @@
         copy.wait()
 
 
-def call(kernel, operands, in_spec, shapes, out_spec, scratch, room, aliases={}):
+def call(kernel, operands, in_spec, shapes, out_spec, scratch, room):
     return pl.pallas_call(
         kernel,
         out_shape=[jax.ShapeDtypeStruct(shape, jnp.float32) for shape in shapes],
         in_specs=[in_spec] * len(operands),
         out_specs=[out_spec] * len(shapes),
         scratch_shapes=scratch,
-        input_output_aliases=aliases,
         compiler_params=pltpu.CompilerParams(vmem_limit_bytes=room * 1024),
         cost_estimate=pl.CostEstimate(flops=2000000, bytes_accessed=800000, transcendentals=0),
     )(*operands)
@@ -525,7 +530,6 @@
         VMEM,
         [],
         16 * 1024,
-        {0: 0, 1: 1},
     )
     pairs_b = both_ways([(i, i + 1) for i in range(1, nx - 1, 2)])
     pairs_a = both_ways([(i, i + 1) for i in range(0, nx - 1, 2)])
@@ -535,7 +539,7 @@
         functools.partial(local_kernel, sizes),
         [held, positions, target6, wall_flags_xaxis, z_flags, coarse_logk.reshape(1, -1)],
         VMEM,
-        [(2, 8, LANES), shape] + [z_shape] * count,
+        [(3, 8, LANES), shape] + [z_shape] * count,
         VMEM,
         [],
         16 * 1024,

time: 26.3 us -> 26.3 us (level)
  no operation moved by 1% of the time
where the time goes in v4:
time: 26.3 us; the launch traced here: 26.1 us
  blocking collectives  16.4 us (62%)
  starting transfers between devices  3.8 us (14%)
  Pallas kernels  3.02 us (11%)
  waiting for transfers between devices  1.49 us (6%)
  between operations  0.77 us (3%)
  local copies, waits for them, and re-layouts  0.65 us (2%)
    all_to_all x1, blocking collectives, shards(): received = lax.all_to_all(send, ('gx', 'gz'), 0, 0, tiled=True)  16.4 us
    pallas_call x5, Pallas kernels, call(): pl.pallas_call(kernel, out_shape=[jax.ShapeDtypeStruct(shape, jnp.float32...  3.02 us
    ppermute x1, starting transfers between devices, shards(): got_a = lax.ppermute(pay_a, 'gx', pairs_a)  3 us
    ppermute x2, waiting for transfers between devices, along_z(): return [lax.ppermute(payloads[0], 'gz', [(0, 1), (1, 0)])]  1.2 us
    ppermute x1, starting transfers between devices, shards(): got_b = lax.ppermute(pay_b, 'gx', pairs_b)  0.66 us
    unnamed x12, local copies, waits for them, and re-layouts  0.65 us
  transfers between devices with their start and end apart: 4, of which 2 were waited for; matrix products, arithmetic and copies ran while one was open for 0% of the time, Pallas kernels for 1%

profile of v4, /device:TPU:0, one launch (start us, length us, event | category | flops | bytes accessed | tf_op | source)
XLA Modules:
  0.0 26.1 jit_solution(5542220945153639564)
XLA Ops:
  0.6 0.0 copy-start.1
  0.6 0.0 copy-start.2
  0.7 0.0 copy-start.4
  0.7 0.0 copy-start.3
  0.7 1.1 %shard_map.86 = (f32[2,4,4,2,8,128]{5,4,3,2,1,0:T(8,128)S(1)}, f32[29,8,128]{2,1,0:T(8,128)S(1)}, f32[29,8,128]{2,1,0:T(8,128)S(1)}) custom-call(f32[2,4,4,2,8,128]{5,4,3,2,1,0:T(8,128)} %bitcast.21, f32[2,4,4,2,8,128]{5,4,3,2,1,0:T(8,128)} %bitcast.12), custom_call_target="tpu_custom_call" | custom-call | flops 2000000 | bytes 800000 | tf_op jit(solution)/shard_map/pallas_call | solution.py:485
  1.8 0.0 copy-start
  1.8 0.0 copy-done.1
  1.8 0.0 copy-done.2
  1.9 0.0 copy-done.4
  1.9 3.0 %collective-permute-start = (f32[29,8,128]{2,1,0:T(8,128)S(1)}, f32[29,8,128]{2,1,0:T(8,128)S(1)}, u32[]{:S(2)}, u32[]{:S(2)}) collective-permute-start(f32[29,8,128]{2,1,0:T(8,128)S(1)} %get-tuple-element.22), channel_id=1, source_target_pairs={{0,2},{4,6},{8,10},{12,14},{16,18},{20,22},{24,26},{28,30},{2,0},{... | collective-permute-start | bytes 356360 | tf_op jit(solution)/shard_map/ppermute | solution.py:536
  4.9 0.7 %collective-permute-start.1 = (f32[29,8,128]{2,1,0:T(8,128)S(1)}, f32[29,8,128]{2,1,0:T(8,128)S(1)}, u32[]{:S(2)}, u32[]{:S(2)}) collective-permute-start(f32[29,8,128]{2,1,0:T(8,128)S(1)} %get-tuple-element.23), channel_id=1, source_target_pairs={{2,4},{6,8},{10,12},{14,16},{18,20},{22,24},{26,28},{4,2},{8,6},{1... | collective-permute-start | bytes 356360 | tf_op jit(solution)/shard_map/ppermute | solution.py:537
  5.6 0.0 copy-start.5
  5.6 0.0 copy-done.3
  5.6 0.0 copy-done
  5.6 0.6 %copy-done.5 = f32[32]{0:T(128)S(1)} copy-done((f32[32]{0:T(128)S(1)}, f32[32]{0:T(128)}, u32[]{:S(2)}) %copy-start.5) | copy-done | bytes 152
  6.2 0.3 %shard_map.88 = (f32[3,8,128]{2,1,0:T(8,128)S(1)}, f32[2,4,4,2,8,128]{5,4,3,2,1,0:T(8,128)S(1)}, f32[9,8,128]{2,1,0:T(8,128)S(1)}) custom-call(f32[2,4,4,2,8,128]{5,4,3,2,1,0:T(8,128)S(1)} %get-tuple-element.16.state, f32[8,128]{1,0:T(8,128)S(1)} %get-tuple-element.19.positions, f32[2,4,4,2,8,128]{5,4,3,2,1,0:T(8,128)S(1)} %bitcast.13, ...), custom_call_target="tpu_custom_call" | custom-call | flops 2000000 | bytes 800000 | tf_op jit(solution)/shard_map/pallas_call | solution.py:485
  6.6 0.1 collective-permute-start.2
  6.7 1.2 %collective-permute-done.2.refs_0_ = f32[9,8,128]{2,1,0:T(8,128)S(1)} collective-permute-done((f32[9,8,128]{2,1,0:T(8,128)S(1)}, f32[9,8,128]{2,1,0:T(8,128)S(1)}, u32[]{:S(2)}, u32[]{:S(2)}) %collective-permute-start.2) | collective-permute-done | bytes 36896 | tf_op jit(solution)/shard_map/ppermute | solution.py:502
  7.9 0.3 %collective-permute-done.got_a = f32[29,8,128]{2,1,0:T(8,128)S(1)} collective-permute-done((f32[29,8,128]{2,1,0:T(8,128)S(1)}, f32[29,8,128]{2,1,0:T(8,128)S(1)}, u32[]{:S(2)}, u32[]{:S(2)}) %collective-permute-start) | collective-permute-done | bytes 118816 | tf_op jit(solution)/shard_map/ppermute | solution.py:536
  8.1 0.0 collective-permute-done.1.got_b
  8.1 0.3 %shard_map.89 = (f32[2,4,4,2,8,128]{5,4,3,2,1,0:T(8,128)S(1)}, f32[32,128]{1,0:T(8,128)S(1)}, f32[12,8,128]{2,1,0:T(8,128)S(1)}) custom-call(f32[2,4,4,2,8,128]{5,4,3,2,1,0:T(8,128)S(1)} %get-tuple-element.16.state, f32[3,8,128]{2,1,0:T(8,128)S(1)} %get-tuple-element.20.small, f32[2,4,4,2,8,128]{5,4,3,2,1,0:T(8,128)S(1)} %get-tuple-element.21.local, ...), custom_call_target="tpu_custom_call" | custom-call | flops 2000000 | bytes 800000 | tf_op jit(solution)/shard_map/pallas_call | solution.py:485
  8.4 0.1 collective-permute-start.3
  8.5 16.4 %all_to_all.11 = f32[32,1,128]{2,1,0:T(1,128)S(1)} all-to-all(f32[32,1,128]{2,1,0:T(1,128)S(1)} %bitcast.15), channel_id=1, replica_groups=mesh['gx'=16,'gz'=2] {'gx','gz'}, dimensions={0} | all-to-all | bytes 32768 | tf_op jit(solution)/shard_map/all_to_all | solution.py:558
  24.9 0.0 collective-permute-done.3.refs_1_
  24.9 1.2 %shard_map.90 = (f32[2,4,4,2,8,128]{5,4,3,2,1,0:T(8,128)}, f32[1,32]{1,0:T(1,128)}) custom-call(f32[2,4,4,2,8,128]{5,4,3,2,1,0:T(8,128)S(1)} %get-tuple-element.16.state, f32[3,8,128]{2,1,0:T(8,128)S(1)} %get-tuple-element.20.small, f32[2,4,4,2,8,128]{5,4,3,2,1,0:T(8,128)S(1)} %get-tuple-element.25.whole, f32[29,8,128]{2,1,0:T(8,128)S(1)} %collective-permute-done.got_a, ...), custom_call_target="tpu_custom_call" | custom-call | flops 2000000 | bytes 800000 | tf_op jit(solution)/shard_map/pallas_call | solution.py:485
  (1 shorter events, 0.0 us)
Async XLA Ops:
  0.6 1.2 %copy-start.1 = (s32[1024]{0:T(1024)S(1)}, s32[1024]{0:T(1024)}, u32[]{:S(2)}) copy-start(s32[1024]{0:T(1024)} %param.10) | copy-start | bytes 12292
  0.6 1.2 %copy-start.2 = (s32[2,1,128]{2,1,0:T(1,128)S(1)}, s32[2,1,128]{2,1,0:T(1,128)}, u32[]{:S(2)}) copy-start(s32[2,1,128]{2,1,0:T(1,128)} %param.13) | copy-start | bytes 3076
  0.7 1.2 %copy-start.4 = (s32[1,2,128]{2,1,0:T(2,128)S(1)}, s32[1,2,128]{2,1,0:T(2,128)}, u32[]{:S(2)}) copy-start(s32[1,2,128]{2,1,0:T(2,128)} %param.11) | copy-start | bytes 3076
  0.7 4.9 %copy-start.3 = (s32[2,2,128]{2,1,0:T(2,128)S(1)}, s32[2,2,128]{2,1,0:T(2,128)}, u32[]{:S(2)}) copy-start(s32[2,2,128]{2,1,0:T(2,128)} %x_wall.1) | copy-start | bytes 6148
  1.8 3.8 %copy-start = (f32[1,2,4,64,128]{4,3,2,1,0:T(8,128)S(1)}, f32[1,2,4,64,128]{4,3,2,1,0:T(8,128)}, u32[]{:S(2)}) copy-start(f32[1,2,4,64,128]{4,3,2,1,0:T(8,128)} %param.8) | copy-start | bytes 786436
  1.9 6.2 %collective-permute-start = (f32[29,8,128]{2,1,0:T(8,128)S(1)}, f32[29,8,128]{2,1,0:T(8,128)S(1)}, u32[]{:S(2)}, u32[]{:S(2)}) collective-permute-start(f32[29,8,128]{2,1,0:T(8,128)S(1)} %get-tuple-element.22), channel_id=1, source_target_pairs={{0,2},{4,6},{8,10},{12,14},{16,18},{20,22},{24,26},{28,30},{2,0},{... | collective-permute-start | bytes 356360 | tf_op jit(solution)/shard_map/ppermute | solution.py:536
  4.9 3.2 %collective-permute-start.1 = (f32[29,8,128]{2,1,0:T(8,128)S(1)}, f32[29,8,128]{2,1,0:T(8,128)S(1)}, u32[]{:S(2)}, u32[]{:S(2)}) collective-permute-start(f32[29,8,128]{2,1,0:T(8,128)S(1)} %get-tuple-element.23), channel_id=1, source_target_pairs={{2,4},{6,8},{10,12},{14,16},{18,20},{22,24},{26,28},{4,2},{8,6},{1... | collective-permute-start | bytes 356360 | tf_op jit(solution)/shard_map/ppermute | solution.py:537
  5.6 0.7 %copy-start.5 = (f32[32]{0:T(128)S(1)}, f32[32]{0:T(128)}, u32[]{:S(2)}) copy-start(f32[32]{0:T(128)} %param.9) | copy-start | bytes 388
  6.6 1.3 %collective-permute-start.2 = (f32[9,8,128]{2,1,0:T(8,128)S(1)}, f32[9,8,128]{2,1,0:T(8,128)S(1)}, u32[]{:S(2)}, u32[]{:S(2)}) collective-permute-start(f32[9,8,128]{2,1,0:T(8,128)S(1)} %get-tuple-element.24), channel_id=1, source_target_pairs={{0,1},{1,0},{2,3},{3,2},{4,5},{5,4},{6,7},{7,6},{8,9},{9,8},{10,11... | collective-permute-start | bytes 110600 | tf_op jit(solution)/shard_map/ppermute | solution.py:502
  8.4 16.4 %collective-permute-start.3 = (f32[12,8,128]{2,1,0:T(8,128)S(1)}, f32[12,8,128]{2,1,0:T(8,128)S(1)}, u32[]{:S(2)}, u32[]{:S(2)}) collective-permute-start(f32[12,8,128]{2,1,0:T(8,128)S(1)} %get-tuple-element.27), channel_id=1, source_target_pairs={{0,1},{1,0},{2,3},{3,2},{4,5},{5,4},{6,7},{7,6},{8,9},{9,8},{10,11... | collective-permute-start | bytes 147464 | tf_op jit(solution)/shard_map/ppermute | solution.py:502

commit v5 on v4

--- a/solution.py
+++ b/solution.py
@@ -19,7 +19,6 @@
 Z_SLOTS, Z_BLOCKS = 8, 9
 W_CORNERS, W_BLOCKS = 8, 12
 X_WALL, Z_WALL, LOGK = 0, 4, 6
-SUMS = 2
 
 
 def derivative_matrix():
@@ -219,7 +218,9 @@
     return weight, flags[z : z + 1, :].astype(jnp.float32)
 
 
-def edges_kernel(sizes, first_a, first_b, cell_of, cell_slot, z_wall, pay_a, pay_b, positions):
+def edges_kernel(
+    sizes, first_a, first_b, cell_of, cell_slot, x_wall, z_wall, logk, pay_a, pay_b, small
+):
     nx, nz = sizes
     x_place, z_place = lax.axis_index("gx"), lax.axis_index("gz")
     rows = Rows()
@@ -236,7 +237,11 @@
         slots.append(slot.astype(jnp.float32))
     row = lax.broadcasted_iota(jnp.int32, (8, LANES), 0)
     block = jnp.where(row == 0, slots[0], jnp.where(row == 1, slots[1], 0.0))
-    positions[...] = block
+    small[0] = block
+    for side in range(2):
+        small[1, X_WALL + 2 * side : X_WALL + 2 * side + 2, :] = x_wall[side].astype(jnp.float32)
+    small[1, Z_WALL : Z_WALL + 2, :] = z_wall[...].astype(jnp.float32)
+    small[1, LOGK : LOGK + 1, 0 : logk.shape[1]] = logk[...]
     flip = jnp.where(x_place % 2 == 0, -1.0, 1.0)
     for first, pay, factor in ((first_a, pay_a, flip), (first_b, pay_b, -flip)):
         for i in range(X_SLOTS):
@@ -251,17 +256,12 @@
             pay[pl.ds(tangential, 2)] = first[pl.ds(tangential, 2)] + terms[2]
 
 
-def local_kernel(sizes, state, positions, target, x_wall, z_wall, logk, small, local, *z_pay):
+def local_kernel(sizes, state, small, target, local, sums, *z_pay):
     nx, nz = sizes
     z_place = lax.axis_index("gz")
     rows = Rows()
     derivative = Derivative(rows, derivative_matrix())
     weights = z_weights(rows)
-    small[0] = positions[...]
-    for side in range(2):
-        small[1, X_WALL + 2 * side : X_WALL + 2 * side + 2, :] = x_wall[side].astype(jnp.float32)
-    small[1, Z_WALL : Z_WALL + 2, :] = z_wall[...].astype(jnp.float32)
-    small[1, LOGK : LOGK + 1, 0 : logk.shape[1]] = logk[...]
     for z in range(2):
         u = load(state, z)
         other = load(state, 1 - z)
@@ -270,19 +270,19 @@
         jumps = y_terms(u, rows, False)
         sign = 1 if z == 0 else -1
         across = z_terms(u, other, float(sign), weights[sign], False)
-        weight, flag = wall_rows(sizes, rows, weights, z, z_wall)
+        weight, flag = wall_rows(sizes, rows, weights, z, small[1, Z_WALL : Z_WALL + 2, :])
         wall = wall_terms(u, 2, -float(sign), weight, flag, False)
         for f, (v, j, a, w) in enumerate(zip(grads + [divergence], jumps, across, wall)):
             local[z, f] = SCALE * v + j + a + w - target[z, f]
         first = sum(local[z, k] * u[k] for k in range(3))
         second = sum(u[k] * u[k] for k in range(3))
-        small[SUMS, z : z + 1, :] = jnp.sum(first, axis=(0, 1, 2))[None]
-        small[SUMS, 2 + z : 3 + z, :] = jnp.sum(second, axis=(0, 1, 2))[None]
+        sums[z : z + 1, :] = jnp.sum(first, axis=(0, 1, 2))[None]
+        sums[2 + z : 3 + z, :] = jnp.sum(second, axis=(0, 1, 2))[None]
     faces = [packed_face(rows, load(state, z), 2 * z - 1) for z in range(2)]
     for direction in range(len(z_pay)):
         upper = z_place == 0 if nz == 2 else direction == 0
         z_pay[direction][0:8] = jnp.where(upper, faces[1], faces[0]).reshape(8, 8, LANES)
-        slot = jnp.where(upper, positions[1:2, :], positions[0:1, :])
+        slot = jnp.where(upper, small[0, 1:2, :], small[0, 0:1, :])
         z_pay[direction][Z_SLOTS] = jnp.broadcast_to(slot, (8, LANES))
 
 
@@ -291,7 +291,7 @@
     return jnp.where(even, b, a) if side == 0 else jnp.where(even, a, b)
 
 
-def sums_kernel(sizes, length, state, small, local, got_a, got_b, *refs):
+def sums_kernel(sizes, length, state, small, local, local_sums, got_a, got_b, *refs):
     nx, nz = sizes
     count = 1 if nz == 2 else 2
     z_got, (whole, send), z_pay = refs[:count], refs[count : count + 2], refs[count + 2 :]
@@ -331,8 +331,8 @@
             for f in range(4):
                 whole[z, f, a] += terms[f]
             total += sum(jnp.sum(terms[k] * mine[k], axis=0) for k in range(3))
-        local_sum = small[SUMS, z : z + 1, :]
-        sums.append((local_sum + jnp.sum(total, axis=0)[None], small[SUMS, 2 + z : 3 + z, :]))
+        first = local_sums[z : z + 1, :] + jnp.sum(total, axis=0)[None]
+        sums.append((first, local_sums[2 + z : 3 + z, :]))
     devices = send.shape[0]
     slots = small[0].astype(jnp.int32)
     place = lax.broadcasted_iota(jnp.int32, (LANES, LANES), 0)
@@ -345,10 +345,12 @@
         value = jnp.where(
             place == position + length, first, jnp.where(place == position + 2 * length, second, 0.0)
         )
-        piece = value.astype(jnp.bfloat16)
-        values += [piece, (value - piece.astype(jnp.float32)).astype(jnp.bfloat16)]
+        for _ in range(3):
+            piece = value.astype(jnp.bfloat16)
+            values.append(piece)
+            value = value - piece.astype(jnp.float32)
     send[...] = lax.dot_general(
-        jnp.concatenate([chosen[0], chosen[0], chosen[1], chosen[1]], axis=1),
+        jnp.concatenate([chosen[0]] * 3 + [chosen[1]] * 3, axis=1),
         jnp.concatenate(values, axis=1),
         (((1,), (1,)), ((), ())),
         preferred_element_type=jnp.float32,
@@ -522,11 +524,19 @@
         [pltpu.VMEM((2, 2, 4, 2, 8, LANES), jnp.float32), pltpu.SemaphoreType.DMA((3,))],
         54600,
     )
-    pay_a, pay_b, positions = call(
+    pay_a, pay_b, small = call(
         functools.partial(edges_kernel, sizes),
-        [first_a, first_b, cell_of.reshape(2, LANES), cell_slot.reshape(-1, LANES), z_flags],
-        VMEM,
-        [x_shape, x_shape, (8, LANES)],
+        [
+            first_a,
+            first_b,
+            cell_of.reshape(2, LANES),
+            cell_slot.reshape(-1, LANES),
+            wall_flags_xaxis,
+            z_flags,
+            coarse_logk.reshape(1, -1),
+        ],
+        VMEM,
+        [x_shape, x_shape, (2, 8, LANES)],
         VMEM,
         [],
         16 * 1024,
@@ -535,11 +545,11 @@
     pairs_a = both_ways([(i, i + 1) for i in range(0, nx - 1, 2)])
     got_a = lax.ppermute(pay_a, "gx", pairs_a)
     got_b = lax.ppermute(pay_b, "gx", pairs_b)
-    small, local, *z_pay = call(
+    local, sums, *z_pay = call(
         functools.partial(local_kernel, sizes),
-        [held, positions, target6, wall_flags_xaxis, z_flags, coarse_logk.reshape(1, -1)],
-        VMEM,
-        [(3, 8, LANES), shape] + [z_shape] * count,
+        [held, small, target6],
+        VMEM,
+        [shape, (4, LANES)] + [z_shape] * count,
         VMEM,
         [],
         16 * 1024,
@@ -547,7 +557,7 @@
     z_got = along_z(z_pay, nz)
     whole, send, *w_pay = call(
         functools.partial(sums_kernel, sizes, length),
-        [held, small, local, got_a, got_b] + z_got,
+        [held, small, local, sums, got_a, got_b] + z_got,
         VMEM,
         [shape, (nx * nz, LANES)] + [w_shape] * count,
         VMEM,

time: 26.3 us -> 26.3 us (level)
  waiting for transfers between devices: 1.49 us -> 2.15 us
  local copies, waits for them, and re-layouts: 0.65 us -> 0.03 us
    ppermute x1, waiting for transfers between devices: 0.29 us -> 0.95 us  [shards(): got_a = lax.ppermute(pay_a, 'gx', pairs_a)]
    unnamed x12, local copies, waits for them, and re-layouts: 0.65 us -> 0.03 us
where the time goes in v5:
time: 26.3 us; the launch traced here: 26.1 us
  blocking collectives  16.4 us (62%)
  starting transfers between devices  3.8 us (14%)
  Pallas kernels  3.03 us (12%)
  waiting for transfers between devices  2.15 us (8%)
  between operations  0.78 us (3%)
    all_to_all x1, blocking collectives, shards(): received = lax.all_to_all(send, ('gx', 'gz'), 0, 0, tiled=True)  16.4 us
    pallas_call x5, Pallas kernels, call(): pl.pallas_call(kernel, out_shape=[jax.ShapeDtypeStruct(shape, jnp.float32...  3.03 us
    ppermute x1, starting transfers between devices, shards(): got_a = lax.ppermute(pay_a, 'gx', pairs_a)  3 us
    ppermute x2, waiting for transfers between devices, along_z(): return [lax.ppermute(payloads[0], 'gz', [(0, 1), (1, 0)])]  1.2 us
    ppermute x1, waiting for transfers between devices, shards(): got_a = lax.ppermute(pay_a, 'gx', pairs_a)  0.95 us
    ppermute x1, starting transfers between devices, shards(): got_b = lax.ppermute(pay_b, 'gx', pairs_b)  0.66 us
  transfers between devices with their start and end apart: 4, of which 2 were waited for; matrix products, arithmetic and copies ran while one was open for 0% of the time, Pallas kernels for 1%

profile of v5, /device:TPU:0, one launch (start us, length us, event | category | flops | bytes accessed | tf_op | source)
XLA Modules:
  0.0 26.1 jit_solution(16104044757613428406)
XLA Ops:
  0.6 0.0 copy-start.1
  0.6 0.0 copy-start.2
  0.7 0.0 copy-start.3
  0.7 0.0 copy-start.4
  0.7 0.0 copy-start.5
  0.7 1.1 %shard_map.86 = (f32[2,4,4,2,8,128]{5,4,3,2,1,0:T(8,128)S(1)}, f32[29,8,128]{2,1,0:T(8,128)S(1)}, f32[29,8,128]{2,1,0:T(8,128)S(1)}) custom-call(f32[2,4,4,2,8,128]{5,4,3,2,1,0:T(8,128)} %bitcast.20, f32[2,4,4,2,8,128]{5,4,3,2,1,0:T(8,128)} %bitcast.12), custom_call_target="tpu_custom_call" | custom-call | flops 2000000 | bytes 800000 | tf_op jit(solution)/shard_map/pallas_call | solution.py:487
  1.8 0.0 copy-start
  1.9 0.0 copy-done.1
  1.9 0.0 copy-done.2
  1.9 0.0 copy-done.3
  1.9 0.0 copy-done.4
  1.9 0.0 copy-done.5
  1.9 3.0 %collective-permute-start = (f32[29,8,128]{2,1,0:T(8,128)S(1)}, f32[29,8,128]{2,1,0:T(8,128)S(1)}, u32[]{:S(2)}, u32[]{:S(2)}) collective-permute-start(f32[29,8,128]{2,1,0:T(8,128)S(1)} %get-tuple-element.22), channel_id=1, source_target_pairs={{0,2},{4,6},{8,10},{12,14},{16,18},{20,22},{24,26},{28,30},{2,0},{... | collective-permute-start | bytes 356360 | tf_op jit(solution)/shard_map/ppermute | solution.py:546
  4.9 0.7 %collective-permute-start.1 = (f32[29,8,128]{2,1,0:T(8,128)S(1)}, f32[29,8,128]{2,1,0:T(8,128)S(1)}, u32[]{:S(2)}, u32[]{:S(2)}) collective-permute-start(f32[29,8,128]{2,1,0:T(8,128)S(1)} %get-tuple-element.23), channel_id=1, source_target_pairs={{2,4},{6,8},{10,12},{14,16},{18,20},{22,24},{26,28},{4,2},{8,6},{1... | collective-permute-start | bytes 356360 | tf_op jit(solution)/shard_map/ppermute | solution.py:547
  5.6 0.0 copy-done
  5.6 0.3 %shard_map.88 = (f32[2,4,4,2,8,128]{5,4,3,2,1,0:T(8,128)S(1)}, f32[4,128]{1,0:T(4,128)S(1)}, f32[9,8,128]{2,1,0:T(8,128)S(1)}) custom-call(f32[2,4,4,2,8,128]{5,4,3,2,1,0:T(8,128)S(1)} %get-tuple-element.16.state, f32[2,8,128]{2,1,0:T(8,128)S(1)} %get-tuple-element.19.small, f32[2,4,4,2,8,128]{5,4,3,2,1,0:T(8,128)S(1)} %bitcast.13), custom_call_target="tpu_custom_call" | custom-call | flops 2000000 | bytes 800000 | tf_op jit(solution)/shard_map/pallas_call | solution.py:487
  6.0 0.1 collective-permute-start.2
  6.0 1.2 %collective-permute-done.2.refs_0_ = f32[9,8,128]{2,1,0:T(8,128)S(1)} collective-permute-done((f32[9,8,128]{2,1,0:T(8,128)S(1)}, f32[9,8,128]{2,1,0:T(8,128)S(1)}, u32[]{:S(2)}, u32[]{:S(2)}) %collective-permute-start.2) | collective-permute-done | bytes 36896 | tf_op jit(solution)/shard_map/ppermute | solution.py:504
  7.2 0.9 %collective-permute-done.got_a = f32[29,8,128]{2,1,0:T(8,128)S(1)} collective-permute-done((f32[29,8,128]{2,1,0:T(8,128)S(1)}, f32[29,8,128]{2,1,0:T(8,128)S(1)}, u32[]{:S(2)}, u32[]{:S(2)}) %collective-permute-start) | collective-permute-done | bytes 118816 | tf_op jit(solution)/shard_map/ppermute | solution.py:546
  8.2 0.0 collective-permute-done.1.got_b
  8.2 0.3 %shard_map.89 = (f32[2,4,4,2,8,128]{5,4,3,2,1,0:T(8,128)S(1)}, f32[32,128]{1,0:T(8,128)S(1)}, f32[12,8,128]{2,1,0:T(8,128)S(1)}) custom-call(f32[2,4,4,2,8,128]{5,4,3,2,1,0:T(8,128)S(1)} %get-tuple-element.16.state, f32[2,8,128]{2,1,0:T(8,128)S(1)} %get-tuple-element.19.small, f32[2,4,4,2,8,128]{5,4,3,2,1,0:T(8,128)S(1)} %get-tuple-element.20.local, ...), custom_call_target="tpu_custom_call" | custom-call | flops 2000000 | bytes 800000 | tf_op jit(solution)/shard_map/pallas_call | solution.py:487
  8.5 0.1 collective-permute-start.3
  8.6 16.4 %all_to_all.11 = f32[32,1,128]{2,1,0:T(1,128)S(1)} all-to-all(f32[32,1,128]{2,1,0:T(1,128)S(1)} %bitcast.15), channel_id=1, replica_groups=mesh['gx'=16,'gz'=2] {'gx','gz'}, dimensions={0} | all-to-all | bytes 32768 | tf_op jit(solution)/shard_map/all_to_all | solution.py:568
  24.9 0.0 collective-permute-done.3.refs_1_
  24.9 1.2 %shard_map.90 = (f32[2,4,4,2,8,128]{5,4,3,2,1,0:T(8,128)}, f32[1,32]{1,0:T(1,128)}) custom-call(f32[2,4,4,2,8,128]{5,4,3,2,1,0:T(8,128)S(1)} %get-tuple-element.16.state, f32[2,8,128]{2,1,0:T(8,128)S(1)} %get-tuple-element.19.small, f32[2,4,4,2,8,128]{5,4,3,2,1,0:T(8,128)S(1)} %get-tuple-element.25.whole, f32[29,8,128]{2,1,0:T(8,128)S(1)} %collective-permute-done.got_a, ...), custom_call_target="tpu_custom_call" | custom-call | flops 2000000 | bytes 800000 | tf_op jit(solution)/shard_map/pallas_call | solution.py:487
  (1 shorter events, 0.0 us)
Async XLA Ops:
  0.6 1.2 %copy-start.1 = (s32[1024]{0:T(1024)S(1)}, s32[1024]{0:T(1024)}, u32[]{:S(2)}) copy-start(s32[1024]{0:T(1024)} %param.10) | copy-start | bytes 12292
  0.6 1.2 %copy-start.2 = (s32[2,2,128]{2,1,0:T(2,128)S(1)}, s32[2,2,128]{2,1,0:T(2,128)}, u32[]{:S(2)}) copy-start(s32[2,2,128]{2,1,0:T(2,128)} %x_wall.1) | copy-start | bytes 6148
  0.7 1.2 %copy-start.3 = (s32[1,2,128]{2,1,0:T(2,128)S(1)}, s32[1,2,128]{2,1,0:T(2,128)}, u32[]{:S(2)}) copy-start(s32[1,2,128]{2,1,0:T(2,128)} %param.11) | copy-start | bytes 3076
  0.7 1.2 %copy-start.4 = (s32[2,1,128]{2,1,0:T(1,128)S(1)}, s32[2,1,128]{2,1,0:T(1,128)}, u32[]{:S(2)}) copy-start(s32[2,1,128]{2,1,0:T(1,128)} %param.13) | copy-start | bytes 3076
  0.7 1.2 %copy-start.5 = (f32[32]{0:T(128)S(1)}, f32[32]{0:T(128)}, u32[]{:S(2)}) copy-start(f32[32]{0:T(128)} %param.9) | copy-start | bytes 388
  1.8 3.8 %copy-start = (f32[1,2,4,64,128]{4,3,2,1,0:T(8,128)S(1)}, f32[1,2,4,64,128]{4,3,2,1,0:T(8,128)}, u32[]{:S(2)}) copy-start(f32[1,2,4,64,128]{4,3,2,1,0:T(8,128)} %param.8) | copy-start | bytes 786436
  1.9 6.2 %collective-permute-start = (f32[29,8,128]{2,1,0:T(8,128)S(1)}, f32[29,8,128]{2,1,0:T(8,128)S(1)}, u32[]{:S(2)}, u32[]{:S(2)}) collective-permute-start(f32[29,8,128]{2,1,0:T(8,128)S(1)} %get-tuple-element.22), channel_id=1, source_target_pairs={{0,2},{4,6},{8,10},{12,14},{16,18},{20,22},{24,26},{28,30},{2,0},{... | collective-permute-start | bytes 356360 | tf_op jit(solution)/shard_map/ppermute | solution.py:546
  4.9 3.2 %collective-permute-start.1 = (f32[29,8,128]{2,1,0:T(8,128)S(1)}, f32[29,8,128]{2,1,0:T(8,128)S(1)}, u32[]{:S(2)}, u32[]{:S(2)}) collective-permute-start(f32[29,8,128]{2,1,0:T(8,128)S(1)} %get-tuple-element.23), channel_id=1, source_target_pairs={{2,4},{6,8},{10,12},{14,16},{18,20},{22,24},{26,28},{4,2},{8,6},{1... | collective-permute-start | bytes 356360 | tf_op jit(solution)/shard_map/ppermute | solution.py:547
  6.0 1.3 %collective-permute-start.2 = (f32[9,8,128]{2,1,0:T(8,128)S(1)}, f32[9,8,128]{2,1,0:T(8,128)S(1)}, u32[]{:S(2)}, u32[]{:S(2)}) collective-permute-start(f32[9,8,128]{2,1,0:T(8,128)S(1)} %get-tuple-element.24), channel_id=1, source_target_pairs={{0,1},{1,0},{2,3},{3,2},{4,5},{5,4},{6,7},{7,6},{8,9},{9,8},{10,11... | collective-permute-start | bytes 110600 | tf_op jit(solution)/shard_map/ppermute | solution.py:504
  8.5 16.4 %collective-permute-start.3 = (f32[12,8,128]{2,1,0:T(8,128)S(1)}, f32[12,8,128]{2,1,0:T(8,128)S(1)}, u32[]{:S(2)}, u32[]{:S(2)}) collective-permute-start(f32[12,8,128]{2,1,0:T(8,128)S(1)} %get-tuple-element.27), channel_id=1, source_target_pairs={{0,1},{1,0},{2,3},{3,2},{4,5},{5,4},{6,7},{7,6},{8,9},{9,8},{10,11... | collective-permute-start | bytes 147464 | tf_op jit(solution)/shard_map/ppermute | solution.py:504

commit v6 on v4

--- a/solution.py
+++ b/solution.py
@@ -345,10 +345,12 @@
         value = jnp.where(
             place == position + length, first, jnp.where(place == position + 2 * length, second, 0.0)
         )
-        piece = value.astype(jnp.bfloat16)
-        values += [piece, (value - piece.astype(jnp.float32)).astype(jnp.bfloat16)]
+        for _ in range(3):
+            piece = value.astype(jnp.bfloat16)
+            values.append(piece)
+            value = value - piece.astype(jnp.float32)
     send[...] = lax.dot_general(
-        jnp.concatenate([chosen[0], chosen[0], chosen[1], chosen[1]], axis=1),
+        jnp.concatenate([chosen[0]] * 3 + [chosen[1]] * 3, axis=1),
         jnp.concatenate(values, axis=1),
         (((1,), (1,)), ((), ())),
         preferred_element_type=jnp.float32,

time: 26.3 us -> 26.3 us (level)
  no operation moved by 1% of the time
where the time goes in v6:
time: 26.3 us; the launch traced here: 26.1 us
  blocking collectives  16.4 us (62%)
  starting transfers between devices  3.8 us (14%)
  Pallas kernels  3.03 us (12%)
  waiting for transfers between devices  1.49 us (6%)
  between operations  0.77 us (3%)
  local copies, waits for them, and re-layouts  0.65 us (2%)
    all_to_all x1, blocking collectives, shards(): received = lax.all_to_all(send, ('gx', 'gz'), 0, 0, tiled=True)  16.4 us
    pallas_call x5, Pallas kernels, call(): pl.pallas_call(kernel, out_shape=[jax.ShapeDtypeStruct(shape, jnp.float32...  3.03 us
    ppermute x1, starting transfers between devices, shards(): got_a = lax.ppermute(pay_a, 'gx', pairs_a)  3 us
    ppermute x2, waiting for transfers between devices, along_z(): return [lax.ppermute(payloads[0], 'gz', [(0, 1), (1, 0)])]  1.2 us
    ppermute x1, starting transfers between devices, shards(): got_b = lax.ppermute(pay_b, 'gx', pairs_b)  0.66 us
    unnamed x12, local copies, waits for them, and re-layouts  0.65 us
  transfers between devices with their start and end apart: 4, of which 2 were waited for; matrix products, arithmetic and copies ran while one was open for 0% of the time, Pallas kernels for 1%

profile of v6, /device:TPU:0, one launch (start us, length us, event | category | flops | bytes accessed | tf_op | source)
XLA Modules:
  0.0 26.1 jit_solution(2140153457449548037)
XLA Ops:
  0.6 0.0 copy-start.1
  0.6 0.0 copy-start.2
  0.7 0.0 copy-start.4
  0.7 0.0 copy-start.3
  0.7 1.1 %shard_map.86 = (f32[2,4,4,2,8,128]{5,4,3,2,1,0:T(8,128)S(1)}, f32[29,8,128]{2,1,0:T(8,128)S(1)}, f32[29,8,128]{2,1,0:T(8,128)S(1)}) custom-call(f32[2,4,4,2,8,128]{5,4,3,2,1,0:T(8,128)} %bitcast.21, f32[2,4,4,2,8,128]{5,4,3,2,1,0:T(8,128)} %bitcast.12), custom_call_target="tpu_custom_call" | custom-call | flops 2000000 | bytes 800000 | tf_op jit(solution)/shard_map/pallas_call | solution.py:487
  1.8 0.0 copy-start
  1.8 0.0 copy-done.1
  1.8 0.0 copy-done.2
  1.9 0.0 copy-done.4
  1.9 3.0 %collective-permute-start = (f32[29,8,128]{2,1,0:T(8,128)S(1)}, f32[29,8,128]{2,1,0:T(8,128)S(1)}, u32[]{:S(2)}, u32[]{:S(2)}) collective-permute-start(f32[29,8,128]{2,1,0:T(8,128)S(1)} %get-tuple-element.22), channel_id=1, source_target_pairs={{0,2},{4,6},{8,10},{12,14},{16,18},{20,22},{24,26},{28,30},{2,0},{... | collective-permute-start | bytes 356360 | tf_op jit(solution)/shard_map/ppermute | solution.py:538
  4.9 0.7 %collective-permute-start.1 = (f32[29,8,128]{2,1,0:T(8,128)S(1)}, f32[29,8,128]{2,1,0:T(8,128)S(1)}, u32[]{:S(2)}, u32[]{:S(2)}) collective-permute-start(f32[29,8,128]{2,1,0:T(8,128)S(1)} %get-tuple-element.23), channel_id=1, source_target_pairs={{2,4},{6,8},{10,12},{14,16},{18,20},{22,24},{26,28},{4,2},{8,6},{1... | collective-permute-start | bytes 356360 | tf_op jit(solution)/shard_map/ppermute | solution.py:539
  5.6 0.0 copy-start.5
  5.6 0.0 copy-done.3
  5.6 0.0 copy-done
  5.6 0.6 %copy-done.5 = f32[32]{0:T(128)S(1)} copy-done((f32[32]{0:T(128)S(1)}, f32[32]{0:T(128)}, u32[]{:S(2)}) %copy-start.5) | copy-done | bytes 152
  6.2 0.3 %shard_map.88 = (f32[3,8,128]{2,1,0:T(8,128)S(1)}, f32[2,4,4,2,8,128]{5,4,3,2,1,0:T(8,128)S(1)}, f32[9,8,128]{2,1,0:T(8,128)S(1)}) custom-call(f32[2,4,4,2,8,128]{5,4,3,2,1,0:T(8,128)S(1)} %get-tuple-element.16.state, f32[8,128]{1,0:T(8,128)S(1)} %get-tuple-element.19.positions, f32[2,4,4,2,8,128]{5,4,3,2,1,0:T(8,128)S(1)} %bitcast.13, ...), custom_call_target="tpu_custom_call" | custom-call | flops 2000000 | bytes 800000 | tf_op jit(solution)/shard_map/pallas_call | solution.py:487
  6.6 0.1 collective-permute-start.2
  6.7 1.2 %collective-permute-done.2.refs_0_ = f32[9,8,128]{2,1,0:T(8,128)S(1)} collective-permute-done((f32[9,8,128]{2,1,0:T(8,128)S(1)}, f32[9,8,128]{2,1,0:T(8,128)S(1)}, u32[]{:S(2)}, u32[]{:S(2)}) %collective-permute-start.2) | collective-permute-done | bytes 36896 | tf_op jit(solution)/shard_map/ppermute | solution.py:504
  7.9 0.3 %collective-permute-done.got_a = f32[29,8,128]{2,1,0:T(8,128)S(1)} collective-permute-done((f32[29,8,128]{2,1,0:T(8,128)S(1)}, f32[29,8,128]{2,1,0:T(8,128)S(1)}, u32[]{:S(2)}, u32[]{:S(2)}) %collective-permute-start) | collective-permute-done | bytes 118816 | tf_op jit(solution)/shard_map/ppermute | solution.py:538
  8.1 0.0 collective-permute-done.1.got_b
  8.1 0.3 %shard_map.89 = (f32[2,4,4,2,8,128]{5,4,3,2,1,0:T(8,128)S(1)}, f32[32,128]{1,0:T(8,128)S(1)}, f32[12,8,128]{2,1,0:T(8,128)S(1)}) custom-call(f32[2,4,4,2,8,128]{5,4,3,2,1,0:T(8,128)S(1)} %get-tuple-element.16.state, f32[3,8,128]{2,1,0:T(8,128)S(1)} %get-tuple-element.20.small, f32[2,4,4,2,8,128]{5,4,3,2,1,0:T(8,128)S(1)} %get-tuple-element.21.local, ...), custom_call_target="tpu_custom_call" | custom-call | flops 2000000 | bytes 800000 | tf_op jit(solution)/shard_map/pallas_call | solution.py:487
  8.4 0.1 collective-permute-start.3
  8.5 16.4 %all_to_all.11 = f32[32,1,128]{2,1,0:T(1,128)S(1)} all-to-all(f32[32,1,128]{2,1,0:T(1,128)S(1)} %bitcast.15), channel_id=1, replica_groups=mesh['gx'=16,'gz'=2] {'gx','gz'}, dimensions={0} | all-to-all | bytes 32768 | tf_op jit(solution)/shard_map/all_to_all | solution.py:560
  24.9 0.0 collective-permute-done.3.refs_1_
  24.9 1.2 %shard_map.90 = (f32[2,4,4,2,8,128]{5,4,3,2,1,0:T(8,128)}, f32[1,32]{1,0:T(1,128)}) custom-call(f32[2,4,4,2,8,128]{5,4,3,2,1,0:T(8,128)S(1)} %get-tuple-element.16.state, f32[3,8,128]{2,1,0:T(8,128)S(1)} %get-tuple-element.20.small, f32[2,4,4,2,8,128]{5,4,3,2,1,0:T(8,128)S(1)} %get-tuple-element.25.whole, f32[29,8,128]{2,1,0:T(8,128)S(1)} %collective-permute-done.got_a, ...), custom_call_target="tpu_custom_call" | custom-call | flops 2000000 | bytes 800000 | tf_op jit(solution)/shard_map/pallas_call | solution.py:487
  (1 shorter events, 0.0 us)
Async XLA Ops:
  0.6 1.2 %copy-start.1 = (s32[1024]{0:T(1024)S(1)}, s32[1024]{0:T(1024)}, u32[]{:S(2)}) copy-start(s32[1024]{0:T(1024)} %param.10) | copy-start | bytes 12292
  0.6 1.2 %copy-start.2 = (s32[2,1,128]{2,1,0:T(1,128)S(1)}, s32[2,1,128]{2,1,0:T(1,128)}, u32[]{:S(2)}) copy-start(s32[2,1,128]{2,1,0:T(1,128)} %param.13) | copy-start | bytes 3076
  0.7 1.2 %copy-start.4 = (s32[1,2,128]{2,1,0:T(2,128)S(1)}, s32[1,2,128]{2,1,0:T(2,128)}, u32[]{:S(2)}) copy-start(s32[1,2,128]{2,1,0:T(2,128)} %param.11) | copy-start | bytes 3076
  0.7 4.9 %copy-start.3 = (s32[2,2,128]{2,1,0:T(2,128)S(1)}, s32[2,2,128]{2,1,0:T(2,128)}, u32[]{:S(2)}) copy-start(s32[2,2,128]{2,1,0:T(2,128)} %x_wall.1) | copy-start | bytes 6148
  1.8 3.8 %copy-start = (f32[1,2,4,64,128]{4,3,2,1,0:T(8,128)S(1)}, f32[1,2,4,64,128]{4,3,2,1,0:T(8,128)}, u32[]{:S(2)}) copy-start(f32[1,2,4,64,128]{4,3,2,1,0:T(8,128)} %param.8) | copy-start | bytes 786436
  1.9 6.2 %collective-permute-start = (f32[29,8,128]{2,1,0:T(8,128)S(1)}, f32[29,8,128]{2,1,0:T(8,128)S(1)}, u32[]{:S(2)}, u32[]{:S(2)}) collective-permute-start(f32[29,8,128]{2,1,0:T(8,128)S(1)} %get-tuple-element.22), channel_id=1, source_target_pairs={{0,2},{4,6},{8,10},{12,14},{16,18},{20,22},{24,26},{28,30},{2,0},{... | collective-permute-start | bytes 356360 | tf_op jit(solution)/shard_map/ppermute | solution.py:538
  4.9 3.2 %collective-permute-start.1 = (f32[29,8,128]{2,1,0:T(8,128)S(1)}, f32[29,8,128]{2,1,0:T(8,128)S(1)}, u32[]{:S(2)}, u32[]{:S(2)}) collective-permute-start(f32[29,8,128]{2,1,0:T(8,128)S(1)} %get-tuple-element.23), channel_id=1, source_target_pairs={{2,4},{6,8},{10,12},{14,16},{18,20},{22,24},{26,28},{4,2},{8,6},{1... | collective-permute-start | bytes 356360 | tf_op jit(solution)/shard_map/ppermute | solution.py:539
  5.6 0.7 %copy-start.5 = (f32[32]{0:T(128)S(1)}, f32[32]{0:T(128)}, u32[]{:S(2)}) copy-start(f32[32]{0:T(128)} %param.9) | copy-start | bytes 388
  6.6 1.3 %collective-permute-start.2 = (f32[9,8,128]{2,1,0:T(8,128)S(1)}, f32[9,8,128]{2,1,0:T(8,128)S(1)}, u32[]{:S(2)}, u32[]{:S(2)}) collective-permute-start(f32[9,8,128]{2,1,0:T(8,128)S(1)} %get-tuple-element.24), channel_id=1, source_target_pairs={{0,1},{1,0},{2,3},{3,2},{4,5},{5,4},{6,7},{7,6},{8,9},{9,8},{10,11... | collective-permute-start | bytes 110600 | tf_op jit(solution)/shard_map/ppermute | solution.py:504
  8.4 16.4 %collective-permute-start.3 = (f32[12,8,128]{2,1,0:T(8,128)S(1)}, f32[12,8,128]{2,1,0:T(8,128)S(1)}, u32[]{:S(2)}, u32[]{:S(2)}) collective-permute-start(f32[12,8,128]{2,1,0:T(8,128)S(1)} %get-tuple-element.27), channel_id=1, source_target_pairs={{0,1},{1,0},{2,3},{3,2},{4,5},{5,4},{6,7},{7,6},{8,9},{9,8},{10,11... | collective-permute-start | bytes 147464 | tf_op jit(solution)/shard_map/ppermute | solution.py:504

commit v7 on v6

--- a/solution.py
+++ b/solution.py
@@ -335,26 +335,29 @@
         sums.append((local_sum + jnp.sum(total, axis=0)[None], small[SUMS, 2 + z : 3 + z, :]))
     devices = send.shape[0]
     slots = small[0].astype(jnp.int32)
-    place = lax.broadcasted_iota(jnp.int32, (LANES, LANES), 0)
-    owner = lax.broadcasted_iota(jnp.int32, (devices, LANES), 0)
-    chosen, values = [], []
-    for z, (first, second) in enumerate(sums):
-        slot = slots[z : z + 1, :]
-        chosen.append(jnp.where(owner == slot // length, 1.0, 0.0).astype(jnp.bfloat16))
-        position = slot % length
-        value = jnp.where(
-            place == position + length, first, jnp.where(place == position + 2 * length, second, 0.0)
-        )
+    elements = 2 * LANES
+    slot = jnp.concatenate([slots[0:1, :], slots[1:2, :]], axis=1)
+    owner = lax.broadcasted_iota(jnp.int32, (devices, elements), 0)
+    place = lax.broadcasted_iota(jnp.int32, (LANES, elements), 0) % length
+    chosen = owner == slot // length
+    position = jnp.where(place == slot % length, 1.0, 0.0).astype(jnp.bfloat16)
+    pieces = []
+    for parts in zip(*sums):
+        value = jnp.where(chosen, jnp.concatenate(parts, axis=1), 0.0)
         for _ in range(3):
             piece = value.astype(jnp.bfloat16)
-            values.append(piece)
+            pieces.append(piece)
             value = value - piece.astype(jnp.float32)
-    send[...] = lax.dot_general(
-        jnp.concatenate([chosen[0]] * 3 + [chosen[1]] * 3, axis=1),
-        jnp.concatenate(values, axis=1),
+    placed = lax.dot_general(
+        jnp.concatenate(pieces, axis=0),
+        position,
         (((1,), (1,)), ((), ())),
         preferred_element_type=jnp.float32,
     )
+    parts = [placed[i * devices : (i + 1) * devices] for i in range(6)]
+    lane = lax.broadcasted_iota(jnp.int32, (devices, LANES), 1)
+    first, second = parts[0] + parts[1] + parts[2], parts[3] + parts[4] + parts[5]
+    send[...] = jnp.where(lane < 2 * length, first, second)
     logk = small[1, LOGK : LOGK + 1, 0:length]
     send[:, 0:length] = jnp.broadcast_to(logk, (devices, length))
     faces = [packed_face(rows, load(whole, z), 2 * z - 1) for z in range(2)]

time: 26.3 us -> 26.2 us (level)
  no operation moved by 1% of the time
where the time goes in v7:
time: 26.2 us; the launch traced here: 26 us
  blocking collectives  16.4 us (63%)
  starting transfers between devices  3.75 us (14%)
  Pallas kernels  3.01 us (11%)
  waiting for transfers between devices  1.49 us (6%)
  between operations  0.76 us (3%)
  local copies, waits for them, and re-layouts  0.65 us (2%)
    all_to_all x1, blocking collectives, shards(): received = lax.all_to_all(send, ('gx', 'gz'), 0, 0, tiled=True)  16.4 us
    pallas_call x5, Pallas kernels, call(): pl.pallas_call(kernel, out_shape=[jax.ShapeDtypeStruct(shape, jnp.float32...  3.01 us
    ppermute x1, starting transfers between devices, shards(): got_a = lax.ppermute(pay_a, 'gx', pairs_a)  3 us
    ppermute x2, waiting for transfers between devices, along_z(): return [lax.ppermute(payloads[0], 'gz', [(0, 1), (1, 0)])]  1.2 us
    ppermute x1, starting transfers between devices, shards(): got_b = lax.ppermute(pay_b, 'gx', pairs_b)  0.66 us
    unnamed x12, local copies, waits for them, and re-layouts  0.65 us
  transfers between devices with their start and end apart: 4, of which 2 were waited for; matrix products, arithmetic and copies ran while one was open for 0% of the time, Pallas kernels for 1%

profile of v7, /device:TPU:0, one launch (start us, length us, event | category | flops | bytes accessed | tf_op | source)
XLA Modules:
  0.0 26.0 jit_solution(8285439597196255888)
XLA Ops:
  0.6 0.0 copy-start.1
  0.6 0.0 copy-start.2
  0.7 0.0 copy-start.4
  0.7 0.0 copy-start.3
  0.7 1.1 %shard_map.86 = (f32[2,4,4,2,8,128]{5,4,3,2,1,0:T(8,128)S(1)}, f32[29,8,128]{2,1,0:T(8,128)S(1)}, f32[29,8,128]{2,1,0:T(8,128)S(1)}) custom-call(f32[2,4,4,2,8,128]{5,4,3,2,1,0:T(8,128)} %bitcast.21, f32[2,4,4,2,8,128]{5,4,3,2,1,0:T(8,128)} %bitcast.12), custom_call_target="tpu_custom_call" | custom-call | flops 2000000 | bytes 800000 | tf_op jit(solution)/shard_map/pallas_call | solution.py:490
  1.8 0.0 copy-start
  1.8 0.0 copy-done.1
  1.8 0.0 copy-done.2
  1.9 0.0 copy-done.4
  1.9 3.0 %collective-permute-start = (f32[29,8,128]{2,1,0:T(8,128)S(1)}, f32[29,8,128]{2,1,0:T(8,128)S(1)}, u32[]{:S(2)}, u32[]{:S(2)}) collective-permute-start(f32[29,8,128]{2,1,0:T(8,128)S(1)} %get-tuple-element.22), channel_id=1, source_target_pairs={{0,2},{4,6},{8,10},{12,14},{16,18},{20,22},{24,26},{28,30},{2,0},{... | collective-permute-start | bytes 356360 | tf_op jit(solution)/shard_map/ppermute | solution.py:541
  4.9 0.7 %collective-permute-start.1 = (f32[29,8,128]{2,1,0:T(8,128)S(1)}, f32[29,8,128]{2,1,0:T(8,128)S(1)}, u32[]{:S(2)}, u32[]{:S(2)}) collective-permute-start(f32[29,8,128]{2,1,0:T(8,128)S(1)} %get-tuple-element.23), channel_id=1, source_target_pairs={{2,4},{6,8},{10,12},{14,16},{18,20},{22,24},{26,28},{4,2},{8,6},{1... | collective-permute-start | bytes 356360 | tf_op jit(solution)/shard_map/ppermute | solution.py:542
  5.6 0.0 copy-start.5
  5.6 0.0 copy-done.3
  5.6 0.0 copy-done
  5.6 0.6 %copy-done.5 = f32[32]{0:T(128)S(1)} copy-done((f32[32]{0:T(128)S(1)}, f32[32]{0:T(128)}, u32[]{:S(2)}) %copy-start.5) | copy-done | bytes 152
  6.2 0.3 %shard_map.88 = (f32[3,8,128]{2,1,0:T(8,128)S(1)}, f32[2,4,4,2,8,128]{5,4,3,2,1,0:T(8,128)S(1)}, f32[9,8,128]{2,1,0:T(8,128)S(1)}) custom-call(f32[2,4,4,2,8,128]{5,4,3,2,1,0:T(8,128)S(1)} %get-tuple-element.16.state, f32[8,128]{1,0:T(8,128)S(1)} %get-tuple-element.19.positions, f32[2,4,4,2,8,128]{5,4,3,2,1,0:T(8,128)S(1)} %bitcast.13, ...), custom_call_target="tpu_custom_call" | custom-call | flops 2000000 | bytes 800000 | tf_op jit(solution)/shard_map/pallas_call | solution.py:490
  6.6 0.1 collective-permute-start.2
  6.7 1.2 %collective-permute-done.2.refs_0_ = f32[9,8,128]{2,1,0:T(8,128)S(1)} collective-permute-done((f32[9,8,128]{2,1,0:T(8,128)S(1)}, f32[9,8,128]{2,1,0:T(8,128)S(1)}, u32[]{:S(2)}, u32[]{:S(2)}) %collective-permute-start.2) | collective-permute-done | bytes 36896 | tf_op jit(solution)/shard_map/ppermute | solution.py:507
  7.9 0.3 %collective-permute-done.got_a = f32[29,8,128]{2,1,0:T(8,128)S(1)} collective-permute-done((f32[29,8,128]{2,1,0:T(8,128)S(1)}, f32[29,8,128]{2,1,0:T(8,128)S(1)}, u32[]{:S(2)}, u32[]{:S(2)}) %collective-permute-start) | collective-permute-done | bytes 118816 | tf_op jit(solution)/shard_map/ppermute | solution.py:541
  8.1 0.0 collective-permute-done.1.got_b
  8.1 0.3 %shard_map.89 = (f32[2,4,4,2,8,128]{5,4,3,2,1,0:T(8,128)S(1)}, f32[32,128]{1,0:T(8,128)S(1)}, f32[12,8,128]{2,1,0:T(8,128)S(1)}) custom-call(f32[2,4,4,2,8,128]{5,4,3,2,1,0:T(8,128)S(1)} %get-tuple-element.16.state, f32[3,8,128]{2,1,0:T(8,128)S(1)} %get-tuple-element.20.small, f32[2,4,4,2,8,128]{5,4,3,2,1,0:T(8,128)S(1)} %get-tuple-element.21.local, ...), custom_call_target="tpu_custom_call" | custom-call | flops 2000000 | bytes 800000 | tf_op jit(solution)/shard_map/pallas_call | solution.py:490
  8.4 0.0 collective-permute-start.3
  8.4 16.4 %all_to_all.11 = f32[32,1,128]{2,1,0:T(1,128)S(1)} all-to-all(f32[32,1,128]{2,1,0:T(1,128)S(1)} %bitcast.15), channel_id=1, replica_groups=mesh['gx'=16,'gz'=2] {'gx','gz'}, dimensions={0} | all-to-all | bytes 32768 | tf_op jit(solution)/shard_map/all_to_all | solution.py:563
  24.8 0.0 collective-permute-done.3.refs_1_
  24.8 1.2 %shard_map.90 = (f32[2,4,4,2,8,128]{5,4,3,2,1,0:T(8,128)}, f32[1,32]{1,0:T(1,128)}) custom-call(f32[2,4,4,2,8,128]{5,4,3,2,1,0:T(8,128)S(1)} %get-tuple-element.16.state, f32[3,8,128]{2,1,0:T(8,128)S(1)} %get-tuple-element.20.small, f32[2,4,4,2,8,128]{5,4,3,2,1,0:T(8,128)S(1)} %get-tuple-element.25.whole, f32[29,8,128]{2,1,0:T(8,128)S(1)} %collective-permute-done.got_a, ...), custom_call_target="tpu_custom_call" | custom-call | flops 2000000 | bytes 800000 | tf_op jit(solution)/shard_map/pallas_call | solution.py:490
  (1 shorter events, 0.0 us)
Async XLA Ops:
  0.6 1.2 %copy-start.1 = (s32[1024]{0:T(1024)S(1)}, s32[1024]{0:T(1024)}, u32[]{:S(2)}) copy-start(s32[1024]{0:T(1024)} %param.10) | copy-start | bytes 12292
  0.6 1.2 %copy-start.2 = (s32[2,1,128]{2,1,0:T(1,128)S(1)}, s32[2,1,128]{2,1,0:T(1,128)}, u32[]{:S(2)}) copy-start(s32[2,1,128]{2,1,0:T(1,128)} %param.13) | copy-start | bytes 3076
  0.7 1.2 %copy-start.4 = (s32[1,2,128]{2,1,0:T(2,128)S(1)}, s32[1,2,128]{2,1,0:T(2,128)}, u32[]{:S(2)}) copy-start(s32[1,2,128]{2,1,0:T(2,128)} %param.11) | copy-start | bytes 3076
  0.7 4.9 %copy-start.3 = (s32[2,2,128]{2,1,0:T(2,128)S(1)}, s32[2,2,128]{2,1,0:T(2,128)}, u32[]{:S(2)}) copy-start(s32[2,2,128]{2,1,0:T(2,128)} %x_wall.1) | copy-start | bytes 6148
  1.8 3.8 %copy-start = (f32[1,2,4,64,128]{4,3,2,1,0:T(8,128)S(1)}, f32[1,2,4,64,128]{4,3,2,1,0:T(8,128)}, u32[]{:S(2)}) copy-start(f32[1,2,4,64,128]{4,3,2,1,0:T(8,128)} %param.8) | copy-start | bytes 786436
  1.9 6.2 %collective-permute-start = (f32[29,8,128]{2,1,0:T(8,128)S(1)}, f32[29,8,128]{2,1,0:T(8,128)S(1)}, u32[]{:S(2)}, u32[]{:S(2)}) collective-permute-start(f32[29,8,128]{2,1,0:T(8,128)S(1)} %get-tuple-element.22), channel_id=1, source_target_pairs={{0,2},{4,6},{8,10},{12,14},{16,18},{20,22},{24,26},{28,30},{2,0},{... | collective-permute-start | bytes 356360 | tf_op jit(solution)/shard_map/ppermute | solution.py:541
  4.9 3.2 %collective-permute-start.1 = (f32[29,8,128]{2,1,0:T(8,128)S(1)}, f32[29,8,128]{2,1,0:T(8,128)S(1)}, u32[]{:S(2)}, u32[]{:S(2)}) collective-permute-start(f32[29,8,128]{2,1,0:T(8,128)S(1)} %get-tuple-element.23), channel_id=1, source_target_pairs={{2,4},{6,8},{10,12},{14,16},{18,20},{22,24},{26,28},{4,2},{8,6},{1... | collective-permute-start | bytes 356360 | tf_op jit(solution)/shard_map/ppermute | solution.py:542
  5.6 0.7 %copy-start.5 = (f32[32]{0:T(128)S(1)}, f32[32]{0:T(128)}, u32[]{:S(2)}) copy-start(f32[32]{0:T(128)} %param.9) | copy-start | bytes 388
  6.6 1.3 %collective-permute-start.2 = (f32[9,8,128]{2,1,0:T(8,128)S(1)}, f32[9,8,128]{2,1,0:T(8,128)S(1)}, u32[]{:S(2)}, u32[]{:S(2)}) collective-permute-start(f32[9,8,128]{2,1,0:T(8,128)S(1)} %get-tuple-element.24), channel_id=1, source_target_pairs={{0,1},{1,0},{2,3},{3,2},{4,5},{5,4},{6,7},{7,6},{8,9},{9,8},{10,11... | collective-permute-start | bytes 110600 | tf_op jit(solution)/shard_map/ppermute | solution.py:507
  8.4 16.4 %collective-permute-start.3 = (f32[12,8,128]{2,1,0:T(8,128)S(1)}, f32[12,8,128]{2,1,0:T(8,128)S(1)}, u32[]{:S(2)}, u32[]{:S(2)}) collective-permute-start(f32[12,8,128]{2,1,0:T(8,128)S(1)} %get-tuple-element.27), channel_id=1, source_target_pairs={{0,1},{1,0},{2,3},{3,2},{4,5},{5,4},{6,7},{7,6},{8,9},{9,8},{10,11... | collective-permute-start | bytes 147464 | tf_op jit(solution)/shard_map/ppermute | solution.py:507

commit v8 on v7

--- a/solution.py
+++ b/solution.py
@@ -407,12 +407,7 @@
     rows = Rows()
     weights = z_weights(rows)
     derivative = Derivative(rows, derivative_matrix().T)
-    held = jnp.exp(-small[1, LOGK : LOGK + 1, 0:length])
-    summed = jnp.sum(received[...], axis=0, keepdims=True)
-    first, second = summed[:, length : 2 * length], summed[:, 2 * length : 3 * length]
-    gradient[...] = -(SCALE / 64.0) * held * (first + SCALE * held * second)
-    copies = [pltpu.make_async_copy(gradient, gradient_out, done.at[2])]
-    copies[0].start()
+    copies = []
     slot_a, slot_b = got_a[X_SLOTS], got_b[X_SLOTS]
     row = lax.broadcasted_iota(jnp.int32, (8, LANES), 0)
     slots = small[0]
@@ -482,6 +477,13 @@
                 adjoint[z, f, a] += terms[f]
         copies.append(pltpu.make_async_copy(adjoint.at[z], adjoint_out.at[z], done.at[z]))
         copies[-1].start()
+        if z == 0:
+            held = jnp.exp(-small[1, LOGK : LOGK + 1, 0:length])
+            summed = jnp.sum(received[...], axis=0, keepdims=True)
+            first, second = summed[:, length : 2 * length], summed[:, 2 * length : 3 * length]
+            gradient[...] = -(SCALE / 64.0) * held * (first + SCALE * held * second)
+            copies.append(pltpu.make_async_copy(gradient, gradient_out, done.at[2]))
+            copies[-1].start()
     for copy in copies:
         copy.wait()
 

time: 26.2 us -> 26.2 us (level)
  no operation moved by 1% of the time
where the time goes in v8:
time: 26.2 us; the launch traced here: 26 us
  blocking collectives  16.4 us (63%)
  starting transfers between devices  3.75 us (14%)
  Pallas kernels  3.01 us (11%)
  waiting for transfers between devices  1.49 us (6%)
  between operations  0.76 us (3%)
  local copies, waits for them, and re-layouts  0.65 us (2%)
    all_to_all x1, blocking collectives, shards(): received = lax.all_to_all(send, ('gx', 'gz'), 0, 0, tiled=True)  16.4 us
    pallas_call x5, Pallas kernels, call(): pl.pallas_call(kernel, out_shape=[jax.ShapeDtypeStruct(shape, jnp.float32...  3.01 us
    ppermute x1, starting transfers between devices, shards(): got_a = lax.ppermute(pay_a, 'gx', pairs_a)  3 us
    ppermute x2, waiting for transfers between devices, along_z(): return [lax.ppermute(payloads[0], 'gz', [(0, 1), (1, 0)])]  1.2 us
    ppermute x1, starting transfers between devices, shards(): got_b = lax.ppermute(pay_b, 'gx', pairs_b)  0.66 us
    unnamed x12, local copies, waits for them, and re-layouts  0.65 us
  transfers between devices with their start and end apart: 4, of which 2 were waited for; matrix products, arithmetic and copies ran while one was open for 0% of the time, Pallas kernels for 1%

profile of v8, /device:TPU:0, one launch (start us, length us, event | category | flops | bytes accessed | tf_op | source)
XLA Modules:
  0.0 26.0 jit_solution(16781274605417705603)
XLA Ops:
  0.6 0.0 copy-start.1
  0.6 0.0 copy-start.2
  0.7 0.0 copy-start.4
  0.7 0.0 copy-start.3
  0.7 1.1 %shard_map.86 = (f32[2,4,4,2,8,128]{5,4,3,2,1,0:T(8,128)S(1)}, f32[29,8,128]{2,1,0:T(8,128)S(1)}, f32[29,8,128]{2,1,0:T(8,128)S(1)}) custom-call(f32[2,4,4,2,8,128]{5,4,3,2,1,0:T(8,128)} %bitcast.21, f32[2,4,4,2,8,128]{5,4,3,2,1,0:T(8,128)} %bitcast.12), custom_call_target="tpu_custom_call" | custom-call | flops 2000000 | bytes 800000 | tf_op jit(solution)/shard_map/pallas_call | solution.py:492
  1.8 0.0 copy-start
  1.8 0.0 copy-done.1
  1.8 0.0 copy-done.2
  1.9 0.0 copy-done.4
  1.9 3.0 %collective-permute-start = (f32[29,8,128]{2,1,0:T(8,128)S(1)}, f32[29,8,128]{2,1,0:T(8,128)S(1)}, u32[]{:S(2)}, u32[]{:S(2)}) collective-permute-start(f32[29,8,128]{2,1,0:T(8,128)S(1)} %get-tuple-element.22), channel_id=1, source_target_pairs={{0,2},{4,6},{8,10},{12,14},{16,18},{20,22},{24,26},{28,30},{2,0},{... | collective-permute-start | bytes 356360 | tf_op jit(solution)/shard_map/ppermute | solution.py:543
  4.9 0.7 %collective-permute-start.1 = (f32[29,8,128]{2,1,0:T(8,128)S(1)}, f32[29,8,128]{2,1,0:T(8,128)S(1)}, u32[]{:S(2)}, u32[]{:S(2)}) collective-permute-start(f32[29,8,128]{2,1,0:T(8,128)S(1)} %get-tuple-element.23), channel_id=1, source_target_pairs={{2,4},{6,8},{10,12},{14,16},{18,20},{22,24},{26,28},{4,2},{8,6},{1... | collective-permute-start | bytes 356360 | tf_op jit(solution)/shard_map/ppermute | solution.py:544
  5.6 0.0 copy-start.5
  5.6 0.0 copy-done.3
  5.6 0.0 copy-done
  5.6 0.6 %copy-done.5 = f32[32]{0:T(128)S(1)} copy-done((f32[32]{0:T(128)S(1)}, f32[32]{0:T(128)}, u32[]{:S(2)}) %copy-start.5) | copy-done | bytes 152
  6.2 0.3 %shard_map.88 = (f32[3,8,128]{2,1,0:T(8,128)S(1)}, f32[2,4,4,2,8,128]{5,4,3,2,1,0:T(8,128)S(1)}, f32[9,8,128]{2,1,0:T(8,128)S(1)}) custom-call(f32[2,4,4,2,8,128]{5,4,3,2,1,0:T(8,128)S(1)} %get-tuple-element.16.state, f32[8,128]{1,0:T(8,128)S(1)} %get-tuple-element.19.positions, f32[2,4,4,2,8,128]{5,4,3,2,1,0:T(8,128)S(1)} %bitcast.13, ...), custom_call_target="tpu_custom_call" | custom-call | flops 2000000 | bytes 800000 | tf_op jit(solution)/shard_map/pallas_call | solution.py:492
  6.6 0.1 collective-permute-start.2
  6.7 1.2 %collective-permute-done.2.refs_0_ = f32[9,8,128]{2,1,0:T(8,128)S(1)} collective-permute-done((f32[9,8,128]{2,1,0:T(8,128)S(1)}, f32[9,8,128]{2,1,0:T(8,128)S(1)}, u32[]{:S(2)}, u32[]{:S(2)}) %collective-permute-start.2) | collective-permute-done | bytes 36896 | tf_op jit(solution)/shard_map/ppermute | solution.py:509
  7.9 0.3 %collective-permute-done.got_a = f32[29,8,128]{2,1,0:T(8,128)S(1)} collective-permute-done((f32[29,8,128]{2,1,0:T(8,128)S(1)}, f32[29,8,128]{2,1,0:T(8,128)S(1)}, u32[]{:S(2)}, u32[]{:S(2)}) %collective-permute-start) | collective-permute-done | bytes 118816 | tf_op jit(solution)/shard_map/ppermute | solution.py:543
  8.1 0.0 collective-permute-done.1.got_b
  8.1 0.3 %shard_map.89 = (f32[2,4,4,2,8,128]{5,4,3,2,1,0:T(8,128)S(1)}, f32[32,128]{1,0:T(8,128)S(1)}, f32[12,8,128]{2,1,0:T(8,128)S(1)}) custom-call(f32[2,4,4,2,8,128]{5,4,3,2,1,0:T(8,128)S(1)} %get-tuple-element.16.state, f32[3,8,128]{2,1,0:T(8,128)S(1)} %get-tuple-element.20.small, f32[2,4,4,2,8,128]{5,4,3,2,1,0:T(8,128)S(1)} %get-tuple-element.21.local, ...), custom_call_target="tpu_custom_call" | custom-call | flops 2000000 | bytes 800000 | tf_op jit(solution)/shard_map/pallas_call | solution.py:492
  8.4 0.0 collective-permute-start.3
  8.4 16.4 %all_to_all.11 = f32[32,1,128]{2,1,0:T(1,128)S(1)} all-to-all(f32[32,1,128]{2,1,0:T(1,128)S(1)} %bitcast.15), channel_id=1, replica_groups=mesh['gx'=16,'gz'=2] {'gx','gz'}, dimensions={0} | all-to-all | bytes 32768 | tf_op jit(solution)/shard_map/all_to_all | solution.py:565
  24.8 0.0 collective-permute-done.3.refs_1_
  24.8 1.2 %shard_map.90 = (f32[2,4,4,2,8,128]{5,4,3,2,1,0:T(8,128)}, f32[1,32]{1,0:T(1,128)}) custom-call(f32[2,4,4,2,8,128]{5,4,3,2,1,0:T(8,128)S(1)} %get-tuple-element.16.state, f32[3,8,128]{2,1,0:T(8,128)S(1)} %get-tuple-element.20.small, f32[2,4,4,2,8,128]{5,4,3,2,1,0:T(8,128)S(1)} %get-tuple-element.25.whole, f32[29,8,128]{2,1,0:T(8,128)S(1)} %collective-permute-done.got_a, ...), custom_call_target="tpu_custom_call" | custom-call | flops 2000000 | bytes 800000 | tf_op jit(solution)/shard_map/pallas_call | solution.py:492
  (1 shorter events, 0.0 us)
Async XLA Ops:
  0.6 1.2 %copy-start.1 = (s32[1024]{0:T(1024)S(1)}, s32[1024]{0:T(1024)}, u32[]{:S(2)}) copy-start(s32[1024]{0:T(1024)} %param.10) | copy-start | bytes 12292
  0.6 1.2 %copy-start.2 = (s32[2,1,128]{2,1,0:T(1,128)S(1)}, s32[2,1,128]{2,1,0:T(1,128)}, u32[]{:S(2)}) copy-start(s32[2,1,128]{2,1,0:T(1,128)} %param.13) | copy-start | bytes 3076
  0.7 1.2 %copy-start.4 = (s32[1,2,128]{2,1,0:T(2,128)S(1)}, s32[1,2,128]{2,1,0:T(2,128)}, u32[]{:S(2)}) copy-start(s32[1,2,128]{2,1,0:T(2,128)} %param.11) | copy-start | bytes 3076
  0.7 4.9 %copy-start.3 = (s32[2,2,128]{2,1,0:T(2,128)S(1)}, s32[2,2,128]{2,1,0:T(2,128)}, u32[]{:S(2)}) copy-start(s32[2,2,128]{2,1,0:T(2,128)} %x_wall.1) | copy-start | bytes 6148
  1.8 3.8 %copy-start = (f32[1,2,4,64,128]{4,3,2,1,0:T(8,128)S(1)}, f32[1,2,4,64,128]{4,3,2,1,0:T(8,128)}, u32[]{:S(2)}) copy-start(f32[1,2,4,64,128]{4,3,2,1,0:T(8,128)} %param.8) | copy-start | bytes 786436
  1.9 6.2 %collective-permute-start = (f32[29,8,128]{2,1,0:T(8,128)S(1)}, f32[29,8,128]{2,1,0:T(8,128)S(1)}, u32[]{:S(2)}, u32[]{:S(2)}) collective-permute-start(f32[29,8,128]{2,1,0:T(8,128)S(1)} %get-tuple-element.22), channel_id=1, source_target_pairs={{0,2},{4,6},{8,10},{12,14},{16,18},{20,22},{24,26},{28,30},{2,0},{... | collective-permute-start | bytes 356360 | tf_op jit(solution)/shard_map/ppermute | solution.py:543
  4.9 3.2 %collective-permute-start.1 = (f32[29,8,128]{2,1,0:T(8,128)S(1)}, f32[29,8,128]{2,1,0:T(8,128)S(1)}, u32[]{:S(2)}, u32[]{:S(2)}) collective-permute-start(f32[29,8,128]{2,1,0:T(8,128)S(1)} %get-tuple-element.23), channel_id=1, source_target_pairs={{2,4},{6,8},{10,12},{14,16},{18,20},{22,24},{26,28},{4,2},{8,6},{1... | collective-permute-start | bytes 356360 | tf_op jit(solution)/shard_map/ppermute | solution.py:544
  5.6 0.7 %copy-start.5 = (f32[32]{0:T(128)S(1)}, f32[32]{0:T(128)}, u32[]{:S(2)}) copy-start(f32[32]{0:T(128)} %param.9) | copy-start | bytes 388
  6.6 1.3 %collective-permute-start.2 = (f32[9,8,128]{2,1,0:T(8,128)S(1)}, f32[9,8,128]{2,1,0:T(8,128)S(1)}, u32[]{:S(2)}, u32[]{:S(2)}) collective-permute-start(f32[9,8,128]{2,1,0:T(8,128)S(1)} %get-tuple-element.24), channel_id=1, source_target_pairs={{0,1},{1,0},{2,3},{3,2},{4,5},{5,4},{6,7},{7,6},{8,9},{9,8},{10,11... | collective-permute-start | bytes 110600 | tf_op jit(solution)/shard_map/ppermute | solution.py:509
  8.4 16.4 %collective-permute-start.3 = (f32[12,8,128]{2,1,0:T(8,128)S(1)}, f32[12,8,128]{2,1,0:T(8,128)S(1)}, u32[]{:S(2)}, u32[]{:S(2)}) collective-permute-start(f32[12,8,128]{2,1,0:T(8,128)S(1)} %get-tuple-element.27), channel_id=1, source_target_pairs={{0,1},{1,0},{2,3},{3,2},{4,5},{5,4},{6,7},{7,6},{8,9},{9,8},{10,11... | collective-permute-start | bytes 147464 | tf_op jit(solution)/shard_map/ppermute | solution.py:509

commit v9 on v8

--- a/solution.py
+++ b/solution.py
@@ -539,6 +539,7 @@
         16 * 1024,
     )
     pairs_b = both_ways([(i, i + 1) for i in range(1, nx - 1, 2)])
+    pairs_b += [(i, i) for i in range(nx) if i not in dict(pairs_b)]
     pairs_a = both_ways([(i, i + 1) for i in range(0, nx - 1, 2)])
     got_a = lax.ppermute(pay_a, "gx", pairs_a)
     got_b = lax.ppermute(pay_b, "gx", pairs_b)

time: 26.2 us -> 26.2 us (level)
  no operation moved by 1% of the time
where the time goes in v9:
time: 26.2 us; the launch traced here: 26 us
  blocking collectives  16.4 us (63%)
  starting transfers between devices  3.75 us (14%)
  Pallas kernels  3.01 us (11%)
  waiting for transfers between devices  1.49 us (6%)
  between operations  0.76 us (3%)
  local copies, waits for them, and re-layouts  0.65 us (2%)
    all_to_all x1, blocking collectives, shards(): received = lax.all_to_all(send, ('gx', 'gz'), 0, 0, tiled=True)  16.4 us
    pallas_call x5, Pallas kernels, call(): pl.pallas_call(kernel, out_shape=[jax.ShapeDtypeStruct(shape, jnp.float32...  3.01 us
    ppermute x1, starting transfers between devices, shards(): got_a = lax.ppermute(pay_a, 'gx', pairs_a)  3 us
    ppermute x2, waiting for transfers between devices, along_z(): return [lax.ppermute(payloads[0], 'gz', [(0, 1), (1, 0)])]  1.2 us
    ppermute x1, starting transfers between devices, shards(): got_b = lax.ppermute(pay_b, 'gx', pairs_b)  0.66 us
    unnamed x12, local copies, waits for them, and re-layouts  0.65 us
  transfers between devices with their start and end apart: 4, of which 2 were waited for; matrix products, arithmetic and copies ran while one was open for 0% of the time, Pallas kernels for 1%

profile of v9, /device:TPU:0, one launch (start us, length us, event | category | flops | bytes accessed | tf_op | source)
XLA Modules:
  0.0 26.0 jit_solution(6285622493203445226)
XLA Ops:
  0.6 0.0 copy-start.1
  0.6 0.0 copy-start.2
  0.7 0.0 copy-start.4
  0.7 0.0 copy-start.3
  0.7 1.1 %shard_map.86 = (f32[2,4,4,2,8,128]{5,4,3,2,1,0:T(8,128)S(1)}, f32[29,8,128]{2,1,0:T(8,128)S(1)}, f32[29,8,128]{2,1,0:T(8,128)S(1)}) custom-call(f32[2,4,4,2,8,128]{5,4,3,2,1,0:T(8,128)} %bitcast.21, f32[2,4,4,2,8,128]{5,4,3,2,1,0:T(8,128)} %bitcast.12), custom_call_target="tpu_custom_call" | custom-call | flops 2000000 | bytes 800000 | tf_op jit(solution)/shard_map/pallas_call | solution.py:492
  1.8 0.0 copy-start
  1.8 0.0 copy-done.1
  1.8 0.0 copy-done.2
  1.9 0.0 copy-done.4
  1.9 3.0 %collective-permute-start = (f32[29,8,128]{2,1,0:T(8,128)S(1)}, f32[29,8,128]{2,1,0:T(8,128)S(1)}, u32[]{:S(2)}, u32[]{:S(2)}) collective-permute-start(f32[29,8,128]{2,1,0:T(8,128)S(1)} %get-tuple-element.22), channel_id=1, source_target_pairs={{0,2},{4,6},{8,10},{12,14},{16,18},{20,22},{24,26},{28,30},{2,0},{... | collective-permute-start | bytes 356360 | tf_op jit(solution)/shard_map/ppermute | solution.py:544
  4.9 0.7 %collective-permute-start.1 = (f32[29,8,128]{2,1,0:T(8,128)S(1)}, f32[29,8,128]{2,1,0:T(8,128)S(1)}, u32[]{:S(2)}, u32[]{:S(2)}) collective-permute-start(f32[29,8,128]{2,1,0:T(8,128)S(1)} %get-tuple-element.23), channel_id=1, source_target_pairs={{2,4},{6,8},{10,12},{14,16},{18,20},{22,24},{26,28},{4,2},{8,6},{1... | collective-permute-start | bytes 356360 | tf_op jit(solution)/shard_map/ppermute | solution.py:545
  5.6 0.0 copy-start.5
  5.6 0.0 copy-done.3
  5.6 0.0 copy-done
  5.6 0.6 %copy-done.5 = f32[32]{0:T(128)S(1)} copy-done((f32[32]{0:T(128)S(1)}, f32[32]{0:T(128)}, u32[]{:S(2)}) %copy-start.5) | copy-done | bytes 152
  6.2 0.3 %shard_map.88 = (f32[3,8,128]{2,1,0:T(8,128)S(1)}, f32[2,4,4,2,8,128]{5,4,3,2,1,0:T(8,128)S(1)}, f32[9,8,128]{2,1,0:T(8,128)S(1)}) custom-call(f32[2,4,4,2,8,128]{5,4,3,2,1,0:T(8,128)S(1)} %get-tuple-element.16.state, f32[8,128]{1,0:T(8,128)S(1)} %get-tuple-element.19.positions, f32[2,4,4,2,8,128]{5,4,3,2,1,0:T(8,128)S(1)} %bitcast.13, ...), custom_call_target="tpu_custom_call" | custom-call | flops 2000000 | bytes 800000 | tf_op jit(solution)/shard_map/pallas_call | solution.py:492
  6.6 0.1 collective-permute-start.2
  6.7 1.2 %collective-permute-done.2.refs_0_ = f32[9,8,128]{2,1,0:T(8,128)S(1)} collective-permute-done((f32[9,8,128]{2,1,0:T(8,128)S(1)}, f32[9,8,128]{2,1,0:T(8,128)S(1)}, u32[]{:S(2)}, u32[]{:S(2)}) %collective-permute-start.2) | collective-permute-done | bytes 36896 | tf_op jit(solution)/shard_map/ppermute | solution.py:509
  7.9 0.3 %collective-permute-done.got_a = f32[29,8,128]{2,1,0:T(8,128)S(1)} collective-permute-done((f32[29,8,128]{2,1,0:T(8,128)S(1)}, f32[29,8,128]{2,1,0:T(8,128)S(1)}, u32[]{:S(2)}, u32[]{:S(2)}) %collective-permute-start) | collective-permute-done | bytes 118816 | tf_op jit(solution)/shard_map/ppermute | solution.py:544
  8.1 0.0 collective-permute-done.1.got_b
  8.1 0.3 %shard_map.89 = (f32[2,4,4,2,8,128]{5,4,3,2,1,0:T(8,128)S(1)}, f32[32,128]{1,0:T(8,128)S(1)}, f32[12,8,128]{2,1,0:T(8,128)S(1)}) custom-call(f32[2,4,4,2,8,128]{5,4,3,2,1,0:T(8,128)S(1)} %get-tuple-element.16.state, f32[3,8,128]{2,1,0:T(8,128)S(1)} %get-tuple-element.20.small, f32[2,4,4,2,8,128]{5,4,3,2,1,0:T(8,128)S(1)} %get-tuple-element.21.local, ...), custom_call_target="tpu_custom_call" | custom-call | flops 2000000 | bytes 800000 | tf_op jit(solution)/shard_map/pallas_call | solution.py:492
  8.4 0.0 collective-permute-start.3
  8.4 16.4 %all_to_all.11 = f32[32,1,128]{2,1,0:T(1,128)S(1)} all-to-all(f32[32,1,128]{2,1,0:T(1,128)S(1)} %bitcast.15), channel_id=1, replica_groups=mesh['gx'=16,'gz'=2] {'gx','gz'}, dimensions={0} | all-to-all | bytes 32768 | tf_op jit(solution)/shard_map/all_to_all | solution.py:566
  24.8 0.0 collective-permute-done.3.refs_1_
  24.8 1.2 %shard_map.90 = (f32[2,4,4,2,8,128]{5,4,3,2,1,0:T(8,128)}, f32[1,32]{1,0:T(1,128)}) custom-call(f32[2,4,4,2,8,128]{5,4,3,2,1,0:T(8,128)S(1)} %get-tuple-element.16.state, f32[3,8,128]{2,1,0:T(8,128)S(1)} %get-tuple-element.20.small, f32[2,4,4,2,8,128]{5,4,3,2,1,0:T(8,128)S(1)} %get-tuple-element.25.whole, f32[29,8,128]{2,1,0:T(8,128)S(1)} %collective-permute-done.got_a, ...), custom_call_target="tpu_custom_call" | custom-call | flops 2000000 | bytes 800000 | tf_op jit(solution)/shard_map/pallas_call | solution.py:492
  (1 shorter events, 0.0 us)
Async XLA Ops:
  0.6 1.2 %copy-start.1 = (s32[1024]{0:T(1024)S(1)}, s32[1024]{0:T(1024)}, u32[]{:S(2)}) copy-start(s32[1024]{0:T(1024)} %param.10) | copy-start | bytes 12292
  0.6 1.2 %copy-start.2 = (s32[2,1,128]{2,1,0:T(1,128)S(1)}, s32[2,1,128]{2,1,0:T(1,128)}, u32[]{:S(2)}) copy-start(s32[2,1,128]{2,1,0:T(1,128)} %param.13) | copy-start | bytes 3076
  0.7 1.2 %copy-start.4 = (s32[1,2,128]{2,1,0:T(2,128)S(1)}, s32[1,2,128]{2,1,0:T(2,128)}, u32[]{:S(2)}) copy-start(s32[1,2,128]{2,1,0:T(2,128)} %param.11) | copy-start | bytes 3076
  0.7 4.9 %copy-start.3 = (s32[2,2,128]{2,1,0:T(2,128)S(1)}, s32[2,2,128]{2,1,0:T(2,128)}, u32[]{:S(2)}) copy-start(s32[2,2,128]{2,1,0:T(2,128)} %x_wall.1) | copy-start | bytes 6148
  1.8 3.8 %copy-start = (f32[1,2,4,64,128]{4,3,2,1,0:T(8,128)S(1)}, f32[1,2,4,64,128]{4,3,2,1,0:T(8,128)}, u32[]{:S(2)}) copy-start(f32[1,2,4,64,128]{4,3,2,1,0:T(8,128)} %param.8) | copy-start | bytes 786436
  1.9 6.2 %collective-permute-start = (f32[29,8,128]{2,1,0:T(8,128)S(1)}, f32[29,8,128]{2,1,0:T(8,128)S(1)}, u32[]{:S(2)}, u32[]{:S(2)}) collective-permute-start(f32[29,8,128]{2,1,0:T(8,128)S(1)} %get-tuple-element.22), channel_id=1, source_target_pairs={{0,2},{4,6},{8,10},{12,14},{16,18},{20,22},{24,26},{28,30},{2,0},{... | collective-permute-start | bytes 356360 | tf_op jit(solution)/shard_map/ppermute | solution.py:544
  4.9 3.2 %collective-permute-start.1 = (f32[29,8,128]{2,1,0:T(8,128)S(1)}, f32[29,8,128]{2,1,0:T(8,128)S(1)}, u32[]{:S(2)}, u32[]{:S(2)}) collective-permute-start(f32[29,8,128]{2,1,0:T(8,128)S(1)} %get-tuple-element.23), channel_id=1, source_target_pairs={{2,4},{6,8},{10,12},{14,16},{18,20},{22,24},{26,28},{4,2},{8,6},{1... | collective-permute-start | bytes 356360 | tf_op jit(solution)/shard_map/ppermute | solution.py:545
  5.6 0.7 %copy-start.5 = (f32[32]{0:T(128)S(1)}, f32[32]{0:T(128)}, u32[]{:S(2)}) copy-start(f32[32]{0:T(128)} %param.9) | copy-start | bytes 388
  6.6 1.3 %collective-permute-start.2 = (f32[9,8,128]{2,1,0:T(8,128)S(1)}, f32[9,8,128]{2,1,0:T(8,128)S(1)}, u32[]{:S(2)}, u32[]{:S(2)}) collective-permute-start(f32[9,8,128]{2,1,0:T(8,128)S(1)} %get-tuple-element.24), channel_id=1, source_target_pairs={{0,1},{1,0},{2,3},{3,2},{4,5},{5,4},{6,7},{7,6},{8,9},{9,8},{10,11... | collective-permute-start | bytes 110600 | tf_op jit(solution)/shard_map/ppermute | solution.py:509
  8.4 16.4 %collective-permute-start.3 = (f32[12,8,128]{2,1,0:T(8,128)S(1)}, f32[12,8,128]{2,1,0:T(8,128)S(1)}, u32[]{:S(2)}, u32[]{:S(2)}) collective-permute-start(f32[12,8,128]{2,1,0:T(8,128)S(1)} %get-tuple-element.27), channel_id=1, source_target_pairs={{0,1},{1,0},{2,3},{3,2},{4,5},{5,4},{6,7},{7,6},{8,9},{9,8},{10,11... | collective-permute-start | bytes 147464 | tf_op jit(solution)/shard_map/ppermute | solution.py:509

commit v10 on v8

--- a/solution.py
+++ b/solution.py
@@ -477,7 +477,7 @@
                 adjoint[z, f, a] += terms[f]
         copies.append(pltpu.make_async_copy(adjoint.at[z], adjoint_out.at[z], done.at[z]))
         copies[-1].start()
-        if z == 0:
+        if z == 1:
             held = jnp.exp(-small[1, LOGK : LOGK + 1, 0:length])
             summed = jnp.sum(received[...], axis=0, keepdims=True)
             first, second = summed[:, length : 2 * length], summed[:, 2 * length : 3 * length]

time: 26.2 us -> 26.2 us (level)
  no operation moved by 1% of the time
where the time goes in v10:
time: 26.2 us; the launch traced here: 26 us
  blocking collectives  16.4 us (63%)
  starting transfers between devices  3.75 us (14%)
  Pallas kernels  3.01 us (11%)
  waiting for transfers between devices  1.49 us (6%)
  between operations  0.76 us (3%)
  local copies, waits for them, and re-layouts  0.65 us (2%)
    all_to_all x1, blocking collectives, shards(): received = lax.all_to_all(send, ('gx', 'gz'), 0, 0, tiled=True)  16.4 us
    pallas_call x5, Pallas kernels, call(): pl.pallas_call(kernel, out_shape=[jax.ShapeDtypeStruct(shape, jnp.float32...  3.01 us
    ppermute x1, starting transfers between devices, shards(): got_a = lax.ppermute(pay_a, 'gx', pairs_a)  3 us
    ppermute x2, waiting for transfers between devices, along_z(): return [lax.ppermute(payloads[0], 'gz', [(0, 1), (1, 0)])]  1.2 us
    ppermute x1, starting transfers between devices, shards(): got_b = lax.ppermute(pay_b, 'gx', pairs_b)  0.66 us
    unnamed x12, local copies, waits for them, and re-layouts  0.65 us
  transfers between devices with their start and end apart: 4, of which 2 were waited for; matrix products, arithmetic and copies ran while one was open for 0% of the time, Pallas kernels for 1%

profile of v10, /device:TPU:0, one launch (start us, length us, event | category | flops | bytes accessed | tf_op | source)
XLA Modules:
  0.0 26.0 jit_solution(1641211967813848391)
XLA Ops:
  0.6 0.0 copy-start.1
  0.6 0.0 copy-start.2
  0.7 0.0 copy-start.4
  0.7 0.0 copy-start.3
  0.7 1.1 %shard_map.86 = (f32[2,4,4,2,8,128]{5,4,3,2,1,0:T(8,128)S(1)}, f32[29,8,128]{2,1,0:T(8,128)S(1)}, f32[29,8,128]{2,1,0:T(8,128)S(1)}) custom-call(f32[2,4,4,2,8,128]{5,4,3,2,1,0:T(8,128)} %bitcast.21, f32[2,4,4,2,8,128]{5,4,3,2,1,0:T(8,128)} %bitcast.12), custom_call_target="tpu_custom_call" | custom-call | flops 2000000 | bytes 800000 | tf_op jit(solution)/shard_map/pallas_call | solution.py:492
  1.8 0.0 copy-start
  1.8 0.0 copy-done.1
  1.8 0.0 copy-done.2
  1.9 0.0 copy-done.4
  1.9 3.0 %collective-permute-start = (f32[29,8,128]{2,1,0:T(8,128)S(1)}, f32[29,8,128]{2,1,0:T(8,128)S(1)}, u32[]{:S(2)}, u32[]{:S(2)}) collective-permute-start(f32[29,8,128]{2,1,0:T(8,128)S(1)} %get-tuple-element.22), channel_id=1, source_target_pairs={{0,2},{4,6},{8,10},{12,14},{16,18},{20,22},{24,26},{28,30},{2,0},{... | collective-permute-start | bytes 356360 | tf_op jit(solution)/shard_map/ppermute | solution.py:543
  4.9 0.7 %collective-permute-start.1 = (f32[29,8,128]{2,1,0:T(8,128)S(1)}, f32[29,8,128]{2,1,0:T(8,128)S(1)}, u32[]{:S(2)}, u32[]{:S(2)}) collective-permute-start(f32[29,8,128]{2,1,0:T(8,128)S(1)} %get-tuple-element.23), channel_id=1, source_target_pairs={{2,4},{6,8},{10,12},{14,16},{18,20},{22,24},{26,28},{4,2},{8,6},{1... | collective-permute-start | bytes 356360 | tf_op jit(solution)/shard_map/ppermute | solution.py:544
  5.6 0.0 copy-start.5
  5.6 0.0 copy-done.3
  5.6 0.0 copy-done
  5.6 0.6 %copy-done.5 = f32[32]{0:T(128)S(1)} copy-done((f32[32]{0:T(128)S(1)}, f32[32]{0:T(128)}, u32[]{:S(2)}) %copy-start.5) | copy-done | bytes 152
  6.2 0.3 %shard_map.88 = (f32[3,8,128]{2,1,0:T(8,128)S(1)}, f32[2,4,4,2,8,128]{5,4,3,2,1,0:T(8,128)S(1)}, f32[9,8,128]{2,1,0:T(8,128)S(1)}) custom-call(f32[2,4,4,2,8,128]{5,4,3,2,1,0:T(8,128)S(1)} %get-tuple-element.16.state, f32[8,128]{1,0:T(8,128)S(1)} %get-tuple-element.19.positions, f32[2,4,4,2,8,128]{5,4,3,2,1,0:T(8,128)S(1)} %bitcast.13, ...), custom_call_target="tpu_custom_call" | custom-call | flops 2000000 | bytes 800000 | tf_op jit(solution)/shard_map/pallas_call | solution.py:492
  6.6 0.1 collective-permute-start.2
  6.7 1.2 %collective-permute-done.2.refs_0_ = f32[9,8,128]{2,1,0:T(8,128)S(1)} collective-permute-done((f32[9,8,128]{2,1,0:T(8,128)S(1)}, f32[9,8,128]{2,1,0:T(8,128)S(1)}, u32[]{:S(2)}, u32[]{:S(2)}) %collective-permute-start.2) | collective-permute-done | bytes 36896 | tf_op jit(solution)/shard_map/ppermute | solution.py:509
  7.9 0.3 %collective-permute-done.got_a = f32[29,8,128]{2,1,0:T(8,128)S(1)} collective-permute-done((f32[29,8,128]{2,1,0:T(8,128)S(1)}, f32[29,8,128]{2,1,0:T(8,128)S(1)}, u32[]{:S(2)}, u32[]{:S(2)}) %collective-permute-start) | collective-permute-done | bytes 118816 | tf_op jit(solution)/shard_map/ppermute | solution.py:543
  8.1 0.0 collective-permute-done.1.got_b
  8.1 0.3 %shard_map.89 = (f32[2,4,4,2,8,128]{5,4,3,2,1,0:T(8,128)S(1)}, f32[32,128]{1,0:T(8,128)S(1)}, f32[12,8,128]{2,1,0:T(8,128)S(1)}) custom-call(f32[2,4,4,2,8,128]{5,4,3,2,1,0:T(8,128)S(1)} %get-tuple-element.16.state, f32[3,8,128]{2,1,0:T(8,128)S(1)} %get-tuple-element.20.small, f32[2,4,4,2,8,128]{5,4,3,2,1,0:T(8,128)S(1)} %get-tuple-element.21.local, ...), custom_call_target="tpu_custom_call" | custom-call | flops 2000000 | bytes 800000 | tf_op jit(solution)/shard_map/pallas_call | solution.py:492
  8.4 0.0 collective-permute-start.3
  8.4 16.4 %all_to_all.11 = f32[32,1,128]{2,1,0:T(1,128)S(1)} all-to-all(f32[32,1,128]{2,1,0:T(1,128)S(1)} %bitcast.15), channel_id=1, replica_groups=mesh['gx'=16,'gz'=2] {'gx','gz'}, dimensions={0} | all-to-all | bytes 32768 | tf_op jit(solution)/shard_map/all_to_all | solution.py:565
  24.8 0.0 collective-permute-done.3.refs_1_
  24.8 1.2 %shard_map.90 = (f32[2,4,4,2,8,128]{5,4,3,2,1,0:T(8,128)}, f32[1,32]{1,0:T(1,128)}) custom-call(f32[2,4,4,2,8,128]{5,4,3,2,1,0:T(8,128)S(1)} %get-tuple-element.16.state, f32[3,8,128]{2,1,0:T(8,128)S(1)} %get-tuple-element.20.small, f32[2,4,4,2,8,128]{5,4,3,2,1,0:T(8,128)S(1)} %get-tuple-element.25.whole, f32[29,8,128]{2,1,0:T(8,128)S(1)} %collective-permute-done.got_a, ...), custom_call_target="tpu_custom_call" | custom-call | flops 2000000 | bytes 800000 | tf_op jit(solution)/shard_map/pallas_call | solution.py:492
  (1 shorter events, 0.0 us)
Async XLA Ops:
  0.6 1.2 %copy-start.1 = (s32[1024]{0:T(1024)S(1)}, s32[1024]{0:T(1024)}, u32[]{:S(2)}) copy-start(s32[1024]{0:T(1024)} %param.10) | copy-start | bytes 12292
  0.6 1.2 %copy-start.2 = (s32[2,1,128]{2,1,0:T(1,128)S(1)}, s32[2,1,128]{2,1,0:T(1,128)}, u32[]{:S(2)}) copy-start(s32[2,1,128]{2,1,0:T(1,128)} %param.13) | copy-start | bytes 3076
  0.7 1.2 %copy-start.4 = (s32[1,2,128]{2,1,0:T(2,128)S(1)}, s32[1,2,128]{2,1,0:T(2,128)}, u32[]{:S(2)}) copy-start(s32[1,2,128]{2,1,0:T(2,128)} %param.11) | copy-start | bytes 3076
  0.7 4.9 %copy-start.3 = (s32[2,2,128]{2,1,0:T(2,128)S(1)}, s32[2,2,128]{2,1,0:T(2,128)}, u32[]{:S(2)}) copy-start(s32[2,2,128]{2,1,0:T(2,128)} %x_wall.1) | copy-start | bytes 6148
  1.8 3.8 %copy-start = (f32[1,2,4,64,128]{4,3,2,1,0:T(8,128)S(1)}, f32[1,2,4,64,128]{4,3,2,1,0:T(8,128)}, u32[]{:S(2)}) copy-start(f32[1,2,4,64,128]{4,3,2,1,0:T(8,128)} %param.8) | copy-start | bytes 786436
  1.9 6.2 %collective-permute-start = (f32[29,8,128]{2,1,0:T(8,128)S(1)}, f32[29,8,128]{2,1,0:T(8,128)S(1)}, u32[]{:S(2)}, u32[]{:S(2)}) collective-permute-start(f32[29,8,128]{2,1,0:T(8,128)S(1)} %get-tuple-element.22), channel_id=1, source_target_pairs={{0,2},{4,6},{8,10},{12,14},{16,18},{20,22},{24,26},{28,30},{2,0},{... | collective-permute-start | bytes 356360 | tf_op jit(solution)/shard_map/ppermute | solution.py:543
  4.9 3.2 %collective-permute-start.1 = (f32[29,8,128]{2,1,0:T(8,128)S(1)}, f32[29,8,128]{2,1,0:T(8,128)S(1)}, u32[]{:S(2)}, u32[]{:S(2)}) collective-permute-start(f32[29,8,128]{2,1,0:T(8,128)S(1)} %get-tuple-element.23), channel_id=1, source_target_pairs={{2,4},{6,8},{10,12},{14,16},{18,20},{22,24},{26,28},{4,2},{8,6},{1... | collective-permute-start | bytes 356360 | tf_op jit(solution)/shard_map/ppermute | solution.py:544
  5.6 0.7 %copy-start.5 = (f32[32]{0:T(128)S(1)}, f32[32]{0:T(128)}, u32[]{:S(2)}) copy-start(f32[32]{0:T(128)} %param.9) | copy-start | bytes 388
  6.6 1.3 %collective-permute-start.2 = (f32[9,8,128]{2,1,0:T(8,128)S(1)}, f32[9,8,128]{2,1,0:T(8,128)S(1)}, u32[]{:S(2)}, u32[]{:S(2)}) collective-permute-start(f32[9,8,128]{2,1,0:T(8,128)S(1)} %get-tuple-element.24), channel_id=1, source_target_pairs={{0,1},{1,0},{2,3},{3,2},{4,5},{5,4},{6,7},{7,6},{8,9},{9,8},{10,11... | collective-permute-start | bytes 110600 | tf_op jit(solution)/shard_map/ppermute | solution.py:509
  8.4 16.4 %collective-permute-start.3 = (f32[12,8,128]{2,1,0:T(8,128)S(1)}, f32[12,8,128]{2,1,0:T(8,128)S(1)}, u32[]{:S(2)}, u32[]{:S(2)}) collective-permute-start(f32[12,8,128]{2,1,0:T(8,128)S(1)} %get-tuple-element.27), channel_id=1, source_target_pairs={{0,1},{1,0},{2,3},{3,2},{4,5},{5,4},{6,7},{7,6},{8,9},{9,8},{10,11... | collective-permute-start | bytes 147464 | tf_op jit(solution)/shard_map/ppermute | solution.py:509
